TPU v7x, 32 devices: a whole 2x2x4 slice. The times are simulated.
32 devices in a mesh: dp: 4 (over y, x), seq: 8 (over z, core).
Axes of the slice: x: 2, y: 2, z: 4, core: 2. Of those that a mesh axis runs over, the one named last changes fastest.
Arguments:
- queries: bfloat16 [32, 128, 4096], P(('dp', 'seq')), parts along dimension 0, may hold values from -6 to 6
- outputs: bfloat16 [32, 128, 4096], P(('dp', 'seq')), parts along dimension 0, may hold values from -3 to 3
- out_grads: bfloat16 [32, 128, 4096], P(('dp', 'seq')), parts along dimension 0, may hold values from -12 to 12
- resp_keys: bfloat16 [32, 128, 512], P(('dp', 'seq')), parts along dimension 0, may hold values from -6 to 6
- resp_values: bfloat16 [32, 128, 512], P(('dp', 'seq')), parts along dimension 0, may hold values from -6 to 6
- lengths: int32 [32], P('dp'), parts along dimension 0, may hold values from 1 to 128, 512 in all
- prompt_keys: bfloat16 [1536, 512], P(('dp', 'seq')), parts along dimension 0, may hold values from -6 to 6
- prompt_values: bfloat16 [1536, 512], P(('dp', 'seq')), parts along dimension 0, may hold values from -6 to 6
Outputs:
- query_grads: bfloat16 [32, 128, 4096], P(('dp', 'seq')), parts along dimension 0
- resp_key_grads: bfloat16 [32, 128, 512], P(('dp', 'seq')), parts along dimension 0
- resp_value_grads: bfloat16 [32, 128, 512], P(('dp', 'seq')), parts along dimension 0
- prompt_key_grads: bfloat16 [1536, 512], P(('dp', 'seq')), parts along dimension 0
- prompt_value_grads: bfloat16 [1536, 512], P(('dp', 'seq')), parts along dimension 0
There are 4 independent parts, one for each index of `dp`. A program takes and returns all parts, laid end to end along the dimension named above; each array names one. Nothing has to cross between parts.
All inputs are finite; a program needn't handle non-finite values.
Results may differ from a plain program's by a relative error of at most 0.0055.
Values may be sent and summed in bfloat16 or wider, within the bound.
No kernel may reach another device: no remote copies, remote signals or barrier semaphores. Data moves between devices by JAX's collectives and lax.ppermute only.
A program may use at most 64 MiB of HBM per device.

v0:
```python
import jax
import jax.numpy as jnp
from jax import lax
from jax.sharding import PartitionSpec as P

HEAD_DIM = 128


def head_group(block, group_index, per_group, head_size):
    width = per_group * head_size
    sliced = lax.slice_in_dim(block, group_index * width, (group_index + 1) * width, axis=1)
    return sliced.reshape(block.shape[0], per_group, head_size)


def kv_column(block, group_index, head_size):
    return lax.slice_in_dim(block, group_index * head_size, (group_index + 1) * head_size, axis=1)


def scores_of(query_rows, key_block, softmax_scale):
    return (
        jnp.einsum("tgd,jd->gtj", query_rows, key_block, preferred_element_type=jnp.float32)
        * softmax_scale
    )


def block_grads(
    scores, grad_rows, row_delta, log_total, key_block, value_block, usable, softmax_scale
):
    probability = jnp.where(usable, jnp.exp(scores - log_total[:, :, None]), 0.0)
    prob_grad = jnp.einsum(
        "tgd,jd->gtj", grad_rows, value_block, preferred_element_type=jnp.float32
    )
    score_grad = (probability * (prob_grad - row_delta[:, :, None])).astype(jnp.bfloat16)
    weights = probability.astype(jnp.bfloat16)
    query_grad = (
        jnp.einsum("gtj,jd->tgd", score_grad, key_block, preferred_element_type=jnp.float32)
        * softmax_scale
    )
    return (query_grad, weights, score_grad)


def key_grads(weights, score_grad, query_rows, grad_rows, softmax_scale):
    value_grad = jnp.einsum("gtj,tgd->jd", weights, grad_rows, preferred_element_type=jnp.float32)
    key_grad = (
        jnp.einsum("gtj,tgd->jd", score_grad, query_rows, preferred_element_type=jnp.float32)
        * softmax_scale
    )
    return (key_grad, value_grad)


def own_path(
    query_all, output_all, grad_all, key_rows, value_rows, prompt_keys, prompt_values, length
):
    row_count = query_all.shape[0]
    kv_width = key_rows.shape[1]
    head_size = HEAD_DIM
    groups = kv_width // head_size
    per_group = query_all.shape[1] // kv_width
    softmax_scale = head_size ** (-0.5)
    position = lax.iota(jnp.int32, row_count)
    live_rows = position < length
    causal = position[None, :] <= position[:, None]
    prompt_usable = live_rows[None, :, None]
    resp_usable = (causal & live_rows[:, None])[None]
    query_list = [
        head_group(query_all, group_index, per_group, head_size) for group_index in range(groups)
    ]
    grad_list = [
        head_group(grad_all, group_index, per_group, head_size) for group_index in range(groups)
    ]
    delta_list = [
        jnp.sum(
            grad_list[group_index].astype(jnp.float32)
            * head_group(output_all, group_index, per_group, head_size).astype(jnp.float32),
            axis=2,
        ).T
        for group_index in range(groups)
    ]
    resp_key_list = [kv_column(key_rows, group_index, head_size) for group_index in range(groups)]
    resp_value_list = [
        kv_column(value_rows, group_index, head_size) for group_index in range(groups)
    ]
    resp_scores = [
        scores_of(query_list[group_index], resp_key_list[group_index], softmax_scale)
        for group_index in range(groups)
    ]
    all_keys, all_values = (
        lax.all_gather(prompt_keys, "seq", axis=0, tiled=True),
        lax.all_gather(prompt_values, "seq", axis=0, tiled=True),
    )
    dquery_list = []
    log_list = []
    weight_list = []
    sgrad_list = []
    for group_index in range(groups):
        key_block = kv_column(all_keys, group_index, head_size)
        value_block = kv_column(all_values, group_index, head_size)
        prompt_scores = scores_of(query_list[group_index], key_block, softmax_scale)
        masked_scores = jnp.where(causal[None], resp_scores[group_index], -1e30)
        top_score = jnp.maximum(jnp.max(prompt_scores, axis=2), jnp.max(masked_scores, axis=2))
        exp_total = jnp.sum(jnp.exp(prompt_scores - top_score[:, :, None]), axis=2)
        exp_total = exp_total + jnp.sum(
            jnp.where(causal[None], jnp.exp(resp_scores[group_index] - top_score[:, :, None]), 0.0),
            axis=2,
        )
        log_total = top_score + jnp.log(exp_total)
        query_grad, weights, score_grad = block_grads(
            prompt_scores,
            grad_list[group_index],
            delta_list[group_index],
            log_total,
            key_block,
            value_block,
            prompt_usable,
            softmax_scale,
        )
        dquery_list.append(query_grad)
        log_list.append(log_total)
        weight_list.append(weights)
        sgrad_list.append(score_grad)
    key_parts = []
    value_parts = []
    for prompt_group_index in range(groups):
        weight_cols = weight_list[prompt_group_index]
        sgrad_cols = sgrad_list[prompt_group_index]
        prompt_key_grad, prompt_value_grad = key_grads(
            weight_cols,
            sgrad_cols,
            query_list[prompt_group_index],
            grad_list[prompt_group_index],
            softmax_scale,
        )
        key_parts.append(prompt_key_grad)
        value_parts.append(prompt_value_grad)
    summed = lax.psum_scatter(
        jnp.concatenate(key_parts + value_parts, axis=1), "seq", scatter_dimension=0, tiled=True
    )
    query_parts = []
    resp_key_parts = []
    resp_value_parts = []
    for group_index in range(groups):
        query_grad, weights, score_grad = block_grads(
            resp_scores[group_index],
            grad_list[group_index],
            delta_list[group_index],
            log_list[group_index],
            resp_key_list[group_index],
            resp_value_list[group_index],
            resp_usable,
            softmax_scale,
        )
        key_grad, value_grad = key_grads(
            weights, score_grad, query_list[group_index], grad_list[group_index], softmax_scale
        )
        query_parts.append(
            (dquery_list[group_index] + query_grad).reshape(row_count, per_group * head_size)
        )
        resp_key_parts.append(key_grad)
        resp_value_parts.append(value_grad)
    query_grads = jnp.concatenate(query_parts, axis=1).astype(jnp.bfloat16)[None]
    resp_key_grads = jnp.concatenate(resp_key_parts, axis=1).astype(jnp.bfloat16)[None]
    resp_value_grads = jnp.concatenate(resp_value_parts, axis=1).astype(jnp.bfloat16)[None]
    prompt_key_grads = summed[:, :kv_width].astype(jnp.bfloat16)
    prompt_value_grads = summed[:, kv_width:].astype(jnp.bfloat16)
    return (query_grads, resp_key_grads, resp_value_grads, prompt_key_grads, prompt_value_grads)


def local(queries, outputs, out_grads, resp_keys, resp_values, lengths, prompt_keys, prompt_values):
    query_all = queries[0]
    output_all = outputs[0]
    grad_all = out_grads[0]
    key_rows = resp_keys[0]
    value_rows = resp_values[0]
    own_index = lax.axis_index("seq")
    length = jnp.sum(jnp.where(lax.iota(jnp.int32, lengths.shape[0]) == own_index, lengths, 0))
    results = own_path(
        query_all, output_all, grad_all, key_rows, value_rows, prompt_keys, prompt_values, length
    )
    return results


def solution(mesh):
    return jax.shard_map(
        local,
        mesh=mesh,
        in_specs=(
            P(("dp", "seq"), None, None),
            P(("dp", "seq"), None, None),
            P(("dp", "seq"), None, None),
            P(("dp", "seq"), None, None),
            P(("dp", "seq"), None, None),
            P("dp"),
            P(("dp", "seq"), None),
            P(("dp", "seq"), None),
        ),
        out_specs=(
            P(("dp", "seq"), None, None),
            P(("dp", "seq"), None, None),
            P(("dp", "seq"), None, None),
            P(("dp", "seq"), None),
            P(("dp", "seq"), None),
        ),
        check_vma=False,
    )
```

profile of v0, /device:TPU:0, one launch (start us, length us, event | category | flops | bytes accessed | tf_op | source)
XLA Modules:
  0.0 126.7 jit_solution(10684870345960674681)
XLA Ops:
  7.2 17.5 %all_gather.6 = bf16[384,512]{1,0:T(8,128)(2,1)} all-gather(bf16[48,512]{1,0:T(8,128)(2,1)} %param.14), channel_id=1, replica_groups=mesh['dp'=4,'seq'=8] {'seq'}, dimensions={0}, use_global_device_ids=true | all-gather | bytes 442368 | tf_op jit(solution)/shard_map/all_gather | solution.py:88
  24.7 1.6 %copy.128 = bf16[1,128,4096]{1,2,0:T(8,128)(2,1)S(1)} copy(bf16[1,128,4096]{2,1,0:T(8,128)(2,1)} %param.8) | data formatting | bytes 2097152 | tf_op args[0]
  31.2 1.3 %fusion.128 = s32[]{:T(128)} fusion(s32[8]{0:T(128)} %param.13, s32[]{:T(128)S(6)} %axis_index.12), kind=kLoop, calls=%fused_computation.210 | loop fusion | flops 23 | bytes 40 | tf_op jit(solution)/shard_map/reduce_sum | solution.py:175
  32.5 1.2 iota_compare_fusion.1
  33.7 15.7 %all_gather.7 = bf16[384,512]{1,0:T(8,128)(2,1)} all-gather(bf16[48,512]{1,0:T(8,128)(2,1)} %param.15), channel_id=1, replica_groups=mesh['dp'=4,'seq'=8] {'seq'}, dimensions={0}, use_global_device_ids=true | all-gather | bytes 442368 | tf_op jit(solution)/shard_map/all_gather | solution.py:89
  49.4 3.0 %bitcast_reduce_fusion.3 = (f32[8,128]{1,0:T(8,128)}, f32[384,128,8]{1,0,2:T(8,128)}) fusion(bf16[128,8,128]{0,2,1:T(8,128)(2,1)S(1)} %bitcast.416, bf16[384,512]{1,0:T(8,128)(2,1)} %all_gather.6), kind=kOutput, calls=%fused_computation.35 | convolution fusion | flops 101448704 | bytes 1937408 | tf_op jit(solution)/shard_map/tgd,jd->gtj/dot_general | solution.py:21
  52.4 1.6 %select_reduce_fusion.7 = (f32[8,128]{1,0:T(8,128)}, f32[8,128,128]{1,2,0:T(8,128)}) fusion(pred[128,128]{0,1:T(8,128)(4,1)S(1)} %iota_compare_fusion, bf16[128,8,128]{0,2,1:T(8,128)(2,1)S(1)} %bitcast.417, bf16[128,512]{1,0:T(8,128)(2,1)S(1)} %bitcast.456), kind=kOutput, calls=%fused_computation.164 | convolution fusion | flops 33946624 | bytes 839680 | tf_op jit(solution)/shard_map/tgd,jd->gtj/dot_general | solution.py:21
  54.0 2.3 %copy.133 = bf16[1,128,4096]{1,2,0:T(8,128)(2,1)} copy(bf16[1,128,4096]{2,1,0:T(8,128)(2,1)} %param.9) | data formatting | bytes 2097152 | tf_op args[1]
  56.2 2.2 %fusion.139 = (bf16[128,1024]{0,1:T(8,128)(2,1)}, bf16[128,1024]{0,1:T(8,128)(2,1)}, bf16[128,1024]{0,1:T(8,128)(2,1)}, bf16[128,1024]{0,1:T(8,128)(2,1)}) fusion(bf16[128,4096]{0,1:T(8,128)(2,1)} %bitcast.433), kind=kLoop, calls=%fused_computation.222 | loop fusion | bytes 2097152 | tf_op jit(solution)/shard_map/slice | solution.py:11
  58.4 2.3 %copy.131 = bf16[1,128,4096]{1,2,0:T(8,128)(2,1)} copy(bf16[1,128,4096]{2,1,0:T(8,128)(2,1)} %param.10) | data formatting | bytes 2097152 | tf_op args[2]
  60.7 1.4 %fusion.137 = (bf16[128,1024]{0,1:T(8,128)(2,1)S(1)}, bf16[128,1024]{0,1:T(8,128)(2,1)S(1)}, bf16[128,1024]{0,1:T(8,128)(2,1)S(1)}, bf16[128,1024]{0,1:T(8,128)(2,1)S(1)}) fusion(bf16[128,4096]{0,1:T(8,128)(2,1)} %bitcast.414), kind=kLoop, calls=%fused_computation.220 | loop fusion | bytes 2097152 | tf_op jit(solution)/shard_map/slice | solution.py:11
  62.2 1.5 %bitcast_reduce_fusion.2 = (f32[8,128]{1,0:T(8,128)S(1)}, f32[384,128,8]{1,0,2:T(8,128)S(1)}) fusion(bf16[128,8,128]{0,2,1:T(8,128)(2,1)S(1)} %bitcast.420, bf16[384,512]{1,0:T(8,128)(2,1)} %all_gather.6), kind=kOutput, calls=%fused_computation.25 | convolution fusion | flops 101448704 | bytes 1937408 | tf_op jit(solution)/shard_map/tgd,jd->gtj/dot_general | solution.py:21
  67.6 1.1 fusion.63
  69.2 1.1 fusion.61
  71.2 1.0 fusion.59
  74.3 1.1 fusion.55
  75.3 1.1 fusion.54
  76.4 1.1 fusion.53
  77.5 1.1 fusion.52
  78.6 3.0 %copy.243 = f32[384,1024]{1,0:T(8,128)} copy(f32[384,1024]{0,1:T(8,128)} %fusion.52) | data formatting | bytes 3145728
  84.4 1.7 %fusion.49 = bf16[8,128,128]{1,2,0:T(8,128)(2,1)} fusion(bf16[128,8,128]{0,2,1:T(8,128)(2,1)S(1)} %bitcast.441, f32[8,128,128]{1,2,0:T(8,128)S(1)} %copy-done.7, f32[8,128]{1,0:T(8,128)S(1)} %bitcast.469, f32[8,128]{1,0:T(8,128)S(1)} %copy-done.55, pred[128,128]{0,1:T(8,128)(4,1)S(1)} %broadcast_and_fusion, bf16[128,512]{1,0:T(8,128)(2,1)} %bitcast.462), kind=kOutput, calls=%fused_computation.81 | convolution fusion | flops 34209792 | bytes 1105920 | tf_op jit(solution)/shard_map/tgd,jd->gtj/dot_general | solution.py:30
  95.2 1.0 pad_maximum_fusion
  96.3 21.0 %reduce-scatter.4.cloned.1.call-done = f32[48,1024]{1,0:T(8,128)} async-done(((f32[384,1024]{1,0:T(8,128)}), f32[48,1024]{1,0:T(8,128)}) %reduce-scatter.4.cloned.1.call-update) | async-done | bytes 196624
  117.3 1.1 copy.244
  (206 shorter events, 24.8 us)
Async XLA Ops:
  7.2 110.2 %reduce-scatter.4.cloned.1.call-start = ((), (), s32[]{:S(2)}) async-start(), calls=%async_computation.1 | async-start | bytes 1769472
  26.4 2.9 %copy-start.34 = (bf16[384,512]{1,0:T(8,128)(2,1)S(1)}, bf16[384,512]{1,0:T(8,128)(2,1)}, u32[]{:S(2)}) copy-start(bf16[384,512]{1,0:T(8,128)(2,1)} %all_gather.6) | copy-start | bytes 1179652
  27.2 3.1 %copy-start.20 = (bf16[128,1024]{0,1:T(8,128)(2,1)}, bf16[128,1024]{0,1:T(8,128)(2,1)S(1)}, u32[]{:S(2)}) copy-start(bf16[128,1024]{0,1:T(8,128)(2,1)S(1)} %get-tuple-element.35) | copy-start | bytes 786436
  60.7 3.0 %copy-start.70 = (f32[8,128]{1,0:T(8,128)S(1)}, f32[8,128]{1,0:T(8,128)}, u32[]{:S(2)}) copy-start(f32[8,128]{1,0:T(8,128)} %get-tuple-element.47) | copy-start | bytes 12292
  60.7 3.0 %copy-start.71 = (f32[8,128]{1,0:T(8,128)S(1)}, f32[8,128]{1,0:T(8,128)}, u32[]{:S(2)}) copy-start(f32[8,128]{1,0:T(8,128)} %get-tuple-element.49) | copy-start | bytes 12292
  60.7 3.1 %copy-start = (f32[384,128,8]{1,0,2:T(8,128)S(1)}, f32[384,128,8]{1,0,2:T(8,128)}, u32[]{:S(2)}) copy-start(f32[384,128,8]{1,0,2:T(8,128)} %get-tuple-element.48) | copy-start | bytes 4718596
  62.1 12.1 %copy-start.26 = (bf16[128,1024]{0,1:T(8,128)(2,1)}, bf16[128,1024]{0,1:T(8,128)(2,1)S(1)}, u32[]{:S(2)}) copy-start(bf16[128,1024]{0,1:T(8,128)(2,1)S(1)} %get-tuple-element.31) | copy-start | bytes 786436
  62.1 13.2 %copy-start.28 = (bf16[128,1024]{0,1:T(8,128)(2,1)}, bf16[128,1024]{0,1:T(8,128)(2,1)S(1)}, u32[]{:S(2)}) copy-start(bf16[128,1024]{0,1:T(8,128)(2,1)S(1)} %get-tuple-element.34) | copy-start | bytes 786436
  62.1 14.3 %copy-start.30 = (bf16[128,1024]{0,1:T(8,128)(2,1)}, bf16[128,1024]{0,1:T(8,128)(2,1)S(1)}, u32[]{:S(2)}) copy-start(bf16[128,1024]{0,1:T(8,128)(2,1)S(1)} %get-tuple-element.33) | copy-start | bytes 786436
  62.1 15.4 %copy-start.32 = (bf16[128,1024]{0,1:T(8,128)(2,1)}, bf16[128,1024]{0,1:T(8,128)(2,1)S(1)}, u32[]{:S(2)}) copy-start(bf16[128,1024]{0,1:T(8,128)(2,1)S(1)} %get-tuple-element.32) | copy-start | bytes 786436
  65.8 8.5 %copy-start.51 = (f32[8,128]{1,0:T(8,128)}, f32[8,128]{1,0:T(8,128)S(1)}, u32[]{:S(2)}) copy-start(f32[8,128]{1,0:T(8,128)S(1)} %log_add_fusion.3) | copy-start | bytes 12292
  67.1 3.2 %copy-start.64 = (f32[128,8]{0,1:T(8,128)}, f32[128,8]{0,1:T(8,128)S(1)}, u32[]{:S(2)}) copy-start(f32[128,8]{0,1:T(8,128)S(1)} %get-tuple-element.22) | copy-start | bytes 12292
  67.1 5.2 %copy-start.66 = (f32[128,8]{0,1:T(8,128)}, f32[128,8]{0,1:T(8,128)S(1)}, u32[]{:S(2)}) copy-start(f32[128,8]{0,1:T(8,128)S(1)} %get-tuple-element.23) | copy-start | bytes 12292
  68.7 6.6 %copy-start.54 = (f32[8,128]{1,0:T(8,128)}, f32[8,128]{1,0:T(8,128)S(1)}, u32[]{:S(2)}) copy-start(f32[8,128]{1,0:T(8,128)S(1)} %log_add_fusion.2) | copy-start | bytes 12292
  70.3 6.1 %copy-start.56 = (f32[8,128]{1,0:T(8,128)}, f32[8,128]{1,0:T(8,128)S(1)}, u32[]{:S(2)}) copy-start(f32[8,128]{1,0:T(8,128)S(1)} %get-tuple-element.57) | copy-start | bytes 12292
  70.3 7.2 %copy-start.58 = (f32[8,128]{1,0:T(8,128)}, f32[8,128]{1,0:T(8,128)S(1)}, u32[]{:S(2)}) copy-start(f32[8,128]{1,0:T(8,128)S(1)} %get-tuple-element.56) | copy-start | bytes 12292
  78.6 3.1 %copy-start.73 = (pred[128]{0:T(512)(128)(4,1)S(1)}, pred[128]{0:T(512)(128)(4,1)}, u32[]{:S(2)}) copy-start(pred[128]{0:T(512)(128)(4,1)} %iota_compare_fusion.1) | copy-start | bytes 388
  83.6 2.9 %copy-start.36 = (bf16[8,128,128]{1,2,0:T(8,128)(2,1)}, bf16[8,128,128]{1,2,0:T(8,128)(2,1)S(1)}, u32[]{:S(2)}) copy-start(bf16[8,128,128]{1,2,0:T(8,128)(2,1)S(1)} %fusion.45) | copy-start | bytes 786436
  83.6 2.6 %copy-start.9 = (f32[8,128,128]{1,2,0:T(8,128)S(1)}, f32[8,128,128]{1,2,0:T(8,128)}, u32[]{:S(2)}) copy-start(f32[8,128,128]{1,2,0:T(8,128)} %get-tuple-element.50) | copy-start | bytes 1572868
  84.1 2.6 %copy-start.38 = (bf16[8,128,128]{1,2,0:T(8,128)(2,1)}, bf16[8,128,128]{1,2,0:T(8,128)(2,1)S(1)}, u32[]{:S(2)}) copy-start(bf16[8,128,128]{1,2,0:T(8,128)(2,1)S(1)} %fusion.47) | copy-start | bytes 786436
  84.1 2.6 %copy-start.22 = (bf16[128,1024]{0,1:T(8,128)(2,1)S(1)}, bf16[128,1024]{0,1:T(8,128)(2,1)}, u32[]{:S(2)}) copy-start(bf16[128,1024]{0,1:T(8,128)(2,1)} %copy-done.20) | copy-start | bytes 786436
  84.4 3.4 %copy-start.19 = (bf16[128,1024]{0,1:T(8,128)(2,1)S(1)}, bf16[128,1024]{0,1:T(8,128)(2,1)}, u32[]{:S(2)}) copy-start(bf16[128,1024]{0,1:T(8,128)(2,1)} %get-tuple-element.37) | copy-start | bytes 786436
  87.0 3.1 %copy-start.13 = (bf16[8,128,384]{1,2,0:T(8,128)(2,1)S(1)}, bf16[8,128,384]{1,2,0:T(8,128)(2,1)}, u32[]{:S(2)}) copy-start(bf16[8,128,384]{1,2,0:T(8,128)(2,1)} %copy-done.12) | copy-start | bytes 2359300
  87.0 3.1 %copy-start.35 = (bf16[384,512]{1,0:T(8,128)(2,1)S(1)}, bf16[384,512]{1,0:T(8,128)(2,1)}, u32[]{:S(2)}) copy-start(bf16[384,512]{1,0:T(8,128)(2,1)} %all_gather.6) | copy-start | bytes 1179652
  (51 other events, 73.3 us)
Sparse Core Ops, SparseCore 0:
  81.8 35.4 reduce-scatter.3
where the time goes:
time: 127 us
  blocking collectives  33.2 us (26%)
  matrix products  28.3 us (22%)
  local copies, waits for them, and re-layouts  23.9 us (19%)
  waiting for transfers between devices  21.1 us (17%)
  between operations  15 us (12%)
  other arithmetic  5.19 us (4%)
    unnamed x2, waiting for transfers between devices  21.1 us
    all_gather x1, blocking collectives, own_path(): lax.all_gather(prompt_keys, 'seq', axis=0, tiled=True)  17.5 us
    unnamed x157, local copies, waits for them, and re-layouts  17.5 us
    all_gather x1, blocking collectives, own_path(): lax.all_gather(prompt_values, 'seq', axis=0, tiled=True)  15.7 us
    dot_general x8, matrix products, scores_of(): jnp.einsum('tgd,jd->gtj', query_rows, key_block, preferred_element_type=j...  10.4 us
    dot_general x8, matrix products, key_grads(): jnp.einsum('gtj,tgd->jd', weights, grad_rows, preferred_element_type=jnp....  5.29 us
    dot_general x8, matrix products, block_grads(): jnp.einsum('tgd,jd->gtj', grad_rows, value_block, preferred_element_type=...  5.09 us
    dot_general x8, matrix products, key_grads(): jnp.einsum('gtj,tgd->jd', score_grad, query_rows, preferred_element_type=...  5.09 us
  transfers between devices with their start and end apart: 1, of which 1 were waited for; matrix products, arithmetic and copies ran while one was open for 10% of the time, Pallas kernels for 0%

commit v1 on v0

v1 whole, which is shorter than its diff:
```python
import functools

import jax
import jax.numpy as jnp
from jax import lax
from jax.experimental import pallas as pl
from jax.experimental.pallas import tpu as pltpu
from jax.sharding import PartitionSpec as P

HEAD_DIM = 128
SCALE = HEAD_DIM ** (-0.5)
LOG2E = 1.4426950408889634
NT = (((1,), (1,)), ((), ()))
CORES = 2
CHUNK = 32
DELTA_TERMS = 3
BF16 = jnp.bfloat16
F32 = jnp.float32
VMEM_SPEC = pl.BlockSpec(memory_space=pltpu.VMEM)
HBM_SPEC = pl.BlockSpec(memory_space=pltpu.HBM)
SMEM_SPEC = pl.BlockSpec(memory_space=pltpu.SMEM)
MIB = 1024 * 1024
PARAMS = pltpu.CompilerParams(vmem_limit_bytes=24 * MIB)


def shape(*dims):
    return jax.ShapeDtypeStruct(dims, BF16)


def dot(a, b, dims=None):
    if dims is None:
        return jnp.dot(a, b, preferred_element_type=F32)
    return lax.dot_general(a, b, dims, preferred_element_type=F32)


def head_slice(index):
    return slice(index * HEAD_DIM, (index + 1) * HEAD_DIM)


def prepare_kernel(groups, len_ref, *refs):
    wide_in, narrow_in, refs = refs[:3], refs[3:5], refs[5:]
    (q_rows, g_rows, q_cols, g_cols, live_ref), narrow_out, refs = refs[:5], refs[5:7], refs[7:]
    wide_buf, (wide_sem, narrow_sem) = refs[:3], refs[3:]
    rows = wide_buf[0].shape[0]
    width = wide_buf[0].shape[1] // groups
    wide = [
        [
            pltpu.make_async_copy(src.at[:, group * width : (group + 1) * width], buf.at[:, group * width : (group + 1) * width], wide_sem.at[group, i])
            for i, (src, buf) in enumerate(zip(wide_in, wide_buf))
        ]
        for group in range(groups)
    ]
    narrow = [pltpu.make_async_copy(src, out, narrow_sem.at[i]) for i, (src, out) in enumerate(zip(narrow_in, narrow_out))]
    for copy in sum(wide, []) + narrow:
        copy.start()
    length = len_ref[lax.axis_index("seq")]
    live_ref[...] = jnp.where(lax.broadcasted_iota(jnp.int32, live_ref.shape, 0) < length, 1.0, 0.0)
    lane = lax.broadcasted_iota(jnp.int32, (rows, HEAD_DIM), 1)
    q_ref, o_ref, g_ref = wide_buf
    heads = width // HEAD_DIM
    for head in range(groups * heads):
        if head % heads == 0:
            for copy in wide[head // heads]:
                copy.wait()
        cols = head_slice(head)
        span = slice(head * rows, (head + 1) * rows)
        q = q_ref[:, cols]
        g = g_ref[:, cols]
        left = jnp.sum(g.astype(F32) * o_ref[:, cols].astype(F32), axis=1, keepdims=True)
        terms = jnp.zeros((rows, HEAD_DIM), F32)
        for term in range(DELTA_TERMS):
            rounded = left.astype(BF16).astype(F32)
            terms = jnp.where(lane == term, rounded, terms)
            left = left - rounded
        q_rows[span, :] = q
        g_rows[span, :HEAD_DIM] = g
        g_rows[span, HEAD_DIM:] = terms.astype(BF16)
        q_cols[:, span] = q.T
        g_cols[:, span] = g.T
    for copy in narrow:
        copy.wait()


def prepare(lengths, q, o, g, rk, rv):
    rows, width = q.shape
    groups = rk.shape[1] // HEAD_DIM
    flat = rows * width // HEAD_DIM
    narrow = [rk, rv]
    return pl.pallas_call(
        functools.partial(prepare_kernel, groups),
        in_specs=[SMEM_SPEC] + [HBM_SPEC] * 5,
        out_specs=[VMEM_SPEC] * 7,
        out_shape=[
            shape(flat, HEAD_DIM),
            shape(flat, 2 * HEAD_DIM),
            shape(HEAD_DIM, flat),
            shape(HEAD_DIM, flat),
            jax.ShapeDtypeStruct((rows, HEAD_DIM), F32),
        ]
        + [shape(*x.shape) for x in narrow],
        scratch_shapes=[pltpu.VMEM((rows, width), BF16)] * 3
        + [pltpu.SemaphoreType.DMA((groups, 3)), pltpu.SemaphoreType.DMA((2,))],
        compiler_params=PARAMS,
        cost_estimate=pl.CostEstimate(flops=rows * width * 4000, bytes_accessed=16 * rows * width, transcendentals=0),
    )(lengths, *[pltpu.with_memory_space_constraint(x, pltpu.HBM) for x in [q, o, g] + narrow])


def attention_kernel(chips, piece_rows, live_ref, q_rows, g_rows, q_cols, g_cols, rk_ref, rv_ref, *rest):
    pieces = CORES * chips
    kv_refs, (dq_ref, drk_ref, drv_ref), rest = rest[:pieces], rest[pieces : pieces + 3], rest[pieces + 3 :]
    d_own, d_other, (k_buf, v_buf, s_buf, dp_buf, p_buf, ds_buf) = rest[:chips], rest[chips], rest[chips + 1 :]
    rows, width = rk_ref.shape
    groups = width // HEAD_DIM
    flat = q_rows.shape[0] // groups
    block = flat // 2
    keys = k_buf.shape[1]
    prompt = keys - rows
    diagonal = lax.broadcasted_iota(jnp.int32, (CHUNK, rows), 1) - lax.broadcasted_iota(jnp.int32, (CHUNK, rows), 0)
    minus = jnp.where(lax.broadcasted_iota(jnp.int32, (keys, HEAD_DIM), 1) < DELTA_TERMS, -1.0, 0.0).astype(BF16)

    def load_keys(group):
        k_cols = head_slice(group)
        v_cols = slice(width + group * HEAD_DIM, width + (group + 1) * HEAD_DIM)
        for i in range(pieces):
            span = slice(i * piece_rows, (i + 1) * piece_rows)
            k_buf[group, span, :] = kv_refs[i][:, k_cols]
            v_buf[group, span, :HEAD_DIM] = kv_refs[i][:, v_cols]
        k_buf[group, prompt:, :] = rk_ref[:, k_cols]
        v_buf[group, prompt:, :HEAD_DIM] = rv_ref[:, k_cols]
        v_buf[group, :, HEAD_DIM:] = minus

    def scores(half):
        group, slot = half // 2, half % 2
        if slot == 0:
            load_keys(group)
        span = slice(half * block, (half + 1) * block)
        s_buf[slot] = dot(q_rows[span, :], k_buf[group], NT)
        dp_buf[slot] = dot(g_rows[span, :], v_buf[group], NT)

    def soften(half):
        slot = half % 2
        for low in range(0, block, CHUNK):
            first = low % rows
            span = slice(low, low + CHUNK)
            s = s_buf[slot, span, :]
            s = jnp.concatenate([s[:, :prompt], jnp.where(diagonal > first, -1e30, s[:, prompt:])], axis=1)
            top = jnp.max(s, axis=1, keepdims=True)
            e = jnp.exp2((s - top) * (SCALE * LOG2E))
            weight = (1.0 / jnp.sum(e, axis=1, keepdims=True)) * live_ref[first : first + CHUNK, :]
            p = e * jnp.concatenate([weight] * (keys // HEAD_DIM), axis=1)
            p_buf[slot, span, :] = p.astype(BF16)
            ds_buf[slot, span, :] = (p * dp_buf[slot, span, :]).astype(BF16)

    def gradients(half):
        group, slot = half // 2, half % 2
        span = slice(half * block, (half + 1) * block)
        dq = (dot(ds_buf[slot], k_buf[group]) * SCALE).astype(BF16)
        for i in range(block // rows):
            dq_ref[:, head_slice(half * (block // rows) + i)] = dq[i * rows : (i + 1) * rows]
        return dot(q_cols[:, span], ds_buf[slot]), dot(g_cols[:, span], p_buf[slot])

    scores(0)
    held = None
    for half in range(2 * groups):
        if half + 1 < 2 * groups:
            scores(half + 1)
        soften(half)
        dk, dv = gradients(half)
        if half % 2 == 0:
            held = (dk, dv)
            continue
        group = half // 2
        dk = ((held[0] + dk) * SCALE).T
        dv = (held[1] + dv).T
        for grad, low in ((dk, 0), (dv, width)):
            cols = slice(low + group * HEAD_DIM, low + (group + 1) * HEAD_DIM)
            for i in range(chips):
                d_own[i][:, cols] = grad[i * piece_rows : (i + 1) * piece_rows]
                d_other[i, :, cols] = grad[(chips + i) * piece_rows : (chips + i + 1) * piece_rows].astype(BF16)
        drk_ref[:, head_slice(group)] = dk[prompt:].astype(BF16)
        drv_ref[:, head_slice(group)] = dv[prompt:].astype(BF16)


def attention(prepared, kv_pieces):
    live, q_rows, g_rows, q_cols, g_cols, rk, rv = prepared
    rows, kv_width = rk.shape
    groups = kv_width // HEAD_DIM
    flat = q_rows.shape[0]
    pieces = len(kv_pieces)
    chips = pieces // CORES
    piece_rows = kv_pieces[0].shape[0]
    keys = pieces * piece_rows + rows
    block = flat // groups // 2
    return pl.pallas_call(
        functools.partial(attention_kernel, chips, piece_rows),
        in_specs=[VMEM_SPEC] * (7 + pieces),
        out_specs=[VMEM_SPEC] * (4 + chips),
        out_shape=[shape(rows, flat // rows * HEAD_DIM), shape(rows, kv_width), shape(rows, kv_width)]
        + [jax.ShapeDtypeStruct((piece_rows, 2 * kv_width), F32)] * chips
        + [shape(chips, piece_rows, 2 * kv_width)],
        scratch_shapes=[
            pltpu.VMEM((groups, keys, HEAD_DIM), BF16),
            pltpu.VMEM((groups, keys, 2 * HEAD_DIM), BF16),
            pltpu.VMEM((2, block, keys), F32),
            pltpu.VMEM((2, block, keys), F32),
            pltpu.VMEM((2, block, keys), BF16),
            pltpu.VMEM((2, block, keys), BF16),
        ],
        compiler_params=PARAMS,
        cost_estimate=pl.CostEstimate(
            flops=10 * flat * keys * HEAD_DIM, bytes_accessed=10 * flat * HEAD_DIM, transcendentals=flat * keys
        ),
    )(live, q_rows, g_rows, q_cols, g_cols, rk, rv, *kv_pieces)


def to_chip(x, chips, step):
    if chips & (chips - 1) == 0:
        route = [chip ^ step for chip in range(chips)]
    else:
        route = [(step - chip) % chips for chip in range(chips)]
    pairs = [(CORES * chip + core, CORES * route[chip] + core) for chip in range(chips) for core in range(CORES)]
    return lax.ppermute(x, "seq", pairs)


def swap_core(x, chips):
    pairs = [(CORES * chip + core, CORES * chip + 1 - core) for chip in range(chips) for core in range(CORES)]
    return lax.ppermute(x, "seq", pairs)


def local(chips, queries, outputs, out_grads, resp_keys, resp_values, lengths, prompt_keys, prompt_values):
    kv_width = prompt_keys.shape[1]
    steps = [1] + list(range(chips - 1, 1, -1))
    kv = jnp.concatenate([prompt_keys, prompt_values], axis=1)
    far = [to_chip(kv, chips, step) for step in steps]
    prepared = prepare(lengths, queries[0], outputs[0], out_grads[0], resp_keys[0], resp_values[0])
    far, prepared = lax.optimization_barrier((far, prepared))
    q_rows, g_rows, q_cols, g_cols, live, rk, rv = prepared
    own = [kv] + far
    other = [swap_core(x, chips) for x in own]
    results = attention((live, q_rows, g_rows, q_cols, g_cols, rk, rv), own + other)
    dq, drk, drv = results[:3]
    swapped = swap_core(results[3 + chips], chips)
    both = [results[3 + i] + swapped[i].astype(F32) for i in range(chips)]
    back = [to_chip(both[1 + steps.index(step)].astype(BF16), chips, step) for step in [2, 1] + list(range(3, chips))]
    total = sum([x.astype(F32) for x in back], both[0]).astype(BF16)
    return dq[None], drk[None], drv[None], total[:, :kv_width], total[:, kv_width:]


def solution(mesh):
    chips = mesh.shape["seq"] // CORES
    split = ("dp", "seq")
    row3 = P(split, None, None)
    row2 = P(split, None)
    return jax.shard_map(
        functools.partial(local, chips),
        mesh=mesh,
        in_specs=(row3, row3, row3, row3, row3, P("dp"), row2, row2),
        out_specs=(row3, row3, row3, row2, row2),
        check_vma=False,
    )
```

time: 127 us -> 38.5 us (0.30)
  blocking collectives: 33.2 us -> 0 us
  matrix products: 28.3 us -> 0 us
  local copies, waits for them, and re-layouts: 23.9 us -> 2.9 us
  between operations: 15 us -> 0.66 us
  starting transfers between devices: 0.04 us -> 10.5 us
  Pallas kernels: 0 us -> 9.88 us
  waiting for transfers between devices: 21.1 us -> 14.3 us
  other arithmetic: 5.19 us -> 0.14 us
    all_gather x2 -> x0, blocking collectives: 33.2 us -> none  [the longest x1 17.5 us: own_path(): lax.all_gather(prompt_keys, 'seq', axis=0, tiled=True)]
    dot_general x40 -> x0, matrix products: 28.3 us -> none  [the longest x8 10.4 us: scores_of(): jnp.einsum('tgd,jd->gtj', query_rows, key_block, preferred_element_type=j...]
    unnamed x2 -> x0, waiting for transfers between devices: 21.1 us -> none
    unnamed x157 -> x3, local copies, waits for them, and re-layouts: 17.5 us -> 1.46 us
    ppermute x0 -> x11, waiting for transfers between devices: none -> 14.3 us  [the longest x6 11.4 us: to_chip(): return lax.ppermute(x, 'seq', pairs)]
    ppermute x0 -> x11, starting transfers between devices: none -> 10.5 us  [the longest x6 9.34 us: to_chip(): return lax.ppermute(x, 'seq', pairs)]
    pallas_call x0 -> x2, Pallas kernels: none -> 9.88 us  [the longest x1 6.46 us: attention(): pl.pallas_call(functools.partial(attention_kernel, chips, piece_rows), in...]
    slice x4 -> x1, local copies, waits for them, and re-layouts: 4.43 us -> 0.64 us  [local(): total[:, kv_width:]]
  transfers between devices with their start and end apart: 1 -> 11, of which waited for: 1 -> 8; matrix products, arithmetic and copies ran while one was open for 10% -> 0% of each run, Pallas kernels for 0% -> 9%
where the time goes in v1:
time: 38.5 us; the launch traced here: 38.3 us
  waiting for transfers between devices  14.3 us (37%)
  starting transfers between devices  10.5 us (27%)
  Pallas kernels  9.88 us (26%)
  local copies, waits for them, and re-layouts  2.9 us (8%)
  between operations  0.66 us (2%)
    ppermute x6, waiting for transfers between devices, to_chip(): return lax.ppermute(x, 'seq', pairs)  11.4 us
    ppermute x6, starting transfers between devices, to_chip(): return lax.ppermute(x, 'seq', pairs)  9.34 us
    pallas_call x1, Pallas kernels, attention(): pl.pallas_call(functools.partial(attention_kernel, chips, piece_rows), in...  6.46 us
    pallas_call x1, Pallas kernels, prepare(): pl.pallas_call(functools.partial(prepare_kernel, groups), in_specs=[SMEM_...  3.42 us
    ppermute x5, waiting for transfers between devices, swap_core(): return lax.ppermute(x, 'seq', pairs)  2.87 us
    unnamed x3, local copies, waits for them, and re-layouts  1.46 us
    ppermute x5, starting transfers between devices, swap_core(): return lax.ppermute(x, 'seq', pairs)  1.12 us
    concatenate x1, local copies, waits for them, and re-layouts, local(): kv = jnp.concatenate([prompt_keys, prompt_values], axis=1)  0.8 us
  transfers between devices with their start and end apart: 11, of which 8 were waited for; matrix products, arithmetic and copies ran while one was open for 0% of the time, Pallas kernels for 9%

profile of v1, /device:TPU:0, one launch (start us, length us, event | category | flops | bytes accessed | tf_op | source)
XLA Modules:
  0.0 38.3 jit_solution(2594055129043831906)
XLA Ops:
  0.6 0.8 %constant_dynamic-update-slice_fusion.1 = bf16[48,1024]{1,0:T(8,128)(2,1)S(1)} fusion(bf16[48,512]{1,0:T(8,128)(2,1)} %param.14), kind=kLoop, calls=%fused_computation.16 | loop fusion | bytes 98304
  1.4 0.8 %constant_dynamic-update-slice_fusion.rest_0_ = bf16[48,1024]{1,0:T(8,128)(2,1)S(1)} fusion(bf16[48,1024]{1,0:T(8,128)(2,1)S(1)} %constant_dynamic-update-slice_fusion.1, bf16[48,512]{1,0:T(8,128)(2,1)} %param.15), kind=kLoop, calls=%fused_computation.15 | loop fusion | bytes 98304 | tf_op jit(solution)/shard_map/concatenate | solution.py:233
  2.2 0.5 %collective-permute-start.3 = (bf16[48,1024]{1,0:T(8,128)(2,1)S(1)}, bf16[48,1024]{1,0:T(8,128)(2,1)S(1)}, u32[]{:S(2)}, u32[]{:S(2)}) collective-permute-start(bf16[48,1024]{1,0:T(8,128)(2,1)S(1)} %constant_dynamic-update-slice_fusion.rest_0_), channel_id=1, source_target_pairs={{0,1},{1,0},{2,3},{3,2},{4,5},{5,4},{6,7},{7,6},{8,9},{9,8},{10,11... | collective-permute-start | bytes 294920 | tf_op jit(solution)/shard_map/ppermute | solution.py:227
  2.7 3.6 %collective-permute-start.2 = (bf16[48,1024]{1,0:T(8,128)(2,1)S(1)}, bf16[48,1024]{1,0:T(8,128)(2,1)S(1)}, u32[]{:S(2)}, u32[]{:S(2)}) collective-permute-start(bf16[48,1024]{1,0:T(8,128)(2,1)S(1)} %constant_dynamic-update-slice_fusion.rest_0_), channel_id=1, source_target_pairs={{0,4},{1,5},{2,6},{3,7},{4,0},{5,1},{6,2},{7,3},{8,12},{9,13},{10,... | collective-permute-start | bytes 294920 | tf_op jit(solution)/shard_map/ppermute | solution.py:222
  6.3 1.3 %collective-permute-start.1 = (bf16[48,1024]{1,0:T(8,128)(2,1)S(1)}, bf16[48,1024]{1,0:T(8,128)(2,1)S(1)}, u32[]{:S(2)}, u32[]{:S(2)}) collective-permute-start(bf16[48,1024]{1,0:T(8,128)(2,1)S(1)} %constant_dynamic-update-slice_fusion.rest_0_), channel_id=1, source_target_pairs={{0,6},{1,7},{2,4},{3,5},{4,2},{5,3},{6,0},{7,1},{8,14},{9,15},{10,... | collective-permute-start | bytes 294920 | tf_op jit(solution)/shard_map/ppermute | solution.py:222
  7.6 0.2 collective-permute-start
  7.9 0.7 %copy-done = s32[8]{0:T(128)S(1)} copy-done((s32[8]{0:T(128)S(1)}, s32[8]{0:T(128)}, u32[]{:S(2)}) %copy-start) | copy-done | bytes 56
  8.5 3.4 %shard_map.119 = (bf16[4096,128]{1,0:T(8,128)(2,1)S(1)}, bf16[4096,256]{1,0:T(8,128)(2,1)S(1)}, bf16[128,4096]{1,0:T(8,128)(2,1)S(1)}, bf16[128,4096]{1,0:T(8,12...) custom-call(s32[8]{0:T(128)S(1)} %copy-done, ...), custom_call_target="tpu_custom_call" | custom-call | flops 2097152000 | bytes 8388608 | tf_op jit(solution)/shard_map/pallas_call | solution.py:89
  11.9 2.2 %collective-permute-done.2.rest_3_ = bf16[48,1024]{1,0:T(8,128)(2,1)S(1)} collective-permute-done((bf16[48,1024]{1,0:T(8,128)(2,1)S(1)}, bf16[48,1024]{1,0:T(8,128)(2,1)S(1)}, u32[]{:S(2)}, u32[]{:S(2)}) %collective-permute-start.2) | collective-permute-done | bytes 98336 | tf_op jit(solution)/shard_map/ppermute | solution.py:222
  14.2 1.1 %collective-permute-done.rest_1_ = bf16[48,1024]{1,0:T(8,128)(2,1)S(1)} collective-permute-done((bf16[48,1024]{1,0:T(8,128)(2,1)S(1)}, bf16[48,1024]{1,0:T(8,128)(2,1)S(1)}, u32[]{:S(2)}, u32[]{:S(2)}) %collective-permute-start) | collective-permute-done | bytes 98336 | tf_op jit(solution)/shard_map/ppermute | solution.py:222
  15.3 0.5 %collective-permute-start.5 = (bf16[48,1024]{1,0:T(8,128)(2,1)S(1)}, bf16[48,1024]{1,0:T(8,128)(2,1)S(1)}, u32[]{:S(2)}, u32[]{:S(2)}) collective-permute-start(bf16[48,1024]{1,0:T(8,128)(2,1)S(1)} %collective-permute-done.1.rest_2_), channel_id=1, source_target_pairs={{0,1},{1,0},{2,3},{3,2},{4,5},{5,4},{6,7},{7,6},{8,9},{9,8},{10,11... | collective-permute-start | bytes 294920 | tf_op jit(solution)/shard_map/ppermute | solution.py:227
  15.8 0.8 %collective-permute-done.4.rest_5_ = bf16[48,1024]{1,0:T(8,128)(2,1)S(1)} collective-permute-done((bf16[48,1024]{1,0:T(8,128)(2,1)S(1)}, bf16[48,1024]{1,0:T(8,128)(2,1)S(1)}, u32[]{:S(2)}, u32[]{:S(2)}) %collective-permute-start.4) | collective-permute-done | bytes 98336 | tf_op jit(solution)/shard_map/ppermute | solution.py:227
  16.6 0.2 collective-permute-done.5.rest_6_
  16.8 0.4 collective-permute-done.6.rest_7_
  17.1 6.5 %shard_map.120 = (bf16[128,4096]{1,0:T(8,128)(2,1)}, bf16[128,512]{1,0:T(8,128)(2,1)}, bf16[128,512]{1,0:T(8,128)(2,1)}, f32[48,1024]{1,0:T(8,128)S(1)}, f32[48,...) custom-call(f32[128,128]{1,0:T(8,128)S(1)} %get-tuple-element.37.live_ref, ...), custom_call_target="tpu_custom_call" | custom-call | flops 2684354560 | bytes 5242880 | tf_op jit(solution)/shard_map/pallas_call | solution.py:194
  23.6 0.2 collective-permute-start.7
  23.7 1.6 %collective-permute-done.7 = bf16[4,48,1024]{2,1,0:T(8,128)(2,1)S(1)} collective-permute-done((bf16[4,48,1024]{2,1,0:T(8,128)(2,1)S(1)}, bf16[4,48,1024]{2,1,0:T(8,128)(2,1)S(1)}, u32[]{:S(2)}, u32[]{:S(2)}) %collective-permute-start.7) | collective-permute-done | bytes 393248 | tf_op jit(solution)/shard_map/ppermute | solution.py:227
  25.3 0.1 fusion.2
  25.4 3.5 %collective-permute-start.8 = (bf16[48,1024]{1,0:T(8,128)(2,1)S(1)}, bf16[48,1024]{1,0:T(8,128)(2,1)S(1)}, u32[]{:S(2)}, u32[]{:S(2)}) collective-permute-start(bf16[48,1024]{1,0:T(8,128)(2,1)S(1)} %get-tuple-element.55), channel_id=1, source_target_pairs={{0,4},{1,5},{2,6},{3,7},{4,0},{5,1},{6,2},{7,3},{8,12},{9,13},{10,... | collective-permute-start | bytes 294920 | tf_op jit(solution)/shard_map/ppermute | solution.py:222
  28.9 0.5 %collective-permute-start.10 = (bf16[48,1024]{1,0:T(8,128)(2,1)S(1)}, bf16[48,1024]{1,0:T(8,128)(2,1)S(1)}, u32[]{:S(2)}, u32[]{:S(2)}) collective-permute-start(bf16[48,1024]{1,0:T(8,128)(2,1)S(1)} %get-tuple-element.56), channel_id=1, source_target_pairs={{0,6},{1,7},{2,4},{3,5},{4,2},{5,3},{6,0},{7,1},{8,14},{9,15},{10,... | collective-permute-start | bytes 294920 | tf_op jit(solution)/shard_map/ppermute | solution.py:222
  29.4 0.2 collective-permute-start.9
  29.6 7.0 %collective-permute-done.8 = bf16[48,1024]{1,0:T(8,128)(2,1)S(1)} collective-permute-done((bf16[48,1024]{1,0:T(8,128)(2,1)S(1)}, bf16[48,1024]{1,0:T(8,128)(2,1)S(1)}, u32[]{:S(2)}, u32[]{:S(2)}) %collective-permute-start.8) | collective-permute-done | bytes 98336 | tf_op jit(solution)/shard_map/ppermute | solution.py:222
  36.6 1.0 %collective-permute-done.9 = bf16[48,1024]{1,0:T(8,128)(2,1)S(1)} collective-permute-done((bf16[48,1024]{1,0:T(8,128)(2,1)S(1)}, bf16[48,1024]{1,0:T(8,128)(2,1)S(1)}, u32[]{:S(2)}, u32[]{:S(2)}) %collective-permute-start.9) | collective-permute-done | bytes 98336 | tf_op jit(solution)/shard_map/ppermute | solution.py:222
  37.7 0.6 %fusion.7 = (bf16[48,512]{1,0:T(8,128)(2,1)}, bf16[48,512]{1,0:T(8,128)(2,1)}) fusion(bf16[48,1024]{1,0:T(8,128)(2,1)S(1)} %fusion.6), kind=kLoop, calls=%fused_computation.17 | loop fusion | bytes 196608 | tf_op jit(solution)/shard_map/slice | solution.py:246
  (7 shorter events, 0.1 us)
Async XLA Ops:
  2.2 13.6 %collective-permute-start.3 = (bf16[48,1024]{1,0:T(8,128)(2,1)S(1)}, bf16[48,1024]{1,0:T(8,128)(2,1)S(1)}, u32[]{:S(2)}, u32[]{:S(2)}) collective-permute-start(bf16[48,1024]{1,0:T(8,128)(2,1)S(1)} %constant_dynamic-update-slice_fusion.rest_0_), channel_id=1, source_target_pairs={{0,1},{1,0},{2,3},{3,2},{4,5},{5,4},{6,7},{7,6},{8,9},{9,8},{10,11... | collective-permute-start | bytes 294920 | tf_op jit(solution)/shard_map/ppermute | solution.py:227
  2.7 11.5 %collective-permute-start.2 = (bf16[48,1024]{1,0:T(8,128)(2,1)S(1)}, bf16[48,1024]{1,0:T(8,128)(2,1)S(1)}, u32[]{:S(2)}, u32[]{:S(2)}) collective-permute-start(bf16[48,1024]{1,0:T(8,128)(2,1)S(1)} %constant_dynamic-update-slice_fusion.rest_0_), channel_id=1, source_target_pairs={{0,4},{1,5},{2,6},{3,7},{4,0},{5,1},{6,2},{7,3},{8,12},{9,13},{10,... | collective-permute-start | bytes 294920 | tf_op jit(solution)/shard_map/ppermute | solution.py:222
  6.3 7.9 %collective-permute-start.1 = (bf16[48,1024]{1,0:T(8,128)(2,1)S(1)}, bf16[48,1024]{1,0:T(8,128)(2,1)S(1)}, u32[]{:S(2)}, u32[]{:S(2)}) collective-permute-start(bf16[48,1024]{1,0:T(8,128)(2,1)S(1)} %constant_dynamic-update-slice_fusion.rest_0_), channel_id=1, source_target_pairs={{0,6},{1,7},{2,4},{3,5},{4,2},{5,3},{6,0},{7,1},{8,14},{9,15},{10,... | collective-permute-start | bytes 294920 | tf_op jit(solution)/shard_map/ppermute | solution.py:222
  7.6 7.7 %collective-permute-start = (bf16[48,1024]{1,0:T(8,128)(2,1)S(1)}, bf16[48,1024]{1,0:T(8,128)(2,1)S(1)}, u32[]{:S(2)}, u32[]{:S(2)}) collective-permute-start(bf16[48,1024]{1,0:T(8,128)(2,1)S(1)} %constant_dynamic-update-slice_fusion.rest_0_), channel_id=1, source_target_pairs={{0,2},{1,3},{2,0},{3,1},{4,6},{5,7},{6,4},{7,5},{8,10},{9,11},{10,... | collective-permute-start | bytes 294920 | tf_op jit(solution)/shard_map/ppermute | solution.py:222
  7.9 0.7 %copy-start = (s32[8]{0:T(128)S(1)}, s32[8]{0:T(128)}, u32[]{:S(2)}) copy-start(s32[8]{0:T(128)} %len_ref.1) | copy-start | bytes 100
  15.3 1.3 %collective-permute-start.4 = (bf16[48,1024]{1,0:T(8,128)(2,1)S(1)}, bf16[48,1024]{1,0:T(8,128)(2,1)S(1)}, u32[]{:S(2)}, u32[]{:S(2)}) collective-permute-start(bf16[48,1024]{1,0:T(8,128)(2,1)S(1)} %collective-permute-done.rest_1_), channel_id=1, source_target_pairs={{0,1},{1,0},{2,3},{3,2},{4,5},{5,4},{6,7},{7,6},{8,9},{9,8},{10,11... | collective-permute-start | bytes 294920 | tf_op jit(solution)/shard_map/ppermute | solution.py:227
  15.3 1.5 %collective-permute-start.5 = (bf16[48,1024]{1,0:T(8,128)(2,1)S(1)}, bf16[48,1024]{1,0:T(8,128)(2,1)S(1)}, u32[]{:S(2)}, u32[]{:S(2)}) collective-permute-start(bf16[48,1024]{1,0:T(8,128)(2,1)S(1)} %collective-permute-done.1.rest_2_), channel_id=1, source_target_pairs={{0,1},{1,0},{2,3},{3,2},{4,5},{5,4},{6,7},{7,6},{8,9},{9,8},{10,11... | collective-permute-start | bytes 294920 | tf_op jit(solution)/shard_map/ppermute | solution.py:227
  15.8 1.3 %collective-permute-start.6 = (bf16[48,1024]{1,0:T(8,128)(2,1)S(1)}, bf16[48,1024]{1,0:T(8,128)(2,1)S(1)}, u32[]{:S(2)}, u32[]{:S(2)}) collective-permute-start(bf16[48,1024]{1,0:T(8,128)(2,1)S(1)} %collective-permute-done.2.rest_3_), channel_id=1, source_target_pairs={{0,1},{1,0},{2,3},{3,2},{4,5},{5,4},{6,7},{7,6},{8,9},{9,8},{10,11... | collective-permute-start | bytes 294920 | tf_op jit(solution)/shard_map/ppermute | solution.py:227
  23.6 1.7 %collective-permute-start.7 = (bf16[4,48,1024]{2,1,0:T(8,128)(2,1)S(1)}, bf16[4,48,1024]{2,1,0:T(8,128)(2,1)S(1)}, u32[]{:S(2)}, u32[]{:S(2)}) collective-permute-start(bf16[4,48,1024]{2,1,0:T(8,128)(2,1)S(1)} %get-tuple-element.51), channel_id=1, source_target_pairs={{0,1},{1,0},{2,3},{3,2},{4,5},{5,4},{6,7},{7,6},{8,9},{9,8},{10,11... | collective-permute-start | bytes 1179656 | tf_op jit(solution)/shard_map/ppermute | solution.py:227
  25.4 11.2 %collective-permute-start.8 = (bf16[48,1024]{1,0:T(8,128)(2,1)S(1)}, bf16[48,1024]{1,0:T(8,128)(2,1)S(1)}, u32[]{:S(2)}, u32[]{:S(2)}) collective-permute-start(bf16[48,1024]{1,0:T(8,128)(2,1)S(1)} %get-tuple-element.55), channel_id=1, source_target_pairs={{0,4},{1,5},{2,6},{3,7},{4,0},{5,1},{6,2},{7,3},{8,12},{9,13},{10,... | collective-permute-start | bytes 294920 | tf_op jit(solution)/shard_map/ppermute | solution.py:222
  28.9 7.7 %collective-permute-start.10 = (bf16[48,1024]{1,0:T(8,128)(2,1)S(1)}, bf16[48,1024]{1,0:T(8,128)(2,1)S(1)}, u32[]{:S(2)}, u32[]{:S(2)}) collective-permute-start(bf16[48,1024]{1,0:T(8,128)(2,1)S(1)} %get-tuple-element.56), channel_id=1, source_target_pairs={{0,6},{1,7},{2,4},{3,5},{4,2},{5,3},{6,0},{7,1},{8,14},{9,15},{10,... | collective-permute-start | bytes 294920 | tf_op jit(solution)/shard_map/ppermute | solution.py:222
  29.4 8.2 %collective-permute-start.9 = (bf16[48,1024]{1,0:T(8,128)(2,1)S(1)}, bf16[48,1024]{1,0:T(8,128)(2,1)S(1)}, u32[]{:S(2)}, u32[]{:S(2)}) collective-permute-start(bf16[48,1024]{1,0:T(8,128)(2,1)S(1)} %get-tuple-element.57), channel_id=1, source_target_pairs={{0,2},{1,3},{2,0},{3,1},{4,6},{5,7},{6,4},{7,5},{8,10},{9,11},{10,... | collective-permute-start | bytes 294920 | tf_op jit(solution)/shard_map/ppermute | solution.py:222

commit v2 on v1

v2 whole, which is shorter than its diff:
```python
import functools

import jax
import jax.numpy as jnp
from jax import lax
from jax.experimental import pallas as pl
from jax.experimental.pallas import tpu as pltpu
from jax.sharding import PartitionSpec as P

HEAD_DIM = 128
SCALE = HEAD_DIM ** (-0.5)
LOG2E = 1.4426950408889634
NT = (((1,), (1,)), ((), ()))
CORES = 2
CHUNK = 32
DELTA_TERMS = 2
BF16 = jnp.bfloat16
F32 = jnp.float32
VMEM_SPEC = pl.BlockSpec(memory_space=pltpu.VMEM)
HBM_SPEC = pl.BlockSpec(memory_space=pltpu.HBM)
SMEM_SPEC = pl.BlockSpec(memory_space=pltpu.SMEM)
MIB = 1024 * 1024
PARAMS = pltpu.CompilerParams(vmem_limit_bytes=24 * MIB)


def shape(*dims):
    return jax.ShapeDtypeStruct(dims, BF16)


def dot(a, b, dims=None):
    if dims is None:
        return jnp.dot(a, b, preferred_element_type=F32)
    return lax.dot_general(a, b, dims, preferred_element_type=F32)


def head_slice(index):
    return slice(index * HEAD_DIM, (index + 1) * HEAD_DIM)


def in_hbm(*arrays):
    return [pltpu.with_memory_space_constraint(x, pltpu.HBM) for x in arrays]


def prepare_kernel(groups, len_ref, *refs):
    wide_in, narrow_in, refs = refs[:3], refs[3:5], refs[5:]
    (q_rows, g_rows, q_cols, g_cols, live_ref), narrow_out, refs = refs[:5], refs[5:7], refs[7:]
    wide_buf, (wide_sem, narrow_sem) = refs[:3], refs[3:]
    rows = wide_buf[0].shape[0]
    width = wide_buf[0].shape[1] // groups
    wide = [
        [
            pltpu.make_async_copy(src.at[:, group * width : (group + 1) * width], buf.at[:, group * width : (group + 1) * width], wide_sem.at[group, i])
            for i, (src, buf) in enumerate(zip(wide_in, wide_buf))
        ]
        for group in range(groups)
    ]
    narrow = [pltpu.make_async_copy(src, out, narrow_sem.at[i]) for i, (src, out) in enumerate(zip(narrow_in, narrow_out))]
    for copy in sum(wide, []) + narrow:
        copy.start()
    length = len_ref[lax.axis_index("seq")]
    live_ref[...] = jnp.where(lax.broadcasted_iota(jnp.int32, live_ref.shape, 0) < length, 1.0, 0.0)
    lane = lax.broadcasted_iota(jnp.int32, (rows, HEAD_DIM), 1)
    square = (HEAD_DIM, HEAD_DIM)
    same = lax.broadcasted_iota(jnp.int32, square, 0) == lax.broadcasted_iota(jnp.int32, square, 1)
    identity = jnp.where(same, 1.0, 0.0).astype(BF16)
    ones = jnp.ones((2 * HEAD_DIM, HEAD_DIM), BF16)
    q_ref, o_ref, g_ref = wide_buf
    heads = width // HEAD_DIM
    for group in range(groups):
        for copy in wide[group]:
            copy.wait()
        for head in range(group * heads, (group + 1) * heads):
            cols = head_slice(head)
            span = slice(head * rows, (head + 1) * rows)
            g = g_ref[:, cols]
            product = g.astype(F32) * o_ref[:, cols].astype(F32)
            high = product.astype(BF16)
            low = (product - high.astype(F32)).astype(BF16)
            left = dot(jnp.concatenate([high, low], axis=1), ones)
            terms = jnp.zeros((rows, HEAD_DIM), F32)
            for term in range(DELTA_TERMS):
                rounded = left.astype(BF16).astype(F32)
                terms = jnp.where(lane == term, rounded, terms)
                left = left - rounded
            q_rows[span, :] = q_ref[:, cols]
            g_rows[span, :HEAD_DIM] = g
            g_rows[span, HEAD_DIM:] = terms.astype(BF16)
        span = slice(group * heads * rows, (group + 1) * heads * rows)
        q_cols[:, span] = dot(identity, q_rows[span, :], NT).astype(BF16)
        g_cols[:, span] = dot(identity, g_rows[span, :HEAD_DIM], NT).astype(BF16)
    for copy in narrow:
        copy.wait()


def prepare(lengths, q, o, g, rk, rv):
    rows, width = q.shape
    groups = rk.shape[1] // HEAD_DIM
    flat = rows * width // HEAD_DIM
    narrow = [rk, rv]
    return pl.pallas_call(
        functools.partial(prepare_kernel, groups),
        in_specs=[SMEM_SPEC] + [HBM_SPEC] * 5,
        out_specs=[VMEM_SPEC] * 7,
        out_shape=[
            shape(flat, HEAD_DIM),
            shape(flat, 2 * HEAD_DIM),
            shape(HEAD_DIM, flat),
            shape(HEAD_DIM, flat),
            jax.ShapeDtypeStruct((rows, HEAD_DIM), F32),
        ]
        + [shape(*x.shape) for x in narrow],
        scratch_shapes=[pltpu.VMEM((rows, width), BF16)] * 3
        + [pltpu.SemaphoreType.DMA((groups, 3)), pltpu.SemaphoreType.DMA((2,))],
        compiler_params=PARAMS,
        cost_estimate=pl.CostEstimate(flops=rows * width * 4000, bytes_accessed=16 * rows * width, transcendentals=0),
    )(lengths, *in_hbm(q, o, g, *narrow))


def read_pieces(joined, refs):
    k_refs, v_refs = [], []
    for both in joined:
        k_refs.append(refs[0].at[0] if both else refs[0])
        v_refs.append(refs[0].at[1] if both else refs[1])
        refs = refs[1 if both else 2 :]
    return k_refs, v_refs, refs


def attention_kernel(chips, piece_rows, joined, live_ref, q_rows, g_rows, q_cols, g_cols, rk_ref, rv_ref, *rest):
    pieces = CORES * chips
    k_refs, v_refs, rest = read_pieces(joined, rest)
    whole, rest = rest[:3], rest[3:]
    d_own, d_other, rest = rest[:chips], rest[chips : 2 * chips], rest[2 * chips :]
    k_buf, v_buf, s_buf, dp_buf, p_buf, ds_buf, dq_buf, drk_buf, drv_buf, sem = rest
    rows, width = rk_ref.shape
    groups = width // HEAD_DIM
    block = q_rows.shape[0] // groups // 2
    per_half = block // rows
    keys = k_buf.shape[1]
    prompt = keys - rows
    diagonal = lax.broadcasted_iota(jnp.int32, (CHUNK, rows), 1) - lax.broadcasted_iota(jnp.int32, (CHUNK, rows), 0)
    minus = jnp.where(lax.broadcasted_iota(jnp.int32, (keys, HEAD_DIM), 1) < DELTA_TERMS, -1.0, 0.0).astype(BF16)

    def place(half):
        return slice(half * block, (half + 1) * block)

    def load_keys(group):
        cols = head_slice(group)
        for i in range(pieces):
            span = slice(i * piece_rows, (i + 1) * piece_rows)
            k_buf[group, span, :] = k_refs[i][:, cols]
            v_buf[group, span, :HEAD_DIM] = v_refs[i][:, cols]
        k_buf[group, prompt:, :] = rk_ref[:, cols]
        v_buf[group, prompt:, :HEAD_DIM] = rv_ref[:, cols]
        v_buf[group, :, HEAD_DIM:] = minus

    def scores(half):
        s_buf[half % 2] = dot(q_rows[place(half), :], k_buf[half // 2], NT)

    def prob_grads(half):
        dp_buf[half % 2] = dot(g_rows[place(half), :], v_buf[half // 2], NT)

    def soften(half, low):
        slot = half % 2
        first = low % rows
        span = slice(low, low + CHUNK)
        s = s_buf[slot, span, :]
        s = jnp.concatenate([s[:, :prompt], jnp.where(diagonal > first, -1e30, s[:, prompt:])], axis=1)
        e = jnp.exp2((s - jnp.max(s, axis=1, keepdims=True)) * (SCALE * LOG2E))
        weight = (1.0 / jnp.sum(e, axis=1, keepdims=True)) * live_ref[first : first + CHUNK, :]
        p = e * jnp.concatenate([weight] * (keys // HEAD_DIM), axis=1)
        p_buf[slot, span, :] = p.astype(BF16)
        ds_buf[slot, span, :] = (p * dp_buf[slot, span, :]).astype(BF16)

    def query_grads(half):
        dq = (dot(ds_buf[half % 2], k_buf[half // 2]) * SCALE).astype(BF16)
        for i in range(per_half):
            dq_buf[:, head_slice(half * per_half + i)] = dq[i * rows : (i + 1) * rows]

    sums = {}

    def key_grads(half):
        sums["k", half] = dot(q_cols[:, place(half)], ds_buf[half % 2])

    def value_grads(half):
        sums["v", half] = dot(g_cols[:, place(half)], p_buf[half % 2])

    def finish(group):
        cols = head_slice(group)
        dk = ((sums["k", 2 * group] + sums["k", 2 * group + 1]) * SCALE).T
        dv = (sums["v", 2 * group] + sums["v", 2 * group + 1]).T
        for kind, grad in enumerate((dk, dv)):
            for i in range(chips):
                d_own[i][kind, :, cols] = grad[i * piece_rows : (i + 1) * piece_rows]
                d_other[i][kind, :, cols] = grad[(chips + i) * piece_rows : (chips + i + 1) * piece_rows].astype(BF16)
        drk_buf[:, cols] = dk[prompt:].astype(BF16)
        drv_buf[:, cols] = dv[prompt:].astype(BF16)
        copies = []
        for i, (buf, out) in enumerate(zip((dq_buf, drk_buf, drv_buf), whole)):
            step = buf.shape[1] // groups
            part = slice(group * step, (group + 1) * step)
            copies.append(pltpu.make_async_copy(buf.at[:, part], out.at[:, part], sem.at[group, i]))
            copies[-1].start()
        return copies

    halves = 2 * groups
    chunks = range(0, block, CHUNK)
    load_keys(0)
    scores(0)
    prob_grads(0)
    stores = []
    for half in range(halves + 1):
        tasks = []
        if half + 1 < halves:
            if (half + 1) % 2 == 0:
                load_keys((half + 1) // 2)
            tasks += [functools.partial(task, half + 1) for task in (scores, prob_grads)]
        if half:
            tasks += [functools.partial(task, half - 1) for task in (key_grads, value_grads, query_grads)]
        done = 0
        for i, low in enumerate(chunks if half < halves else ()):
            while done < len(tasks) and done * len(chunks) <= i * len(tasks):
                tasks[done]()
                done += 1
            soften(half, low)
        for task in tasks[done:]:
            task()
        if half and half % 2 == 0:
            stores += finish(half // 2 - 1)
    for copy in stores:
        copy.wait()


def attention(prepared, kv_pieces):
    q_rows, g_rows, q_cols, g_cols, live, rk, rv = prepared
    rows, kv_width = rk.shape
    groups = kv_width // HEAD_DIM
    flat = q_rows.shape[0]
    wide = (rows, flat // rows * HEAD_DIM)
    pieces = len(kv_pieces)
    chips = pieces // CORES
    piece_rows = kv_pieces[0][0].shape[-2]
    joined = [len(piece) == 1 for piece in kv_pieces]
    flat_pieces = sum(kv_pieces, [])
    keys = pieces * piece_rows + rows
    block = flat // groups // 2
    return pl.pallas_call(
        functools.partial(attention_kernel, chips, piece_rows, joined),
        in_specs=[VMEM_SPEC] * (7 + len(flat_pieces)),
        out_specs=[HBM_SPEC] * 3 + [VMEM_SPEC] * (2 * chips),
        out_shape=[shape(*wide), shape(rows, kv_width), shape(rows, kv_width)]
        + [jax.ShapeDtypeStruct((2, piece_rows, kv_width), F32)] * chips
        + [shape(2, piece_rows, kv_width)] * chips,
        scratch_shapes=[
            pltpu.VMEM((groups, keys, HEAD_DIM), BF16),
            pltpu.VMEM((groups, keys, 2 * HEAD_DIM), BF16),
            pltpu.VMEM((2, block, keys), F32),
            pltpu.VMEM((2, block, keys), F32),
            pltpu.VMEM((2, block, keys), BF16),
            pltpu.VMEM((2, block, keys), BF16),
            pltpu.VMEM(wide, BF16),
            pltpu.VMEM((rows, kv_width), BF16),
            pltpu.VMEM((rows, kv_width), BF16),
            pltpu.SemaphoreType.DMA((groups, 3)),
        ],
        compiler_params=PARAMS,
        cost_estimate=pl.CostEstimate(
            flops=10 * flat * keys * HEAD_DIM, bytes_accessed=10 * flat * HEAD_DIM, transcendentals=flat * keys
        ),
    )(live, q_rows, g_rows, q_cols, g_cols, rk, rv, *flat_pieces)


def exchange(x, links):
    routes = [(a, b) for pair in links for a, b in (pair, pair[::-1])]
    pairs = [(CORES * a + core, CORES * b + core) for a, b in routes for core in range(CORES)]
    return lax.ppermute(x, "seq", pairs)


def chip_links(chips, step):
    return [(chip, chip ^ step) for chip in range(chips) if chip < chip ^ step]


def swap_core(x, chips):
    pairs = [(CORES * chip + core, CORES * chip + 1 - core) for chip in range(chips) for core in range(CORES)]
    return lax.ppermute(x, "seq", pairs)


def local(chips, queries, outputs, out_grads, resp_keys, resp_values, lengths, prompt_keys, prompt_values):
    steps = list(range(1, chips))
    raw = [prompt_keys, prompt_values]
    kind = lax.broadcasted_iota(jnp.int32, (2,) + prompt_keys.shape, 0)
    kv = [jnp.where(kind == 0, prompt_keys[None], prompt_values[None])]
    far = [[exchange(x, chip_links(chips, step)) for x in (raw if step == 2 else kv)] for step in steps]
    prepared = prepare(lengths, queries[0], outputs[0], out_grads[0], resp_keys[0], resp_values[0])
    live = prepared[4]
    far = [[lax.optimization_barrier((x, live))[0] for x in piece] for piece in far]
    own = [kv] + far
    other = [[swap_core(x, chips) for x in piece] for piece in own]
    dq, drk, drv, *grads = attention(prepared, own + other)
    both = [grads[i] + swap_core(grads[chips + i], chips).astype(F32) for i in range(chips)]
    back = [exchange(both[step].astype(BF16), chip_links(chips, step)) for step in steps[1:] + steps[:1]]
    total = sum([x.astype(F32) for x in back], both[0]).astype(BF16)
    return dq[None], drk[None], drv[None], total[0], total[1]


def solution(mesh):
    chips = mesh.shape["seq"] // CORES
    split = ("dp", "seq")
    row3 = P(split, None, None)
    row2 = P(split, None)
    return jax.shard_map(
        functools.partial(local, chips),
        mesh=mesh,
        in_specs=(row3, row3, row3, row3, row3, P("dp"), row2, row2),
        out_specs=(row3, row3, row3, row2, row2),
        check_vma=False,
    )
```

time: 38.5 us -> 37.9 us (0.984)
  waiting for transfers between devices: 14.3 us -> 9.86 us
  starting transfers between devices: 10.5 us -> 14.6 us
  local copies, waits for them, and re-layouts: 2.9 us -> 1.3 us
  other arithmetic: 0.14 us -> 1.03 us
    ppermute x6 -> x7, starting transfers between devices: 9.34 us -> 12.4 us  [exchange(): return lax.ppermute(x, 'seq', pairs)]
    ppermute x6 -> x7, waiting for transfers between devices: 11.4 us -> 8.69 us  [exchange(): return lax.ppermute(x, 'seq', pairs)]
    ppermute x5 -> x9, waiting for transfers between devices: 2.87 us -> 1.17 us  [swap_core(): return lax.ppermute(x, 'seq', pairs)]
    ppermute x5 -> x9, starting transfers between devices: 1.12 us -> 2.18 us  [swap_core(): return lax.ppermute(x, 'seq', pairs)]
    select_n x0 -> x1, other arithmetic: none -> 0.91 us  [local(): kv = [jnp.where(kind == 0, prompt_keys[None], prompt_values[None])]]
    unnamed x3 -> x2, local copies, waits for them, and re-layouts: 1.46 us -> 0.66 us
    concatenate x1 -> x0, local copies, waits for them, and re-layouts: 0.8 us -> none  [local(): kv = jnp.concatenate([prompt_keys, prompt_values], axis=1)]
    slice x1 -> x0, local copies, waits for them, and re-layouts: 0.64 us -> none  [local(): total[:, kv_width:]]
  transfers between devices with their start and end apart: 11 -> 16, of which waited for: 8 -> 6; matrix products, arithmetic and copies ran while one was open for 0% -> 3% of each run, Pallas kernels for 9% -> 9%
where the time goes in v2:
time: 37.9 us; the launch traced here: 37.7 us
  starting transfers between devices  14.6 us (39%)
  Pallas kernels  10.2 us (27%)
  waiting for transfers between devices  9.86 us (26%)
  local copies, waits for them, and re-layouts  1.3 us (3%)
  other arithmetic  1.03 us (3%)
  between operations  0.71 us (2%)
    ppermute x7, starting transfers between devices, exchange(): return lax.ppermute(x, 'seq', pairs)  12.4 us
    ppermute x7, waiting for transfers between devices, exchange(): return lax.ppermute(x, 'seq', pairs)  8.69 us
    pallas_call x1, Pallas kernels, attention(): pl.pallas_call(functools.partial(attention_kernel, chips, piece_rows, joi...  6.67 us
    pallas_call x1, Pallas kernels, prepare(): pl.pallas_call(functools.partial(prepare_kernel, groups), in_specs=[SMEM_...  3.57 us
    ppermute x9, starting transfers between devices, swap_core(): return lax.ppermute(x, 'seq', pairs)  2.18 us
    ppermute x9, waiting for transfers between devices, swap_core(): return lax.ppermute(x, 'seq', pairs)  1.17 us
    select_n x1, other arithmetic, local(): kv = [jnp.where(kind == 0, prompt_keys[None], prompt_values[None])]  0.91 us
  transfers between devices with their start and end apart: 16, of which 6 were waited for; matrix products, arithmetic and copies ran while one was open for 3% of the time, Pallas kernels for 9%

profile of v2, /device:TPU:0, one launch (start us, length us, event | category | flops | bytes accessed | tf_op | source)
XLA Modules:
  0.0 37.7 jit_solution(7943167601608613077)
XLA Ops:
  0.6 4.1 %collective-permute-start.1 = (bf16[48,512]{1,0:T(8,128)(2,1)}, bf16[48,512]{1,0:T(8,128)(2,1)S(1)}, u32[]{:S(2)}, u32[]{:S(2)}) collective-permute-start(bf16[48,512]{1,0:T(8,128)(2,1)} %param.14), channel_id=1, source_target_pairs={{0,4},{1,5},{4,0},{5,1},{2,6},{3,7},{6,2},{7,3},{8,12},{9,13},{12,... | collective-permute-start | bytes 147464 | tf_op jit(solution)/shard_map/ppermute | solution.py:275
  4.7 0.1 collective-permute-start.2
  4.8 0.9 %broadcast_select_fusion.rest_0_ = bf16[2,48,512]{2,1,0:T(8,128)(2,1)S(1)} fusion(pred[2]{0:T(512)(128)(4,1)S(1)} %iota_compare_fusion, bf16[48,512]{1,0:T(8,128)(2,1)} %param.15, bf16[48,512]{1,0:T(8,128)(2,1)} %param.14), kind=kLoop, calls=%fused_computation.4 | loop fusion | flops 49152 | bytes 196610 | tf_op jit(solution)/shard_map/jit(_where)/select_n | solution.py:291
  5.7 0.1 collective-permute-start.4
  5.8 3.9 %collective-permute-start.3 = (bf16[2,48,512]{2,1,0:T(8,128)(2,1)S(1)}, bf16[2,48,512]{2,1,0:T(8,128)(2,1)S(1)}, u32[]{:S(2)}, u32[]{:S(2)}) collective-permute-start(bf16[2,48,512]{2,1,0:T(8,128)(2,1)S(1)} %broadcast_select_fusion.rest_0_), channel_id=1, source_target_pairs={{0,6},{1,7},{6,0},{7,1},{2,4},{3,5},{4,2},{5,3},{8,14},{9,15},{14,... | collective-permute-start | bytes 294920 | tf_op jit(solution)/shard_map/ppermute | solution.py:275
  9.7 0.7 %copy-done = s32[8]{0:T(128)S(1)} copy-done((s32[8]{0:T(128)S(1)}, s32[8]{0:T(128)}, u32[]{:S(2)}) %copy-start) | copy-done | bytes 56
  10.4 3.6 %shard_map.119 = (bf16[4096,128]{1,0:T(8,128)(2,1)S(1)}, bf16[4096,256]{1,0:T(8,128)(2,1)S(1)}, bf16[128,4096]{1,0:T(8,128)(2,1)S(1)}, bf16[128,4096]{1,0:T(8,12...) custom-call(s32[8]{0:T(128)S(1)} %copy-done, ...), custom_call_target="tpu_custom_call" | custom-call | flops 2097152000 | bytes 8388608 | tf_op jit(solution)/shard_map/pallas_call | solution.py:100
  14.0 1.3 %collective-permute-done.rest_1_ = bf16[2,48,512]{2,1,0:T(8,128)(2,1)S(1)} collective-permute-done((bf16[2,48,512]{2,1,0:T(8,128)(2,1)S(1)}, bf16[2,48,512]{2,1,0:T(8,128)(2,1)S(1)}, u32[]{:S(2)}, u32[]{:S(2)}) %collective-permute-start) | collective-permute-done | bytes 98336 | tf_op jit(solution)/shard_map/ppermute | solution.py:275
  15.3 0.5 %collective-permute-start.8 = (bf16[2,48,512]{2,1,0:T(8,128)(2,1)S(1)}, bf16[2,48,512]{2,1,0:T(8,128)(2,1)S(1)}, u32[]{:S(2)}, u32[]{:S(2)}) collective-permute-start(bf16[2,48,512]{2,1,0:T(8,128)(2,1)S(1)} %collective-permute-done.3.rest_4_), channel_id=1, source_target_pairs={{0,1},{1,0},{2,3},{3,2},{4,5},{5,4},{6,7},{7,6},{8,9},{9,8},{10,11... | collective-permute-start | bytes 294920 | tf_op jit(solution)/shard_map/ppermute | solution.py:284
  15.9 0.4 %collective-permute-start.7 = (bf16[48,512]{1,0:T(8,128)(2,1)S(1)}, bf16[48,512]{1,0:T(8,128)(2,1)S(1)}, u32[]{:S(2)}, u32[]{:S(2)}) collective-permute-start(bf16[48,512]{1,0:T(8,128)(2,1)S(1)} %collective-permute-done.2.rest_3_), channel_id=1, source_target_pairs={{0,1},{1,0},{2,3},{3,2},{4,5},{5,4},{6,7},{7,6},{8,9},{9,8},{10,11... | collective-permute-start | bytes 147464 | tf_op jit(solution)/shard_map/ppermute | solution.py:284
  16.3 0.7 %collective-permute-done.6.rest_7_ = bf16[48,512]{1,0:T(8,128)(2,1)S(1)} collective-permute-done((bf16[48,512]{1,0:T(8,128)(2,1)S(1)}, bf16[48,512]{1,0:T(8,128)(2,1)S(1)}, u32[]{:S(2)}, u32[]{:S(2)}) %collective-permute-start.6) | collective-permute-done | bytes 49184 | tf_op jit(solution)/shard_map/ppermute | solution.py:284
  17.0 0.2 collective-permute-done.7.rest_8_
  17.2 6.7 %shard_map.120 = (bf16[128,4096]{1,0:T(8,128)(2,1)}, bf16[128,512]{1,0:T(8,128)(2,1)}, bf16[128,512]{1,0:T(8,128)(2,1)}, f32[2,48,512]{2,1,0:T(8,128)S(1)}, f32[...) custom-call(f32[128,128]{1,0:T(8,128)S(1)} %get-tuple-element.27.liv, ...), custom_call_target="tpu_custom_call" | custom-call | flops 2684354560 | bytes 5242880 | tf_op jit(solution)/shard_map/pallas_call | solution.py:246
  23.9 0.4 %collective-permute-start.10 = (bf16[2,48,512]{2,1,0:T(8,128)(2,1)S(1)}, bf16[2,48,512]{2,1,0:T(8,128)(2,1)S(1)}, u32[]{:S(2)}, u32[]{:S(2)}) collective-permute-start(bf16[2,48,512]{2,1,0:T(8,128)(2,1)S(1)} %get-tuple-element.44), channel_id=1, source_target_pairs={{0,1},{1,0},{2,3},{3,2},{4,5},{5,4},{6,7},{7,6},{8,9},{9,8},{10,11... | collective-permute-start | bytes 294920 | tf_op jit(solution)/shard_map/ppermute | solution.py:284
  24.3 0.2 collective-permute-start.9
  24.4 0.3 collective-permute-start.12
  24.8 0.2 collective-permute-start.14
  25.0 0.3 collective-permute-done.10
  25.3 1.5 %collective-permute-start.11 = (bf16[2,48,512]{2,1,0:T(8,128)(2,1)S(1)}, bf16[2,48,512]{2,1,0:T(8,128)(2,1)S(1)}, u32[]{:S(2)}, u32[]{:S(2)}) collective-permute-start(bf16[2,48,512]{2,1,0:T(8,128)(2,1)S(1)} %add_convert_fusion.3), channel_id=1, source_target_pairs={{0,4},{1,5},{4,0},{5,1},{2,6},{3,7},{6,2},{7,3},{8,12},{9,13},{12,... | collective-permute-start | bytes 294920 | tf_op jit(solution)/shard_map/ppermute | solution.py:275
  26.8 2.8 %collective-permute-start.13 = (bf16[2,48,512]{2,1,0:T(8,128)(2,1)S(1)}, bf16[2,48,512]{2,1,0:T(8,128)(2,1)S(1)}, u32[]{:S(2)}, u32[]{:S(2)}) collective-permute-start(bf16[2,48,512]{2,1,0:T(8,128)(2,1)S(1)} %add_convert_fusion.2), channel_id=1, source_target_pairs={{0,6},{1,7},{6,0},{7,1},{2,4},{3,5},{4,2},{5,3},{8,14},{9,15},{14,... | collective-permute-start | bytes 294920 | tf_op jit(solution)/shard_map/ppermute | solution.py:275
  29.6 0.1 collective-permute-start.15
  29.6 6.5 %collective-permute-done.11 = bf16[2,48,512]{2,1,0:T(8,128)(2,1)S(1)} collective-permute-done((bf16[2,48,512]{2,1,0:T(8,128)(2,1)S(1)}, bf16[2,48,512]{2,1,0:T(8,128)(2,1)S(1)}, u32[]{:S(2)}, u32[]{:S(2)}) %collective-permute-start.11) | collective-permute-done | bytes 98336 | tf_op jit(solution)/shard_map/ppermute | solution.py:275
  36.1 0.9 %collective-permute-done.15 = bf16[2,48,512]{2,1,0:T(8,128)(2,1)S(1)} collective-permute-done((bf16[2,48,512]{2,1,0:T(8,128)(2,1)S(1)}, bf16[2,48,512]{2,1,0:T(8,128)(2,1)S(1)}, u32[]{:S(2)}, u32[]{:S(2)}) %collective-permute-start.15) | collective-permute-done | bytes 98336 | tf_op jit(solution)/shard_map/ppermute | solution.py:275
  37.1 0.6 %slice_bitcast_fusion = (bf16[48,512]{1,0:T(8,128)(2,1)}, bf16[48,512]{1,0:T(8,128)(2,1)}) fusion(bf16[2,48,512]{2,1,0:T(8,128)(2,1)S(1)} %add_convert_fusion), kind=kLoop, calls=%fused_computation.5 | loop fusion | bytes 196608 | tf_op jit(solution)/shard_map/squeeze | solution.py:302
  (19 shorter events, 0.2 us)
Async XLA Ops:
  0.6 15.2 %collective-permute-start.1 = (bf16[48,512]{1,0:T(8,128)(2,1)}, bf16[48,512]{1,0:T(8,128)(2,1)S(1)}, u32[]{:S(2)}, u32[]{:S(2)}) collective-permute-start(bf16[48,512]{1,0:T(8,128)(2,1)} %param.14), channel_id=1, source_target_pairs={{0,4},{1,5},{4,0},{5,1},{2,6},{3,7},{6,2},{7,3},{8,12},{9,13},{12,... | collective-permute-start | bytes 147464 | tf_op jit(solution)/shard_map/ppermute | solution.py:275
  4.7 11.1 %collective-permute-start.2 = (bf16[48,512]{1,0:T(8,128)(2,1)}, bf16[48,512]{1,0:T(8,128)(2,1)S(1)}, u32[]{:S(2)}, u32[]{:S(2)}) collective-permute-start(bf16[48,512]{1,0:T(8,128)(2,1)} %param.15), channel_id=1, source_target_pairs={{0,4},{1,5},{4,0},{5,1},{2,6},{3,7},{6,2},{7,3},{8,12},{9,13},{12,... | collective-permute-start | bytes 147464 | tf_op jit(solution)/shard_map/ppermute | solution.py:275
  5.7 10.6 %collective-permute-start.4 = (bf16[2,48,512]{2,1,0:T(8,128)(2,1)S(1)}, bf16[2,48,512]{2,1,0:T(8,128)(2,1)S(1)}, u32[]{:S(2)}, u32[]{:S(2)}) collective-permute-start(bf16[2,48,512]{2,1,0:T(8,128)(2,1)S(1)} %broadcast_select_fusion.rest_0_), channel_id=1, source_target_pairs={{0,1},{1,0},{2,3},{3,2},{4,5},{5,4},{6,7},{7,6},{8,9},{9,8},{10,11... | collective-permute-start | bytes 294920 | tf_op jit(solution)/shard_map/ppermute | solution.py:284
  5.8 8.2 %collective-permute-start.3 = (bf16[2,48,512]{2,1,0:T(8,128)(2,1)S(1)}, bf16[2,48,512]{2,1,0:T(8,128)(2,1)S(1)}, u32[]{:S(2)}, u32[]{:S(2)}) collective-permute-start(bf16[2,48,512]{2,1,0:T(8,128)(2,1)S(1)} %broadcast_select_fusion.rest_0_), channel_id=1, source_target_pairs={{0,6},{1,7},{6,0},{7,1},{2,4},{3,5},{4,2},{5,3},{8,14},{9,15},{14,... | collective-permute-start | bytes 294920 | tf_op jit(solution)/shard_map/ppermute | solution.py:275
  9.7 5.5 %collective-permute-start = (bf16[2,48,512]{2,1,0:T(8,128)(2,1)S(1)}, bf16[2,48,512]{2,1,0:T(8,128)(2,1)S(1)}, u32[]{:S(2)}, u32[]{:S(2)}) collective-permute-start(bf16[2,48,512]{2,1,0:T(8,128)(2,1)S(1)} %broadcast_select_fusion.rest_0_), channel_id=1, source_target_pairs={{0,2},{1,3},{2,0},{3,1},{4,6},{5,7},{6,4},{7,5},{8,10},{9,11},{10,... | collective-permute-start | bytes 294920 | tf_op jit(solution)/shard_map/ppermute | solution.py:275
  9.7 0.7 %copy-start = (s32[8]{0:T(128)S(1)}, s32[8]{0:T(128)}, u32[]{:S(2)}) copy-start(s32[8]{0:T(128)} %len_ref.1) | copy-start | bytes 100
  15.3 1.9 %collective-permute-start.5 = (bf16[2,48,512]{2,1,0:T(8,128)(2,1)S(1)}, bf16[2,48,512]{2,1,0:T(8,128)(2,1)S(1)}, u32[]{:S(2)}, u32[]{:S(2)}) collective-permute-start(bf16[2,48,512]{2,1,0:T(8,128)(2,1)S(1)} %collective-permute-done.rest_1_), channel_id=1, source_target_pairs={{0,1},{1,0},{2,3},{3,2},{4,5},{5,4},{6,7},{7,6},{8,9},{9,8},{10,11... | collective-permute-start | bytes 294920 | tf_op jit(solution)/shard_map/ppermute | solution.py:284
  15.3 1.9 %collective-permute-start.8 = (bf16[2,48,512]{2,1,0:T(8,128)(2,1)S(1)}, bf16[2,48,512]{2,1,0:T(8,128)(2,1)S(1)}, u32[]{:S(2)}, u32[]{:S(2)}) collective-permute-start(bf16[2,48,512]{2,1,0:T(8,128)(2,1)S(1)} %collective-permute-done.3.rest_4_), channel_id=1, source_target_pairs={{0,1},{1,0},{2,3},{3,2},{4,5},{5,4},{6,7},{7,6},{8,9},{9,8},{10,11... | collective-permute-start | bytes 294920 | tf_op jit(solution)/shard_map/ppermute | solution.py:284
  15.8 1.2 %collective-permute-start.6 = (bf16[48,512]{1,0:T(8,128)(2,1)S(1)}, bf16[48,512]{1,0:T(8,128)(2,1)S(1)}, u32[]{:S(2)}, u32[]{:S(2)}) collective-permute-start(bf16[48,512]{1,0:T(8,128)(2,1)S(1)} %collective-permute-done.1.rest_2_), channel_id=1, source_target_pairs={{0,1},{1,0},{2,3},{3,2},{4,5},{5,4},{6,7},{7,6},{8,9},{9,8},{10,11... | collective-permute-start | bytes 147464 | tf_op jit(solution)/shard_map/ppermute | solution.py:284
  15.9 1.3 %collective-permute-start.7 = (bf16[48,512]{1,0:T(8,128)(2,1)S(1)}, bf16[48,512]{1,0:T(8,128)(2,1)S(1)}, u32[]{:S(2)}, u32[]{:S(2)}) collective-permute-start(bf16[48,512]{1,0:T(8,128)(2,1)S(1)} %collective-permute-done.2.rest_3_), channel_id=1, source_target_pairs={{0,1},{1,0},{2,3},{3,2},{4,5},{5,4},{6,7},{7,6},{8,9},{9,8},{10,11... | collective-permute-start | bytes 147464 | tf_op jit(solution)/shard_map/ppermute | solution.py:284
  23.9 1.4 %collective-permute-start.10 = (bf16[2,48,512]{2,1,0:T(8,128)(2,1)S(1)}, bf16[2,48,512]{2,1,0:T(8,128)(2,1)S(1)}, u32[]{:S(2)}, u32[]{:S(2)}) collective-permute-start(bf16[2,48,512]{2,1,0:T(8,128)(2,1)S(1)} %get-tuple-element.44), channel_id=1, source_target_pairs={{0,1},{1,0},{2,3},{3,2},{4,5},{5,4},{6,7},{7,6},{8,9},{9,8},{10,11... | collective-permute-start | bytes 294920 | tf_op jit(solution)/shard_map/ppermute | solution.py:284
  24.3 5.4 %collective-permute-start.9 = (bf16[2,48,512]{2,1,0:T(8,128)(2,1)S(1)}, bf16[2,48,512]{2,1,0:T(8,128)(2,1)S(1)}, u32[]{:S(2)}, u32[]{:S(2)}) collective-permute-start(bf16[2,48,512]{2,1,0:T(8,128)(2,1)S(1)} %get-tuple-element.42), channel_id=1, source_target_pairs={{0,1},{1,0},{2,3},{3,2},{4,5},{5,4},{6,7},{7,6},{8,9},{9,8},{10,11... | collective-permute-start | bytes 294920 | tf_op jit(solution)/shard_map/ppermute | solution.py:284
  24.4 2.3 %collective-permute-start.12 = (bf16[2,48,512]{2,1,0:T(8,128)(2,1)S(1)}, bf16[2,48,512]{2,1,0:T(8,128)(2,1)S(1)}, u32[]{:S(2)}, u32[]{:S(2)}) collective-permute-start(bf16[2,48,512]{2,1,0:T(8,128)(2,1)S(1)} %get-tuple-element.46), channel_id=1, source_target_pairs={{0,1},{1,0},{2,3},{3,2},{4,5},{5,4},{6,7},{7,6},{8,9},{9,8},{10,11... | collective-permute-start | bytes 294920 | tf_op jit(solution)/shard_map/ppermute | solution.py:284
  24.8 4.7 %collective-permute-start.14 = (bf16[2,48,512]{2,1,0:T(8,128)(2,1)S(1)}, bf16[2,48,512]{2,1,0:T(8,128)(2,1)S(1)}, u32[]{:S(2)}, u32[]{:S(2)}) collective-permute-start(bf16[2,48,512]{2,1,0:T(8,128)(2,1)S(1)} %get-tuple-element.48), channel_id=1, source_target_pairs={{0,1},{1,0},{2,3},{3,2},{4,5},{5,4},{6,7},{7,6},{8,9},{9,8},{10,11... | collective-permute-start | bytes 294920 | tf_op jit(solution)/shard_map/ppermute | solution.py:284
  25.3 10.8 %collective-permute-start.11 = (bf16[2,48,512]{2,1,0:T(8,128)(2,1)S(1)}, bf16[2,48,512]{2,1,0:T(8,128)(2,1)S(1)}, u32[]{:S(2)}, u32[]{:S(2)}) collective-permute-start(bf16[2,48,512]{2,1,0:T(8,128)(2,1)S(1)} %add_convert_fusion.3), channel_id=1, source_target_pairs={{0,4},{1,5},{4,0},{5,1},{2,6},{3,7},{6,2},{7,3},{8,12},{9,13},{12,... | collective-permute-start | bytes 294920 | tf_op jit(solution)/shard_map/ppermute | solution.py:275
  26.8 9.3 %collective-permute-start.13 = (bf16[2,48,512]{2,1,0:T(8,128)(2,1)S(1)}, bf16[2,48,512]{2,1,0:T(8,128)(2,1)S(1)}, u32[]{:S(2)}, u32[]{:S(2)}) collective-permute-start(bf16[2,48,512]{2,1,0:T(8,128)(2,1)S(1)} %add_convert_fusion.2), channel_id=1, source_target_pairs={{0,6},{1,7},{6,0},{7,1},{2,4},{3,5},{4,2},{5,3},{8,14},{9,15},{14,... | collective-permute-start | bytes 294920 | tf_op jit(solution)/shard_map/ppermute | solution.py:275
  29.6 7.5 %collective-permute-start.15 = (bf16[2,48,512]{2,1,0:T(8,128)(2,1)S(1)}, bf16[2,48,512]{2,1,0:T(8,128)(2,1)S(1)}, u32[]{:S(2)}, u32[]{:S(2)}) collective-permute-start(bf16[2,48,512]{2,1,0:T(8,128)(2,1)S(1)} %add_convert_fusion.1), channel_id=1, source_target_pairs={{0,2},{1,3},{2,0},{3,1},{4,6},{5,7},{6,4},{7,5},{8,10},{9,11},{10,... | collective-permute-start | bytes 294920 | tf_op jit(solution)/shard_map/ppermute | solution.py:275

commit v3 on v2

--- a/solution.py
+++ b/solution.py
@@ -128,13 +128,12 @@
 def attention_kernel(chips, piece_rows, joined, live_ref, q_rows, g_rows, q_cols, g_cols, rk_ref, rv_ref, *rest):
     pieces = CORES * chips
     k_refs, v_refs, rest = read_pieces(joined, rest)
-    whole, rest = rest[:3], rest[3:]
+    (ds_ref, drk_ref, drv_ref), rest = rest[:3], rest[3:]
     d_own, d_other, rest = rest[:chips], rest[chips : 2 * chips], rest[2 * chips :]
-    k_buf, v_buf, s_buf, dp_buf, p_buf, ds_buf, dq_buf, drk_buf, drv_buf, sem = rest
+    k_buf, v_buf, s_buf, dp_buf, p_buf = rest
     rows, width = rk_ref.shape
     groups = width // HEAD_DIM
     block = q_rows.shape[0] // groups // 2
-    per_half = block // rows
     keys = k_buf.shape[1]
     prompt = keys - rows
     diagonal = lax.broadcasted_iota(jnp.int32, (CHUNK, rows), 1) - lax.broadcasted_iota(jnp.int32, (CHUNK, rows), 0)
@@ -169,65 +168,34 @@
         weight = (1.0 / jnp.sum(e, axis=1, keepdims=True)) * live_ref[first : first + CHUNK, :]
         p = e * jnp.concatenate([weight] * (keys // HEAD_DIM), axis=1)
         p_buf[slot, span, :] = p.astype(BF16)
-        ds_buf[slot, span, :] = (p * dp_buf[slot, span, :]).astype(BF16)
-
-    def query_grads(half):
-        dq = (dot(ds_buf[half % 2], k_buf[half // 2]) * SCALE).astype(BF16)
-        for i in range(per_half):
-            dq_buf[:, head_slice(half * per_half + i)] = dq[i * rows : (i + 1) * rows]
-
-    sums = {}
-
-    def key_grads(half):
-        sums["k", half] = dot(q_cols[:, place(half)], ds_buf[half % 2])
-
-    def value_grads(half):
-        sums["v", half] = dot(g_cols[:, place(half)], p_buf[half % 2])
-
-    def finish(group):
-        cols = head_slice(group)
-        dk = ((sums["k", 2 * group] + sums["k", 2 * group + 1]) * SCALE).T
-        dv = (sums["v", 2 * group] + sums["v", 2 * group + 1]).T
+        ds_ref[half * block + low : half * block + low + CHUNK, :] = (p * dp_buf[slot, span, :]).astype(BF16)
+
+    halves = 2 * groups
+    held = None
+    for half in range(-1, halves):
+        if half + 1 < halves:
+            if (half + 1) % 2 == 0:
+                load_keys((half + 1) // 2)
+            scores(half + 1)
+            prob_grads(half + 1)
+        if half < 0:
+            continue
+        for low in range(0, block, CHUNK):
+            soften(half, low)
+        dk = dot(q_cols[:, place(half)], ds_ref[place(half), :])
+        dv = dot(g_cols[:, place(half)], p_buf[half % 2])
+        if half % 2 == 0:
+            held = (dk, dv)
+            continue
+        cols = head_slice(half // 2)
+        dk = ((held[0] + dk) * SCALE).T
+        dv = (held[1] + dv).T
         for kind, grad in enumerate((dk, dv)):
             for i in range(chips):
                 d_own[i][kind, :, cols] = grad[i * piece_rows : (i + 1) * piece_rows]
                 d_other[i][kind, :, cols] = grad[(chips + i) * piece_rows : (chips + i + 1) * piece_rows].astype(BF16)
-        drk_buf[:, cols] = dk[prompt:].astype(BF16)
-        drv_buf[:, cols] = dv[prompt:].astype(BF16)
-        copies = []
-        for i, (buf, out) in enumerate(zip((dq_buf, drk_buf, drv_buf), whole)):
-            step = buf.shape[1] // groups
-            part = slice(group * step, (group + 1) * step)
-            copies.append(pltpu.make_async_copy(buf.at[:, part], out.at[:, part], sem.at[group, i]))
-            copies[-1].start()
-        return copies
-
-    halves = 2 * groups
-    chunks = range(0, block, CHUNK)
-    load_keys(0)
-    scores(0)
-    prob_grads(0)
-    stores = []
-    for half in range(halves + 1):
-        tasks = []
-        if half + 1 < halves:
-            if (half + 1) % 2 == 0:
-                load_keys((half + 1) // 2)
-            tasks += [functools.partial(task, half + 1) for task in (scores, prob_grads)]
-        if half:
-            tasks += [functools.partial(task, half - 1) for task in (key_grads, value_grads, query_grads)]
-        done = 0
-        for i, low in enumerate(chunks if half < halves else ()):
-            while done < len(tasks) and done * len(chunks) <= i * len(tasks):
-                tasks[done]()
-                done += 1
-            soften(half, low)
-        for task in tasks[done:]:
-            task()
-        if half and half % 2 == 0:
-            stores += finish(half // 2 - 1)
-    for copy in stores:
-        copy.wait()
+        drk_ref[:, cols] = dk[prompt:].astype(BF16)
+        drv_ref[:, cols] = dv[prompt:].astype(BF16)
 
 
 def attention(prepared, kv_pieces):
@@ -235,7 +203,6 @@
     rows, kv_width = rk.shape
     groups = kv_width // HEAD_DIM
     flat = q_rows.shape[0]
-    wide = (rows, flat // rows * HEAD_DIM)
     pieces = len(kv_pieces)
     chips = pieces // CORES
     piece_rows = kv_pieces[0][0].shape[-2]
@@ -246,8 +213,8 @@
     return pl.pallas_call(
         functools.partial(attention_kernel, chips, piece_rows, joined),
         in_specs=[VMEM_SPEC] * (7 + len(flat_pieces)),
-        out_specs=[HBM_SPEC] * 3 + [VMEM_SPEC] * (2 * chips),
-        out_shape=[shape(*wide), shape(rows, kv_width), shape(rows, kv_width)]
+        out_specs=[VMEM_SPEC] * (3 + 2 * chips),
+        out_shape=[shape(flat, keys), shape(rows, kv_width), shape(rows, kv_width)]
         + [jax.ShapeDtypeStruct((2, piece_rows, kv_width), F32)] * chips
         + [shape(2, piece_rows, kv_width)] * chips,
         scratch_shapes=[
@@ -256,17 +223,62 @@
             pltpu.VMEM((2, block, keys), F32),
             pltpu.VMEM((2, block, keys), F32),
             pltpu.VMEM((2, block, keys), BF16),
-            pltpu.VMEM((2, block, keys), BF16),
-            pltpu.VMEM(wide, BF16),
-            pltpu.VMEM((rows, kv_width), BF16),
-            pltpu.VMEM((rows, kv_width), BF16),
-            pltpu.SemaphoreType.DMA((groups, 3)),
         ],
         compiler_params=PARAMS,
         cost_estimate=pl.CostEstimate(
             flops=10 * flat * keys * HEAD_DIM, bytes_accessed=10 * flat * HEAD_DIM, transcendentals=flat * keys
         ),
     )(live, q_rows, g_rows, q_cols, g_cols, rk, rv, *flat_pieces)
+
+
+def query_grad_kernel(joined, ds_ref, rk_ref, drk_in, drv_in, *rest):
+    k_refs, _, rest = read_pieces(joined, rest)
+    (dq_out, drk_out, drv_out), (k_buf, dq_buf, wide_sem, narrow_sem) = rest[:3], rest[3:]
+    rows, width = rk_ref.shape
+    groups = width // HEAD_DIM
+    flat = ds_ref.shape[0] // groups
+    step = dq_buf.shape[1] // groups
+    copies = [
+        pltpu.make_async_copy(src, out, narrow_sem.at[i]) for i, (src, out) in enumerate(((drk_in, drk_out), (drv_in, drv_out)))
+    ]
+    for copy in copies:
+        copy.start()
+    for group in range(groups):
+        low = 0
+        for ref in k_refs + [rk_ref]:
+            k_buf[group, low : low + ref.shape[0], :] = ref[:, head_slice(group)]
+            low += ref.shape[0]
+        dq = (dot(ds_ref[group * flat : (group + 1) * flat, :], k_buf[group]) * SCALE).astype(BF16)
+        for i in range(flat // rows):
+            dq_buf[:, head_slice(group * (flat // rows) + i)] = dq[i * rows : (i + 1) * rows]
+        part = slice(group * step, (group + 1) * step)
+        copies.append(pltpu.make_async_copy(dq_buf.at[:, part], dq_out.at[:, part], wide_sem.at[group]))
+        copies[-1].start()
+    for copy in copies:
+        copy.wait()
+
+
+def query_grads(ds, rk, drk, drv, kv_pieces):
+    rows, kv_width = rk.shape
+    flat, keys = ds.shape
+    groups = kv_width // HEAD_DIM
+    wide = (rows, flat // rows * HEAD_DIM)
+    joined = [len(piece) == 1 for piece in kv_pieces]
+    flat_pieces = sum(kv_pieces, [])
+    return pl.pallas_call(
+        functools.partial(query_grad_kernel, joined),
+        in_specs=[VMEM_SPEC] * (4 + len(flat_pieces)),
+        out_specs=[HBM_SPEC] * 3,
+        out_shape=[shape(*wide), shape(rows, kv_width), shape(rows, kv_width)],
+        scratch_shapes=[
+            pltpu.VMEM((groups, keys, HEAD_DIM), BF16),
+            pltpu.VMEM(wide, BF16),
+            pltpu.SemaphoreType.DMA((groups,)),
+            pltpu.SemaphoreType.DMA((2,)),
+        ],
+        compiler_params=PARAMS,
+        cost_estimate=pl.CostEstimate(flops=4 * flat * keys * HEAD_DIM, bytes_accessed=4 * flat * keys, transcendentals=0),
+    )(ds, rk, drk, drv, *flat_pieces)
 
 
 def exchange(x, links):
@@ -292,12 +304,20 @@
     far = [[exchange(x, chip_links(chips, step)) for x in (raw if step == 2 else kv)] for step in steps]
     prepared = prepare(lengths, queries[0], outputs[0], out_grads[0], resp_keys[0], resp_values[0])
     live = prepared[4]
-    far = [[lax.optimization_barrier((x, live))[0] for x in piece] for piece in far]
+    far[1] = [lax.optimization_barrier((x, live))[0] for x in far[1]]
+    first = [swap_core(x, chips) for x in far[1]]
+    far = [piece if i == 1 else [lax.optimization_barrier((x, first))[0] for x in piece] for i, piece in enumerate(far)]
     own = [kv] + far
-    other = [[swap_core(x, chips) for x in piece] for piece in own]
-    dq, drk, drv, *grads = attention(prepared, own + other)
-    both = [grads[i] + swap_core(grads[chips + i], chips).astype(F32) for i in range(chips)]
-    back = [exchange(both[step].astype(BF16), chip_links(chips, step)) for step in steps[1:] + steps[:1]]
+    other = [first if i == 2 else [swap_core(x, chips) for x in piece] for i, piece in enumerate(own)]
+    ds, drk, drv, *grads = attention(prepared, own + other)
+    both = [None] * chips
+    for step in [0] + steps[1:] + steps[:1]:
+        both[step] = grads[step] + swap_core(grads[chips + step], chips).astype(F32)
+    sent = [x.astype(BF16) for x in both]
+    back = [exchange(sent[step], chip_links(chips, step)) for step in steps[1:] + steps[:1]]
+    ds = lax.optimization_barrier((ds, [sent[step] for step in steps[1:] + steps[:1]]))[0]
+    dq, drk, drv = query_grads(ds, prepared[5], drk, drv, own + other)
+    dq, back[0] = lax.optimization_barrier((dq, back[0]))
     total = sum([x.astype(F32) for x in back], both[0]).astype(BF16)
     return dq[None], drk[None], drv[None], total[0], total[1]
 

time: 37.9 us -> 36.3 us (0.958)
  waiting for transfers between devices: 9.86 us -> 6.91 us
  Pallas kernels: 10.2 us -> 11.3 us
    ppermute x7, waiting for transfers between devices: 8.69 us -> 4.68 us  [exchange(): return lax.ppermute(x, 'seq', pairs)]
    pallas_call x0 -> x1, Pallas kernels: none -> 2.25 us  [query_grads(): pl.pallas_call(functools.partial(query_grad_kernel, joined), in_specs=[VM...]
    pallas_call x1, Pallas kernels: 6.67 us -> 5.45 us  [attention(): pl.pallas_call(functools.partial(attention_kernel, chips, piece_rows, joi...]
    ppermute x9, waiting for transfers between devices: 1.17 us -> 2.23 us  [swap_core(): return lax.ppermute(x, 'seq', pairs)]
  transfers between devices with their start and end apart: 16 -> 16, of which waited for: 6 -> 7; matrix products, arithmetic and copies ran while one was open for 3% -> 3% of each run, Pallas kernels for 9% -> 16%
where the time goes in v3:
time: 36.3 us; the launch traced here: 36.2 us
  starting transfers between devices  14.9 us (41%)
  Pallas kernels  11.3 us (31%)
  waiting for transfers between devices  6.91 us (19%)
  local copies, waits for them, and re-layouts  1.3 us (4%)
  other arithmetic  1.03 us (3%)
  between operations  0.72 us (2%)
    ppermute x7, starting transfers between devices, exchange(): return lax.ppermute(x, 'seq', pairs)  12.7 us
    pallas_call x1, Pallas kernels, attention(): pl.pallas_call(functools.partial(attention_kernel, chips, piece_rows, joi...  5.45 us
    ppermute x7, waiting for transfers between devices, exchange(): return lax.ppermute(x, 'seq', pairs)  4.68 us
    pallas_call x1, Pallas kernels, prepare(): pl.pallas_call(functools.partial(prepare_kernel, groups), in_specs=[SMEM_...  3.57 us
    pallas_call x1, Pallas kernels, query_grads(): pl.pallas_call(functools.partial(query_grad_kernel, joined), in_specs=[VM...  2.25 us
    ppermute x9, starting transfers between devices, swap_core(): return lax.ppermute(x, 'seq', pairs)  2.24 us
    ppermute x9, waiting for transfers between devices, swap_core(): return lax.ppermute(x, 'seq', pairs)  2.23 us
    select_n x1, other arithmetic, local(): kv = [jnp.where(kind == 0, prompt_keys[None], prompt_values[None])]  0.91 us
  transfers between devices with their start and end apart: 16, of which 7 were waited for; matrix products, arithmetic and copies ran while one was open for 3% of the time, Pallas kernels for 16%

profile of v3, /device:TPU:0, one launch (start us, length us, event | category | flops | bytes accessed | tf_op | source)
XLA Modules:
  0.0 36.2 jit_solution(8095076665232180351)
XLA Ops:
  0.6 4.1 %collective-permute-start.1 = (bf16[48,512]{1,0:T(8,128)(2,1)}, bf16[48,512]{1,0:T(8,128)(2,1)S(1)}, u32[]{:S(2)}, u32[]{:S(2)}) collective-permute-start(bf16[48,512]{1,0:T(8,128)(2,1)} %param.14), channel_id=1, source_target_pairs={{0,4},{1,5},{4,0},{5,1},{2,6},{3,7},{6,2},{7,3},{8,12},{9,13},{12,... | collective-permute-start | bytes 147464 | tf_op jit(solution)/shard_map/ppermute | solution.py:287
  4.8 0.9 %broadcast_select_fusion.rest_0_ = bf16[2,48,512]{2,1,0:T(8,128)(2,1)S(1)} fusion(pred[2]{0:T(512)(128)(4,1)S(1)} %iota_compare_fusion, bf16[48,512]{1,0:T(8,128)(2,1)} %param.15, bf16[48,512]{1,0:T(8,128)(2,1)} %param.14), kind=kLoop, calls=%fused_computation.4 | loop fusion | flops 49152 | bytes 196610 | tf_op jit(solution)/shard_map/jit(_where)/select_n | solution.py:303
  5.7 3.9 %collective-permute-start.5 = (bf16[2,48,512]{2,1,0:T(8,128)(2,1)S(1)}, bf16[2,48,512]{2,1,0:T(8,128)(2,1)S(1)}, u32[]{:S(2)}, u32[]{:S(2)}) collective-permute-start(bf16[2,48,512]{2,1,0:T(8,128)(2,1)S(1)} %broadcast_select_fusion.rest_0_), channel_id=1, source_target_pairs={{0,6},{1,7},{6,0},{7,1},{2,4},{3,5},{4,2},{5,3},{8,14},{9,15},{14,... | collective-permute-start | bytes 294920 | tf_op jit(solution)/shard_map/ppermute | solution.py:287
  9.7 0.7 %copy-done = s32[8]{0:T(128)S(1)} copy-done((s32[8]{0:T(128)S(1)}, s32[8]{0:T(128)}, u32[]{:S(2)}) %copy-start) | copy-done | bytes 56
  10.3 3.6 %shard_map.119 = (bf16[4096,128]{1,0:T(8,128)(2,1)S(1)}, bf16[4096,256]{1,0:T(8,128)(2,1)S(1)}, bf16[128,4096]{1,0:T(8,128)(2,1)S(1)}, bf16[128,4096]{1,0:T(8,12...) custom-call(s32[8]{0:T(128)S(1)} %copy-done, ...), custom_call_target="tpu_custom_call" | custom-call | flops 2097152000 | bytes 8388608 | tf_op jit(solution)/shard_map/pallas_call | solution.py:100
  14.0 0.5 %collective-permute-start.4 = (bf16[48,512]{1,0:T(8,128)(2,1)S(1)}, bf16[48,512]{1,0:T(8,128)(2,1)S(1)}, u32[]{:S(2)}, u32[]{:S(2)}) collective-permute-start(bf16[48,512]{1,0:T(8,128)(2,1)S(1)} %collective-permute-done.3.rest_3_), channel_id=1, source_target_pairs={{0,1},{1,0},{2,3},{3,2},{4,5},{5,4},{6,7},{7,6},{8,9},{9,8},{10,11... | collective-permute-start | bytes 147464 | tf_op jit(solution)/shard_map/ppermute | solution.py:296
  14.6 0.6 %collective-permute-done.2.rest_7_ = bf16[48,512]{1,0:T(8,128)(2,1)S(1)} collective-permute-done((bf16[48,512]{1,0:T(8,128)(2,1)S(1)}, bf16[48,512]{1,0:T(8,128)(2,1)S(1)}, u32[]{:S(2)}, u32[]{:S(2)}) %collective-permute-start.2) | collective-permute-done | bytes 49184 | tf_op jit(solution)/shard_map/ppermute | solution.py:296
  15.2 0.2 collective-permute-done.4.rest_8_
  15.4 0.4 collective-permute-start.7
  15.7 0.2 collective-permute-start.8
  15.9 0.8 %collective-permute-done.7.rest_6_ = bf16[2,48,512]{2,1,0:T(8,128)(2,1)S(1)} collective-permute-done((bf16[2,48,512]{2,1,0:T(8,128)(2,1)S(1)}, bf16[2,48,512]{2,1,0:T(8,128)(2,1)S(1)}, u32[]{:S(2)}, u32[]{:S(2)}) %collective-permute-start.7) | collective-permute-done | bytes 98336 | tf_op jit(solution)/shard_map/ppermute | solution.py:296
  16.7 0.3 collective-permute-done.8.rest_9_
  17.0 5.4 %shard_map.120 = (bf16[4096,512]{1,0:T(8,128)(2,1)S(1)}, bf16[128,512]{1,0:T(8,128)(2,1)S(1)}, bf16[128,512]{1,0:T(8,128)(2,1)S(1)}, f32[2,48,512]{2,1,0:T(8,128...) custom-call(f32[128,128]{1,0:T(8,128)S(1)} %get-tuple-element.33.liv, ...), custom_call_target="tpu_custom_call" | custom-call | flops 2684354560 | bytes 5242880 | tf_op jit(solution)/shard_map/pallas_call | solution.py:213
  22.5 0.2 collective-permute-start.9
  22.7 0.3 collective-permute-start.10
  23.0 0.2 collective-permute-start.11
  23.2 0.3 collective-permute-start.13
  23.6 0.3 collective-permute-done.9
  23.9 1.3 %collective-permute-start.12 = (bf16[2,48,512]{2,1,0:T(8,128)(2,1)S(1)}, bf16[2,48,512]{2,1,0:T(8,128)(2,1)S(1)}, u32[]{:S(2)}, u32[]{:S(2)}) collective-permute-start(bf16[2,48,512]{2,1,0:T(8,128)(2,1)S(1)} %add_convert_fusion.3), channel_id=1, source_target_pairs={{0,4},{1,5},{4,0},{5,1},{2,6},{3,7},{6,2},{7,3},{8,12},{9,13},{12,... | collective-permute-start | bytes 294920 | tf_op jit(solution)/shard_map/ppermute | solution.py:287
  25.2 3.2 %collective-permute-start.14 = (bf16[2,48,512]{2,1,0:T(8,128)(2,1)S(1)}, bf16[2,48,512]{2,1,0:T(8,128)(2,1)S(1)}, u32[]{:S(2)}, u32[]{:S(2)}) collective-permute-start(bf16[2,48,512]{2,1,0:T(8,128)(2,1)S(1)} %add_convert_fusion.2), channel_id=1, source_target_pairs={{0,6},{1,7},{6,0},{7,1},{2,4},{3,5},{4,2},{5,3},{8,14},{9,15},{14,... | collective-permute-start | bytes 294920 | tf_op jit(solution)/shard_map/ppermute | solution.py:287
  28.5 2.2 %shard_map.121 = (bf16[128,4096]{1,0:T(8,128)(2,1)}, bf16[128,512]{1,0:T(8,128)(2,1)}, bf16[128,512]{1,0:T(8,128)(2,1)}) custom-call(bf16[4096,512]{1,0:T(8,128)(2,1)S(1)} %get-tuple-element.51.ds_ref, bf16[128,512]{1,0:T(8,128)(2,1)S(1)} %get-tuple-element.38.rk_ref, bf16[128,512]{1,0:T(8,128)(2,1)S(1)} %get-tuple-element.52.drk_in, ...), custom_call_target="tpu_custom_call" | custom-call | flops 1073741824 | bytes 8388608 | tf_op jit(solution)/shard_map/pallas_call | solution.py:268
  30.8 3.9 %collective-permute-done.12 = bf16[2,48,512]{2,1,0:T(8,128)(2,1)S(1)} collective-permute-done((bf16[2,48,512]{2,1,0:T(8,128)(2,1)S(1)}, bf16[2,48,512]{2,1,0:T(8,128)(2,1)S(1)}, u32[]{:S(2)}, u32[]{:S(2)}) %collective-permute-start.12) | collective-permute-done | bytes 98336 | tf_op jit(solution)/shard_map/ppermute | solution.py:287
  34.7 0.8 %collective-permute-done.15 = bf16[2,48,512]{2,1,0:T(8,128)(2,1)S(1)} collective-permute-done((bf16[2,48,512]{2,1,0:T(8,128)(2,1)S(1)}, bf16[2,48,512]{2,1,0:T(8,128)(2,1)S(1)}, u32[]{:S(2)}, u32[]{:S(2)}) %collective-permute-start.15) | collective-permute-done | bytes 98336 | tf_op jit(solution)/shard_map/ppermute | solution.py:287
  35.5 0.6 %slice_bitcast_fusion = (bf16[48,512]{1,0:T(8,128)(2,1)}, bf16[48,512]{1,0:T(8,128)(2,1)}) fusion(bf16[2,48,512]{2,1,0:T(8,128)(2,1)S(1)} %add_convert_fusion), kind=kLoop, calls=%fused_computation.5 | loop fusion | bytes 196608 | tf_op jit(solution)/shard_map/squeeze | solution.py:322
  (20 shorter events, 0.5 us)
Async XLA Ops:
  0.6 13.3 %collective-permute-start.1 = (bf16[48,512]{1,0:T(8,128)(2,1)}, bf16[48,512]{1,0:T(8,128)(2,1)S(1)}, u32[]{:S(2)}, u32[]{:S(2)}) collective-permute-start(bf16[48,512]{1,0:T(8,128)(2,1)} %param.14), channel_id=1, source_target_pairs={{0,4},{1,5},{4,0},{5,1},{2,6},{3,7},{6,2},{7,3},{8,12},{9,13},{12,... | collective-permute-start | bytes 147464 | tf_op jit(solution)/shard_map/ppermute | solution.py:287
  4.7 9.2 %collective-permute-start.3 = (bf16[48,512]{1,0:T(8,128)(2,1)}, bf16[48,512]{1,0:T(8,128)(2,1)S(1)}, u32[]{:S(2)}, u32[]{:S(2)}) collective-permute-start(bf16[48,512]{1,0:T(8,128)(2,1)} %param.15), channel_id=1, source_target_pairs={{0,4},{1,5},{4,0},{5,1},{2,6},{3,7},{6,2},{7,3},{8,12},{9,13},{12,... | collective-permute-start | bytes 147464 | tf_op jit(solution)/shard_map/ppermute | solution.py:287
  5.7 8.8 %collective-permute-start.5 = (bf16[2,48,512]{2,1,0:T(8,128)(2,1)S(1)}, bf16[2,48,512]{2,1,0:T(8,128)(2,1)S(1)}, u32[]{:S(2)}, u32[]{:S(2)}) collective-permute-start(bf16[2,48,512]{2,1,0:T(8,128)(2,1)S(1)} %broadcast_select_fusion.rest_0_), channel_id=1, source_target_pairs={{0,6},{1,7},{6,0},{7,1},{2,4},{3,5},{4,2},{5,3},{8,14},{9,15},{14,... | collective-permute-start | bytes 294920 | tf_op jit(solution)/shard_map/ppermute | solution.py:287
  9.7 5.7 %collective-permute-start = (bf16[2,48,512]{2,1,0:T(8,128)(2,1)S(1)}, bf16[2,48,512]{2,1,0:T(8,128)(2,1)S(1)}, u32[]{:S(2)}, u32[]{:S(2)}) collective-permute-start(bf16[2,48,512]{2,1,0:T(8,128)(2,1)S(1)} %broadcast_select_fusion.rest_0_), channel_id=1, source_target_pairs={{0,2},{1,3},{2,0},{3,1},{4,6},{5,7},{6,4},{7,5},{8,10},{9,11},{10,... | collective-permute-start | bytes 294920 | tf_op jit(solution)/shard_map/ppermute | solution.py:287
  9.7 0.7 %copy-start = (s32[8]{0:T(128)S(1)}, s32[8]{0:T(128)}, u32[]{:S(2)}) copy-start(s32[8]{0:T(128)} %len_ref.1) | copy-start | bytes 100
  13.9 1.3 %collective-permute-start.2 = (bf16[48,512]{1,0:T(8,128)(2,1)S(1)}, bf16[48,512]{1,0:T(8,128)(2,1)S(1)}, u32[]{:S(2)}, u32[]{:S(2)}) collective-permute-start(bf16[48,512]{1,0:T(8,128)(2,1)S(1)} %collective-permute-done.1.rest_2_), channel_id=1, source_target_pairs={{0,1},{1,0},{2,3},{3,2},{4,5},{5,4},{6,7},{7,6},{8,9},{9,8},{10,11... | collective-permute-start | bytes 147464 | tf_op jit(solution)/shard_map/ppermute | solution.py:296
  14.0 1.4 %collective-permute-start.4 = (bf16[48,512]{1,0:T(8,128)(2,1)S(1)}, bf16[48,512]{1,0:T(8,128)(2,1)S(1)}, u32[]{:S(2)}, u32[]{:S(2)}) collective-permute-start(bf16[48,512]{1,0:T(8,128)(2,1)S(1)} %collective-permute-done.3.rest_3_), channel_id=1, source_target_pairs={{0,1},{1,0},{2,3},{3,2},{4,5},{5,4},{6,7},{7,6},{8,9},{9,8},{10,11... | collective-permute-start | bytes 147464 | tf_op jit(solution)/shard_map/ppermute | solution.py:296
  14.5 1.4 %collective-permute-start.6 = (bf16[2,48,512]{2,1,0:T(8,128)(2,1)S(1)}, bf16[2,48,512]{2,1,0:T(8,128)(2,1)S(1)}, u32[]{:S(2)}, u32[]{:S(2)}) collective-permute-start(bf16[2,48,512]{2,1,0:T(8,128)(2,1)S(1)} %broadcast_select_fusion.rest_0_), channel_id=1, source_target_pairs={{0,1},{1,0},{2,3},{3,2},{4,5},{5,4},{6,7},{7,6},{8,9},{9,8},{10,11... | collective-permute-start | bytes 294920 | tf_op jit(solution)/shard_map/ppermute | solution.py:296
  15.4 1.3 %collective-permute-start.7 = (bf16[2,48,512]{2,1,0:T(8,128)(2,1)S(1)}, bf16[2,48,512]{2,1,0:T(8,128)(2,1)S(1)}, u32[]{:S(2)}, u32[]{:S(2)}) collective-permute-start(bf16[2,48,512]{2,1,0:T(8,128)(2,1)S(1)} %collective-permute-done.rest_1_), channel_id=1, source_target_pairs={{0,1},{1,0},{2,3},{3,2},{4,5},{5,4},{6,7},{7,6},{8,9},{9,8},{10,11... | collective-permute-start | bytes 294920 | tf_op jit(solution)/shard_map/ppermute | solution.py:296
  15.7 1.3 %collective-permute-start.8 = (bf16[2,48,512]{2,1,0:T(8,128)(2,1)S(1)}, bf16[2,48,512]{2,1,0:T(8,128)(2,1)S(1)}, u32[]{:S(2)}, u32[]{:S(2)}) collective-permute-start(bf16[2,48,512]{2,1,0:T(8,128)(2,1)S(1)} %collective-permute-done.5.rest_4_), channel_id=1, source_target_pairs={{0,1},{1,0},{2,3},{3,2},{4,5},{5,4},{6,7},{7,6},{8,9},{9,8},{10,11... | collective-permute-start | bytes 294920 | tf_op jit(solution)/shard_map/ppermute | solution.py:296
  22.5 1.4 %collective-permute-start.9 = (bf16[2,48,512]{2,1,0:T(8,128)(2,1)S(1)}, bf16[2,48,512]{2,1,0:T(8,128)(2,1)S(1)}, u32[]{:S(2)}, u32[]{:S(2)}) collective-permute-start(bf16[2,48,512]{2,1,0:T(8,128)(2,1)S(1)} %get-tuple-element.46), channel_id=1, source_target_pairs={{0,1},{1,0},{2,3},{3,2},{4,5},{5,4},{6,7},{7,6},{8,9},{9,8},{10,11... | collective-permute-start | bytes 294920 | tf_op jit(solution)/shard_map/ppermute | solution.py:296
  22.7 2.5 %collective-permute-start.10 = (bf16[2,48,512]{2,1,0:T(8,128)(2,1)S(1)}, bf16[2,48,512]{2,1,0:T(8,128)(2,1)S(1)}, u32[]{:S(2)}, u32[]{:S(2)}) collective-permute-start(bf16[2,48,512]{2,1,0:T(8,128)(2,1)S(1)} %get-tuple-element.48), channel_id=1, source_target_pairs={{0,1},{1,0},{2,3},{3,2},{4,5},{5,4},{6,7},{7,6},{8,9},{9,8},{10,11... | collective-permute-start | bytes 294920 | tf_op jit(solution)/shard_map/ppermute | solution.py:296
  23.0 5.4 %collective-permute-start.11 = (bf16[2,48,512]{2,1,0:T(8,128)(2,1)S(1)}, bf16[2,48,512]{2,1,0:T(8,128)(2,1)S(1)}, u32[]{:S(2)}, u32[]{:S(2)}) collective-permute-start(bf16[2,48,512]{2,1,0:T(8,128)(2,1)S(1)} %get-tuple-element.50), channel_id=1, source_target_pairs={{0,1},{1,0},{2,3},{3,2},{4,5},{5,4},{6,7},{7,6},{8,9},{9,8},{10,11... | collective-permute-start | bytes 294920 | tf_op jit(solution)/shard_map/ppermute | solution.py:296
  23.2 11.5 %collective-permute-start.13 = (bf16[2,48,512]{2,1,0:T(8,128)(2,1)S(1)}, bf16[2,48,512]{2,1,0:T(8,128)(2,1)S(1)}, u32[]{:S(2)}, u32[]{:S(2)}) collective-permute-start(bf16[2,48,512]{2,1,0:T(8,128)(2,1)S(1)} %get-tuple-element.59), channel_id=1, source_target_pairs={{0,1},{1,0},{2,3},{3,2},{4,5},{5,4},{6,7},{7,6},{8,9},{9,8},{10,11... | collective-permute-start | bytes 294920 | tf_op jit(solution)/shard_map/ppermute | solution.py:296
  23.9 10.8 %collective-permute-start.12 = (bf16[2,48,512]{2,1,0:T(8,128)(2,1)S(1)}, bf16[2,48,512]{2,1,0:T(8,128)(2,1)S(1)}, u32[]{:S(2)}, u32[]{:S(2)}) collective-permute-start(bf16[2,48,512]{2,1,0:T(8,128)(2,1)S(1)} %add_convert_fusion.3), channel_id=1, source_target_pairs={{0,4},{1,5},{4,0},{5,1},{2,6},{3,7},{6,2},{7,3},{8,12},{9,13},{12,... | collective-permute-start | bytes 294920 | tf_op jit(solution)/shard_map/ppermute | solution.py:287
  25.2 9.5 %collective-permute-start.14 = (bf16[2,48,512]{2,1,0:T(8,128)(2,1)S(1)}, bf16[2,48,512]{2,1,0:T(8,128)(2,1)S(1)}, u32[]{:S(2)}, u32[]{:S(2)}) collective-permute-start(bf16[2,48,512]{2,1,0:T(8,128)(2,1)S(1)} %add_convert_fusion.2), channel_id=1, source_target_pairs={{0,6},{1,7},{6,0},{7,1},{2,4},{3,5},{4,2},{5,3},{8,14},{9,15},{14,... | collective-permute-start | bytes 294920 | tf_op jit(solution)/shard_map/ppermute | solution.py:287
  28.4 7.0 %collective-permute-start.15 = (bf16[2,48,512]{2,1,0:T(8,128)(2,1)S(1)}, bf16[2,48,512]{2,1,0:T(8,128)(2,1)S(1)}, u32[]{:S(2)}, u32[]{:S(2)}) collective-permute-start(bf16[2,48,512]{2,1,0:T(8,128)(2,1)S(1)} %add_convert_fusion.1), channel_id=1, source_target_pairs={{0,2},{1,3},{2,0},{3,1},{4,6},{5,7},{6,4},{7,5},{8,10},{9,11},{10,... | collective-permute-start | bytes 294920 | tf_op jit(solution)/shard_map/ppermute | solution.py:287

commit v4 on v3

--- a/solution.py
+++ b/solution.py
@@ -41,10 +41,11 @@
     return [pltpu.with_memory_space_constraint(x, pltpu.HBM) for x in arrays]
 
 
-def prepare_kernel(groups, len_ref, *refs):
+def prepare_kernel(groups, *refs):
+    len_in, refs = refs[0], refs[1:]
     wide_in, narrow_in, refs = refs[:3], refs[3:5], refs[5:]
     (q_rows, g_rows, q_cols, g_cols, live_ref), narrow_out, refs = refs[:5], refs[5:7], refs[7:]
-    wide_buf, (wide_sem, narrow_sem) = refs[:3], refs[3:]
+    wide_buf, (len_ref, wide_sem, narrow_sem) = refs[:3], refs[3:]
     rows = wide_buf[0].shape[0]
     width = wide_buf[0].shape[1] // groups
     wide = [
@@ -55,10 +56,9 @@
         for group in range(groups)
     ]
     narrow = [pltpu.make_async_copy(src, out, narrow_sem.at[i]) for i, (src, out) in enumerate(zip(narrow_in, narrow_out))]
-    for copy in sum(wide, []) + narrow:
+    narrow.append(pltpu.make_async_copy(len_in, len_ref, narrow_sem.at[len(narrow)]))
+    for copy in narrow[-1:] + sum(wide, []) + narrow[:-1]:
         copy.start()
-    length = len_ref[lax.axis_index("seq")]
-    live_ref[...] = jnp.where(lax.broadcasted_iota(jnp.int32, live_ref.shape, 0) < length, 1.0, 0.0)
     lane = lax.broadcasted_iota(jnp.int32, (rows, HEAD_DIM), 1)
     square = (HEAD_DIM, HEAD_DIM)
     same = lax.broadcasted_iota(jnp.int32, square, 0) == lax.broadcasted_iota(jnp.int32, square, 1)
@@ -90,6 +90,8 @@
         g_cols[:, span] = dot(identity, g_rows[span, :HEAD_DIM], NT).astype(BF16)
     for copy in narrow:
         copy.wait()
+    length = len_ref[lax.axis_index("seq")]
+    live_ref[...] = jnp.where(lax.broadcasted_iota(jnp.int32, live_ref.shape, 0) < length, 1.0, 0.0)
 
 
 def prepare(lengths, q, o, g, rk, rv):
@@ -99,7 +101,7 @@
     narrow = [rk, rv]
     return pl.pallas_call(
         functools.partial(prepare_kernel, groups),
-        in_specs=[SMEM_SPEC] + [HBM_SPEC] * 5,
+        in_specs=[HBM_SPEC] * 6,
         out_specs=[VMEM_SPEC] * 7,
         out_shape=[
             shape(flat, HEAD_DIM),
@@ -110,10 +112,10 @@
         ]
         + [shape(*x.shape) for x in narrow],
         scratch_shapes=[pltpu.VMEM((rows, width), BF16)] * 3
-        + [pltpu.SemaphoreType.DMA((groups, 3)), pltpu.SemaphoreType.DMA((2,))],
+        + [pltpu.SMEM(lengths.shape, jnp.int32), pltpu.SemaphoreType.DMA((groups, 3)), pltpu.SemaphoreType.DMA((3,))],
         compiler_params=PARAMS,
         cost_estimate=pl.CostEstimate(flops=rows * width * 4000, bytes_accessed=16 * rows * width, transcendentals=0),
-    )(lengths, *in_hbm(q, o, g, *narrow))
+    )(*in_hbm(lengths, q, o, g, *narrow))
 
 
 def read_pieces(joined, refs):

time: 36.3 us -> 35.7 us (0.983)
  waiting for transfers between devices: 6.91 us -> 8.22 us
  Pallas kernels: 11.3 us -> 10.6 us
  local copies, waits for them, and re-layouts: 1.3 us -> 0.64 us
  starting transfers between devices: 14.9 us -> 14.3 us
    ppermute x7, waiting for transfers between devices: 4.68 us -> 6.11 us  [exchange(): return lax.ppermute(x, 'seq', pairs)]
    unnamed x2 -> x0, local copies, waits for them, and re-layouts: 0.66 us -> none
    pallas_call x1, Pallas kernels: 3.57 us -> 3.06 us  [prepare(): pl.pallas_call(functools.partial(prepare_kernel, groups), in_specs=[HBM_S...]
    ppermute x7, starting transfers between devices: 12.7 us -> 12.2 us  [exchange(): return lax.ppermute(x, 'seq', pairs)]
  transfers between devices with their start and end apart: 16 -> 16, of which waited for: 7 -> 9; matrix products, arithmetic and copies ran while one was open for 3% -> 3% of each run, Pallas kernels for 16% -> 15%
where the time goes in v4:
time: 35.7 us; the launch traced here: 35.5 us
  starting transfers between devices  14.3 us (40%)
  Pallas kernels  10.6 us (30%)
  waiting for transfers between devices  8.22 us (23%)
  other arithmetic  1.04 us (3%)
  between operations  0.69 us (2%)
  local copies, waits for them, and re-layouts  0.64 us (2%)
    ppermute x7, starting transfers between devices, exchange(): return lax.ppermute(x, 'seq', pairs)  12.2 us
    ppermute x7, waiting for transfers between devices, exchange(): return lax.ppermute(x, 'seq', pairs)  6.11 us
    pallas_call x1, Pallas kernels, attention(): pl.pallas_call(functools.partial(attention_kernel, chips, piece_rows, joi...  5.28 us
    pallas_call x1, Pallas kernels, prepare(): pl.pallas_call(functools.partial(prepare_kernel, groups), in_specs=[HBM_S...  3.06 us
    pallas_call x1, Pallas kernels, query_grads(): pl.pallas_call(functools.partial(query_grad_kernel, joined), in_specs=[VM...  2.25 us
    ppermute x9, starting transfers between devices, swap_core(): return lax.ppermute(x, 'seq', pairs)  2.11 us
    ppermute x9, waiting for transfers between devices, swap_core(): return lax.ppermute(x, 'seq', pairs)  2.11 us
    select_n x1, other arithmetic, local(): kv = [jnp.where(kind == 0, prompt_keys[None], prompt_values[None])]  0.91 us
  transfers between devices with their start and end apart: 16, of which 9 were waited for; matrix products, arithmetic and copies ran while one was open for 3% of the time, Pallas kernels for 15%

profile of v4, /device:TPU:0, one launch (start us, length us, event | category | flops | bytes accessed | tf_op | source)
XLA Modules:
  0.0 35.5 jit_solution(16755940487642797388)
XLA Ops:
  0.6 4.1 %collective-permute-start.1 = (bf16[48,512]{1,0:T(8,128)(2,1)}, bf16[48,512]{1,0:T(8,128)(2,1)S(1)}, u32[]{:S(2)}, u32[]{:S(2)}) collective-permute-start(bf16[48,512]{1,0:T(8,128)(2,1)} %param.14), channel_id=1, source_target_pairs={{0,4},{1,5},{4,0},{5,1},{2,6},{3,7},{6,2},{7,3},{8,12},{9,13},{12,... | collective-permute-start | bytes 147464 | tf_op jit(solution)/shard_map/ppermute | solution.py:289
  4.8 0.9 %broadcast_select_fusion.rest_0_ = bf16[2,48,512]{2,1,0:T(8,128)(2,1)S(1)} fusion(pred[2]{0:T(512)(128)(4,1)S(1)} %iota_compare_fusion, bf16[48,512]{1,0:T(8,128)(2,1)} %param.15, bf16[48,512]{1,0:T(8,128)(2,1)} %param.14), kind=kLoop, calls=%fused_computation.4 | loop fusion | flops 49152 | bytes 196610 | tf_op jit(solution)/shard_map/jit(_where)/select_n | solution.py:305
  5.7 3.9 %collective-permute-start.5 = (bf16[2,48,512]{2,1,0:T(8,128)(2,1)S(1)}, bf16[2,48,512]{2,1,0:T(8,128)(2,1)S(1)}, u32[]{:S(2)}, u32[]{:S(2)}) collective-permute-start(bf16[2,48,512]{2,1,0:T(8,128)(2,1)S(1)} %broadcast_select_fusion.rest_0_), channel_id=1, source_target_pairs={{0,6},{1,7},{6,0},{7,1},{2,4},{3,5},{4,2},{5,3},{8,14},{9,15},{14,... | collective-permute-start | bytes 294920 | tf_op jit(solution)/shard_map/ppermute | solution.py:289
  9.7 3.1 %shard_map.119 = (bf16[4096,128]{1,0:T(8,128)(2,1)S(1)}, bf16[4096,256]{1,0:T(8,128)(2,1)S(1)}, bf16[128,4096]{1,0:T(8,128)(2,1)S(1)}, bf16[128,4096]{1,0:T(8,12...) custom-call(s32[8]{0:T(128)} %refs_0_.1, ...), custom_call_target="tpu_custom_call" | custom-call | flops 2097152000 | bytes 8388608 | tf_op jit(solution)/shard_map/pallas_call | solution.py:102
  12.7 0.4 %collective-permute-done.3.rest_3_ = bf16[48,512]{1,0:T(8,128)(2,1)S(1)} collective-permute-done((bf16[48,512]{1,0:T(8,128)(2,1)}, bf16[48,512]{1,0:T(8,128)(2,1)S(1)}, u32[]{:S(2)}, u32[]{:S(2)}) %collective-permute-start.3) | collective-permute-done | bytes 49184 | tf_op jit(solution)/shard_map/ppermute | solution.py:289
  13.1 0.5 %collective-permute-start.4 = (bf16[48,512]{1,0:T(8,128)(2,1)S(1)}, bf16[48,512]{1,0:T(8,128)(2,1)S(1)}, u32[]{:S(2)}, u32[]{:S(2)}) collective-permute-start(bf16[48,512]{1,0:T(8,128)(2,1)S(1)} %collective-permute-done.3.rest_3_), channel_id=1, source_target_pairs={{0,1},{1,0},{2,3},{3,2},{4,5},{5,4},{6,7},{7,6},{8,9},{9,8},{10,11... | collective-permute-start | bytes 147464 | tf_op jit(solution)/shard_map/ppermute | solution.py:298
  13.6 0.7 %collective-permute-done.2.rest_7_ = bf16[48,512]{1,0:T(8,128)(2,1)S(1)} collective-permute-done((bf16[48,512]{1,0:T(8,128)(2,1)S(1)}, bf16[48,512]{1,0:T(8,128)(2,1)S(1)}, u32[]{:S(2)}, u32[]{:S(2)}) %collective-permute-start.2) | collective-permute-done | bytes 49184 | tf_op jit(solution)/shard_map/ppermute | solution.py:298
  14.3 0.2 collective-permute-done.4.rest_8_
  14.5 0.4 %collective-permute-done.rest_1_ = bf16[2,48,512]{2,1,0:T(8,128)(2,1)S(1)} collective-permute-done((bf16[2,48,512]{2,1,0:T(8,128)(2,1)S(1)}, bf16[2,48,512]{2,1,0:T(8,128)(2,1)S(1)}, u32[]{:S(2)}, u32[]{:S(2)}) %collective-permute-start) | collective-permute-done | bytes 98336 | tf_op jit(solution)/shard_map/ppermute | solution.py:289
  14.9 0.5 %collective-permute-start.8 = (bf16[2,48,512]{2,1,0:T(8,128)(2,1)S(1)}, bf16[2,48,512]{2,1,0:T(8,128)(2,1)S(1)}, u32[]{:S(2)}, u32[]{:S(2)}) collective-permute-start(bf16[2,48,512]{2,1,0:T(8,128)(2,1)S(1)} %collective-permute-done.5.rest_4_), channel_id=1, source_target_pairs={{0,1},{1,0},{2,3},{3,2},{4,5},{5,4},{6,7},{7,6},{8,9},{9,8},{10,11... | collective-permute-start | bytes 294920 | tf_op jit(solution)/shard_map/ppermute | solution.py:298
  15.4 0.8 %collective-permute-done.7.rest_6_ = bf16[2,48,512]{2,1,0:T(8,128)(2,1)S(1)} collective-permute-done((bf16[2,48,512]{2,1,0:T(8,128)(2,1)S(1)}, bf16[2,48,512]{2,1,0:T(8,128)(2,1)S(1)}, u32[]{:S(2)}, u32[]{:S(2)}) %collective-permute-start.7) | collective-permute-done | bytes 98336 | tf_op jit(solution)/shard_map/ppermute | solution.py:298
  16.2 0.2 collective-permute-done.8.rest_9_
  16.3 5.3 %shard_map.120 = (bf16[4096,512]{1,0:T(8,128)(2,1)S(1)}, bf16[128,512]{1,0:T(8,128)(2,1)S(1)}, bf16[128,512]{1,0:T(8,128)(2,1)S(1)}, f32[2,48,512]{2,1,0:T(8,128...) custom-call(f32[128,128]{1,0:T(8,128)S(1)} %get-tuple-element.33.liv, ...), custom_call_target="tpu_custom_call" | custom-call | flops 2684354560 | bytes 5242880 | tf_op jit(solution)/shard_map/pallas_call | solution.py:215
  21.6 0.4 %collective-permute-start.9 = (bf16[2,48,512]{2,1,0:T(8,128)(2,1)S(1)}, bf16[2,48,512]{2,1,0:T(8,128)(2,1)S(1)}, u32[]{:S(2)}, u32[]{:S(2)}) collective-permute-start(bf16[2,48,512]{2,1,0:T(8,128)(2,1)S(1)} %get-tuple-element.46), channel_id=1, source_target_pairs={{0,1},{1,0},{2,3},{3,2},{4,5},{5,4},{6,7},{7,6},{8,9},{9,8},{10,11... | collective-permute-start | bytes 294920 | tf_op jit(solution)/shard_map/ppermute | solution.py:298
  22.0 0.2 collective-permute-start.10
  22.2 0.4 %collective-permute-start.11 = (bf16[2,48,512]{2,1,0:T(8,128)(2,1)S(1)}, bf16[2,48,512]{2,1,0:T(8,128)(2,1)S(1)}, u32[]{:S(2)}, u32[]{:S(2)}) collective-permute-start(bf16[2,48,512]{2,1,0:T(8,128)(2,1)S(1)} %get-tuple-element.50), channel_id=1, source_target_pairs={{0,1},{1,0},{2,3},{3,2},{4,5},{5,4},{6,7},{7,6},{8,9},{9,8},{10,11... | collective-permute-start | bytes 294920 | tf_op jit(solution)/shard_map/ppermute | solution.py:298
  22.6 0.2 collective-permute-start.13
  22.7 0.3 collective-permute-done.9
  23.0 2.0 %collective-permute-start.12 = (bf16[2,48,512]{2,1,0:T(8,128)(2,1)S(1)}, bf16[2,48,512]{2,1,0:T(8,128)(2,1)S(1)}, u32[]{:S(2)}, u32[]{:S(2)}) collective-permute-start(bf16[2,48,512]{2,1,0:T(8,128)(2,1)S(1)} %add_convert_fusion.3), channel_id=1, source_target_pairs={{0,4},{1,5},{4,0},{5,1},{2,6},{3,7},{6,2},{7,3},{8,12},{9,13},{12,... | collective-permute-start | bytes 294920 | tf_op jit(solution)/shard_map/ppermute | solution.py:289
  25.0 2.0 %collective-permute-start.14 = (bf16[2,48,512]{2,1,0:T(8,128)(2,1)S(1)}, bf16[2,48,512]{2,1,0:T(8,128)(2,1)S(1)}, u32[]{:S(2)}, u32[]{:S(2)}) collective-permute-start(bf16[2,48,512]{2,1,0:T(8,128)(2,1)S(1)} %add_convert_fusion.2), channel_id=1, source_target_pairs={{0,6},{1,7},{6,0},{7,1},{2,4},{3,5},{4,2},{5,3},{8,14},{9,15},{14,... | collective-permute-start | bytes 294920 | tf_op jit(solution)/shard_map/ppermute | solution.py:289
  27.2 2.2 %shard_map.121 = (bf16[128,4096]{1,0:T(8,128)(2,1)}, bf16[128,512]{1,0:T(8,128)(2,1)}, bf16[128,512]{1,0:T(8,128)(2,1)}) custom-call(bf16[4096,512]{1,0:T(8,128)(2,1)S(1)} %get-tuple-element.51.ds_ref, bf16[128,512]{1,0:T(8,128)(2,1)S(1)} %get-tuple-element.38.rk_ref, bf16[128,512]{1,0:T(8,128)(2,1)S(1)} %get-tuple-element.52.drk_in, ...), custom_call_target="tpu_custom_call" | custom-call | flops 1073741824 | bytes 8388608 | tf_op jit(solution)/shard_map/pallas_call | solution.py:270
  29.5 4.4 %collective-permute-done.12 = bf16[2,48,512]{2,1,0:T(8,128)(2,1)S(1)} collective-permute-done((bf16[2,48,512]{2,1,0:T(8,128)(2,1)S(1)}, bf16[2,48,512]{2,1,0:T(8,128)(2,1)S(1)}, u32[]{:S(2)}, u32[]{:S(2)}) %collective-permute-start.12) | collective-permute-done | bytes 98336 | tf_op jit(solution)/shard_map/ppermute | solution.py:289
  33.9 0.9 %collective-permute-done.15 = bf16[2,48,512]{2,1,0:T(8,128)(2,1)S(1)} collective-permute-done((bf16[2,48,512]{2,1,0:T(8,128)(2,1)S(1)}, bf16[2,48,512]{2,1,0:T(8,128)(2,1)S(1)}, u32[]{:S(2)}, u32[]{:S(2)}) %collective-permute-start.15) | collective-permute-done | bytes 98336 | tf_op jit(solution)/shard_map/ppermute | solution.py:289
  34.9 0.6 %slice_bitcast_fusion = (bf16[48,512]{1,0:T(8,128)(2,1)}, bf16[48,512]{1,0:T(8,128)(2,1)}) fusion(bf16[2,48,512]{2,1,0:T(8,128)(2,1)S(1)} %add_convert_fusion), kind=kLoop, calls=%fused_computation.5 | loop fusion | bytes 196608 | tf_op jit(solution)/shard_map/squeeze | solution.py:324
  (18 shorter events, 0.3 us)
Async XLA Ops:
  0.6 12.5 %collective-permute-start.1 = (bf16[48,512]{1,0:T(8,128)(2,1)}, bf16[48,512]{1,0:T(8,128)(2,1)S(1)}, u32[]{:S(2)}, u32[]{:S(2)}) collective-permute-start(bf16[48,512]{1,0:T(8,128)(2,1)} %param.14), channel_id=1, source_target_pairs={{0,4},{1,5},{4,0},{5,1},{2,6},{3,7},{6,2},{7,3},{8,12},{9,13},{12,... | collective-permute-start | bytes 147464 | tf_op jit(solution)/shard_map/ppermute | solution.py:289
  4.7 8.4 %collective-permute-start.3 = (bf16[48,512]{1,0:T(8,128)(2,1)}, bf16[48,512]{1,0:T(8,128)(2,1)S(1)}, u32[]{:S(2)}, u32[]{:S(2)}) collective-permute-start(bf16[48,512]{1,0:T(8,128)(2,1)} %param.15), channel_id=1, source_target_pairs={{0,4},{1,5},{4,0},{5,1},{2,6},{3,7},{6,2},{7,3},{8,12},{9,13},{12,... | collective-permute-start | bytes 147464 | tf_op jit(solution)/shard_map/ppermute | solution.py:289
  5.7 7.9 %collective-permute-start.5 = (bf16[2,48,512]{2,1,0:T(8,128)(2,1)S(1)}, bf16[2,48,512]{2,1,0:T(8,128)(2,1)S(1)}, u32[]{:S(2)}, u32[]{:S(2)}) collective-permute-start(bf16[2,48,512]{2,1,0:T(8,128)(2,1)S(1)} %broadcast_select_fusion.rest_0_), channel_id=1, source_target_pairs={{0,6},{1,7},{6,0},{7,1},{2,4},{3,5},{4,2},{5,3},{8,14},{9,15},{14,... | collective-permute-start | bytes 294920 | tf_op jit(solution)/shard_map/ppermute | solution.py:289
  9.7 5.2 %collective-permute-start = (bf16[2,48,512]{2,1,0:T(8,128)(2,1)S(1)}, bf16[2,48,512]{2,1,0:T(8,128)(2,1)S(1)}, u32[]{:S(2)}, u32[]{:S(2)}) collective-permute-start(bf16[2,48,512]{2,1,0:T(8,128)(2,1)S(1)} %broadcast_select_fusion.rest_0_), channel_id=1, source_target_pairs={{0,2},{1,3},{2,0},{3,1},{4,6},{5,7},{6,4},{7,5},{8,10},{9,11},{10,... | collective-permute-start | bytes 294920 | tf_op jit(solution)/shard_map/ppermute | solution.py:289
  13.1 1.2 %collective-permute-start.2 = (bf16[48,512]{1,0:T(8,128)(2,1)S(1)}, bf16[48,512]{1,0:T(8,128)(2,1)S(1)}, u32[]{:S(2)}, u32[]{:S(2)}) collective-permute-start(bf16[48,512]{1,0:T(8,128)(2,1)S(1)} %collective-permute-done.1.rest_2_), channel_id=1, source_target_pairs={{0,1},{1,0},{2,3},{3,2},{4,5},{5,4},{6,7},{7,6},{8,9},{9,8},{10,11... | collective-permute-start | bytes 147464 | tf_op jit(solution)/shard_map/ppermute | solution.py:298
  13.1 1.4 %collective-permute-start.4 = (bf16[48,512]{1,0:T(8,128)(2,1)S(1)}, bf16[48,512]{1,0:T(8,128)(2,1)S(1)}, u32[]{:S(2)}, u32[]{:S(2)}) collective-permute-start(bf16[48,512]{1,0:T(8,128)(2,1)S(1)} %collective-permute-done.3.rest_3_), channel_id=1, source_target_pairs={{0,1},{1,0},{2,3},{3,2},{4,5},{5,4},{6,7},{7,6},{8,9},{9,8},{10,11... | collective-permute-start | bytes 147464 | tf_op jit(solution)/shard_map/ppermute | solution.py:298
  13.6 1.8 %collective-permute-start.6 = (bf16[2,48,512]{2,1,0:T(8,128)(2,1)S(1)}, bf16[2,48,512]{2,1,0:T(8,128)(2,1)S(1)}, u32[]{:S(2)}, u32[]{:S(2)}) collective-permute-start(bf16[2,48,512]{2,1,0:T(8,128)(2,1)S(1)} %broadcast_select_fusion.rest_0_), channel_id=1, source_target_pairs={{0,1},{1,0},{2,3},{3,2},{4,5},{5,4},{6,7},{7,6},{8,9},{9,8},{10,11... | collective-permute-start | bytes 294920 | tf_op jit(solution)/shard_map/ppermute | solution.py:298
  14.9 1.3 %collective-permute-start.7 = (bf16[2,48,512]{2,1,0:T(8,128)(2,1)S(1)}, bf16[2,48,512]{2,1,0:T(8,128)(2,1)S(1)}, u32[]{:S(2)}, u32[]{:S(2)}) collective-permute-start(bf16[2,48,512]{2,1,0:T(8,128)(2,1)S(1)} %collective-permute-done.rest_1_), channel_id=1, source_target_pairs={{0,1},{1,0},{2,3},{3,2},{4,5},{5,4},{6,7},{7,6},{8,9},{9,8},{10,11... | collective-permute-start | bytes 294920 | tf_op jit(solution)/shard_map/ppermute | solution.py:298
  14.9 1.5 %collective-permute-start.8 = (bf16[2,48,512]{2,1,0:T(8,128)(2,1)S(1)}, bf16[2,48,512]{2,1,0:T(8,128)(2,1)S(1)}, u32[]{:S(2)}, u32[]{:S(2)}) collective-permute-start(bf16[2,48,512]{2,1,0:T(8,128)(2,1)S(1)} %collective-permute-done.5.rest_4_), channel_id=1, source_target_pairs={{0,1},{1,0},{2,3},{3,2},{4,5},{5,4},{6,7},{7,6},{8,9},{9,8},{10,11... | collective-permute-start | bytes 294920 | tf_op jit(solution)/shard_map/ppermute | solution.py:298
  21.6 1.4 %collective-permute-start.9 = (bf16[2,48,512]{2,1,0:T(8,128)(2,1)S(1)}, bf16[2,48,512]{2,1,0:T(8,128)(2,1)S(1)}, u32[]{:S(2)}, u32[]{:S(2)}) collective-permute-start(bf16[2,48,512]{2,1,0:T(8,128)(2,1)S(1)} %get-tuple-element.46), channel_id=1, source_target_pairs={{0,1},{1,0},{2,3},{3,2},{4,5},{5,4},{6,7},{7,6},{8,9},{9,8},{10,11... | collective-permute-start | bytes 294920 | tf_op jit(solution)/shard_map/ppermute | solution.py:298
  22.0 3.0 %collective-permute-start.10 = (bf16[2,48,512]{2,1,0:T(8,128)(2,1)S(1)}, bf16[2,48,512]{2,1,0:T(8,128)(2,1)S(1)}, u32[]{:S(2)}, u32[]{:S(2)}) collective-permute-start(bf16[2,48,512]{2,1,0:T(8,128)(2,1)S(1)} %get-tuple-element.48), channel_id=1, source_target_pairs={{0,1},{1,0},{2,3},{3,2},{4,5},{5,4},{6,7},{7,6},{8,9},{9,8},{10,11... | collective-permute-start | bytes 294920 | tf_op jit(solution)/shard_map/ppermute | solution.py:298
  22.2 4.9 %collective-permute-start.11 = (bf16[2,48,512]{2,1,0:T(8,128)(2,1)S(1)}, bf16[2,48,512]{2,1,0:T(8,128)(2,1)S(1)}, u32[]{:S(2)}, u32[]{:S(2)}) collective-permute-start(bf16[2,48,512]{2,1,0:T(8,128)(2,1)S(1)} %get-tuple-element.50), channel_id=1, source_target_pairs={{0,1},{1,0},{2,3},{3,2},{4,5},{5,4},{6,7},{7,6},{8,9},{9,8},{10,11... | collective-permute-start | bytes 294920 | tf_op jit(solution)/shard_map/ppermute | solution.py:298
  22.6 11.3 %collective-permute-start.13 = (bf16[2,48,512]{2,1,0:T(8,128)(2,1)S(1)}, bf16[2,48,512]{2,1,0:T(8,128)(2,1)S(1)}, u32[]{:S(2)}, u32[]{:S(2)}) collective-permute-start(bf16[2,48,512]{2,1,0:T(8,128)(2,1)S(1)} %get-tuple-element.59), channel_id=1, source_target_pairs={{0,1},{1,0},{2,3},{3,2},{4,5},{5,4},{6,7},{7,6},{8,9},{9,8},{10,11... | collective-permute-start | bytes 294920 | tf_op jit(solution)/shard_map/ppermute | solution.py:298
  23.0 10.8 %collective-permute-start.12 = (bf16[2,48,512]{2,1,0:T(8,128)(2,1)S(1)}, bf16[2,48,512]{2,1,0:T(8,128)(2,1)S(1)}, u32[]{:S(2)}, u32[]{:S(2)}) collective-permute-start(bf16[2,48,512]{2,1,0:T(8,128)(2,1)S(1)} %add_convert_fusion.3), channel_id=1, source_target_pairs={{0,4},{1,5},{4,0},{5,1},{2,6},{3,7},{6,2},{7,3},{8,12},{9,13},{12,... | collective-permute-start | bytes 294920 | tf_op jit(solution)/shard_map/ppermute | solution.py:289
  25.0 8.8 %collective-permute-start.14 = (bf16[2,48,512]{2,1,0:T(8,128)(2,1)S(1)}, bf16[2,48,512]{2,1,0:T(8,128)(2,1)S(1)}, u32[]{:S(2)}, u32[]{:S(2)}) collective-permute-start(bf16[2,48,512]{2,1,0:T(8,128)(2,1)S(1)} %add_convert_fusion.2), channel_id=1, source_target_pairs={{0,6},{1,7},{6,0},{7,1},{2,4},{3,5},{4,2},{5,3},{8,14},{9,15},{14,... | collective-permute-start | bytes 294920 | tf_op jit(solution)/shard_map/ppermute | solution.py:289
  27.1 7.7 %collective-permute-start.15 = (bf16[2,48,512]{2,1,0:T(8,128)(2,1)S(1)}, bf16[2,48,512]{2,1,0:T(8,128)(2,1)S(1)}, u32[]{:S(2)}, u32[]{:S(2)}) collective-permute-start(bf16[2,48,512]{2,1,0:T(8,128)(2,1)S(1)} %add_convert_fusion.1), channel_id=1, source_target_pairs={{0,2},{1,3},{2,0},{3,1},{4,6},{5,7},{6,4},{7,5},{8,10},{9,11},{10,... | collective-permute-start | bytes 294920 | tf_op jit(solution)/shard_map/ppermute | solution.py:289

commit v5 on v4

--- a/solution.py
+++ b/solution.py
@@ -313,11 +313,13 @@
     other = [first if i == 2 else [swap_core(x, chips) for x in piece] for i, piece in enumerate(own)]
     ds, drk, drv, *grads = attention(prepared, own + other)
     both = [None] * chips
-    for step in [0] + steps[1:] + steps[:1]:
+    for step in steps[1:] + steps[:1]:
         both[step] = grads[step] + swap_core(grads[chips + step], chips).astype(F32)
-    sent = [x.astype(BF16) for x in both]
-    back = [exchange(sent[step], chip_links(chips, step)) for step in steps[1:] + steps[:1]]
-    ds = lax.optimization_barrier((ds, [sent[step] for step in steps[1:] + steps[:1]]))[0]
+    sent = [x.astype(BF16) for x in both[1:]]
+    home = lax.optimization_barrier((grads[chips], sent[0]))[0]
+    both[0] = grads[0] + swap_core(home, chips).astype(F32)
+    back = [exchange(sent[step - 1], chip_links(chips, step)) for step in steps[1:] + steps[:1]]
+    ds = lax.optimization_barrier((ds, [sent[step - 1] for step in steps[1:] + steps[:1]]))[0]
     dq, drk, drv = query_grads(ds, prepared[5], drk, drv, own + other)
     dq, back[0] = lax.optimization_barrier((dq, back[0]))
     total = sum([x.astype(F32) for x in back], both[0]).astype(BF16)

time: 35.7 us -> 35.7 us (level)
  no operation moved by 1% of the time
where the time goes in v5:
time: 35.7 us; the launch traced here: 35.5 us
  starting transfers between devices  14.3 us (40%)
  Pallas kernels  10.6 us (30%)
  waiting for transfers between devices  8.29 us (23%)
  other arithmetic  1.04 us (3%)
  between operations  0.7 us (2%)
  local copies, waits for them, and re-layouts  0.64 us (2%)
    ppermute x7, starting transfers between devices, exchange(): return lax.ppermute(x, 'seq', pairs)  12.2 us
    ppermute x7, waiting for transfers between devices, exchange(): return lax.ppermute(x, 'seq', pairs)  6.04 us
    pallas_call x1, Pallas kernels, attention(): pl.pallas_call(functools.partial(attention_kernel, chips, piece_rows, joi...  5.28 us
    pallas_call x1, Pallas kernels, prepare(): pl.pallas_call(functools.partial(prepare_kernel, groups), in_specs=[HBM_S...  3.06 us
    ppermute x9, waiting for transfers between devices, swap_core(): return lax.ppermute(x, 'seq', pairs)  2.26 us
    pallas_call x1, Pallas kernels, query_grads(): pl.pallas_call(functools.partial(query_grad_kernel, joined), in_specs=[VM...  2.25 us
    ppermute x9, starting transfers between devices, swap_core(): return lax.ppermute(x, 'seq', pairs)  2.03 us
    select_n x1, other arithmetic, local(): kv = [jnp.where(kind == 0, prompt_keys[None], prompt_values[None])]  0.91 us
  transfers between devices with their start and end apart: 16, of which 9 were waited for; matrix products, arithmetic and copies ran while one was open for 3% of the time, Pallas kernels for 15%

profile of v5, /device:TPU:0, one launch (start us, length us, event | category | flops | bytes accessed | tf_op | source)
XLA Modules:
  0.0 35.5 jit_solution(215119225358625691)
XLA Ops:
  0.6 4.1 %collective-permute-start.1 = (bf16[48,512]{1,0:T(8,128)(2,1)}, bf16[48,512]{1,0:T(8,128)(2,1)S(1)}, u32[]{:S(2)}, u32[]{:S(2)}) collective-permute-start(bf16[48,512]{1,0:T(8,128)(2,1)} %param.14), channel_id=1, source_target_pairs={{0,4},{1,5},{4,0},{5,1},{2,6},{3,7},{6,2},{7,3},{8,12},{9,13},{12,... | collective-permute-start | bytes 147464 | tf_op jit(solution)/shard_map/ppermute | solution.py:289
  4.7 0.1 collective-permute-start.3
  4.8 0.9 %broadcast_select_fusion.rest_0_ = bf16[2,48,512]{2,1,0:T(8,128)(2,1)S(1)} fusion(pred[2]{0:T(512)(128)(4,1)S(1)} %iota_compare_fusion, bf16[48,512]{1,0:T(8,128)(2,1)} %param.15, bf16[48,512]{1,0:T(8,128)(2,1)} %param.14), kind=kLoop, calls=%fused_computation.4 | loop fusion | flops 49152 | bytes 196610 | tf_op jit(solution)/shard_map/jit(_where)/select_n | solution.py:305
  5.7 3.9 %collective-permute-start.5 = (bf16[2,48,512]{2,1,0:T(8,128)(2,1)S(1)}, bf16[2,48,512]{2,1,0:T(8,128)(2,1)S(1)}, u32[]{:S(2)}, u32[]{:S(2)}) collective-permute-start(bf16[2,48,512]{2,1,0:T(8,128)(2,1)S(1)} %broadcast_select_fusion.rest_0_), channel_id=1, source_target_pairs={{0,6},{1,7},{6,0},{7,1},{2,4},{3,5},{4,2},{5,3},{8,14},{9,15},{14,... | collective-permute-start | bytes 294920 | tf_op jit(solution)/shard_map/ppermute | solution.py:289
  9.7 3.1 %shard_map.119 = (bf16[4096,128]{1,0:T(8,128)(2,1)S(1)}, bf16[4096,256]{1,0:T(8,128)(2,1)S(1)}, bf16[128,4096]{1,0:T(8,128)(2,1)S(1)}, bf16[128,4096]{1,0:T(8,12...) custom-call(s32[8]{0:T(128)} %refs_0_.1, ...), custom_call_target="tpu_custom_call" | custom-call | flops 2097152000 | bytes 8388608 | tf_op jit(solution)/shard_map/pallas_call | solution.py:102
  12.7 0.4 %collective-permute-done.3.rest_3_ = bf16[48,512]{1,0:T(8,128)(2,1)S(1)} collective-permute-done((bf16[48,512]{1,0:T(8,128)(2,1)}, bf16[48,512]{1,0:T(8,128)(2,1)S(1)}, u32[]{:S(2)}, u32[]{:S(2)}) %collective-permute-start.3) | collective-permute-done | bytes 49184 | tf_op jit(solution)/shard_map/ppermute | solution.py:289
  13.1 0.5 %collective-permute-start.4 = (bf16[48,512]{1,0:T(8,128)(2,1)S(1)}, bf16[48,512]{1,0:T(8,128)(2,1)S(1)}, u32[]{:S(2)}, u32[]{:S(2)}) collective-permute-start(bf16[48,512]{1,0:T(8,128)(2,1)S(1)} %collective-permute-done.3.rest_3_), channel_id=1, source_target_pairs={{0,1},{1,0},{2,3},{3,2},{4,5},{5,4},{6,7},{7,6},{8,9},{9,8},{10,11... | collective-permute-start | bytes 147464 | tf_op jit(solution)/shard_map/ppermute | solution.py:298
  13.6 0.7 %collective-permute-done.2.rest_7_ = bf16[48,512]{1,0:T(8,128)(2,1)S(1)} collective-permute-done((bf16[48,512]{1,0:T(8,128)(2,1)S(1)}, bf16[48,512]{1,0:T(8,128)(2,1)S(1)}, u32[]{:S(2)}, u32[]{:S(2)}) %collective-permute-start.2) | collective-permute-done | bytes 49184 | tf_op jit(solution)/shard_map/ppermute | solution.py:298
  14.3 0.2 collective-permute-done.4.rest_8_
  14.5 0.4 %collective-permute-done.rest_1_ = bf16[2,48,512]{2,1,0:T(8,128)(2,1)S(1)} collective-permute-done((bf16[2,48,512]{2,1,0:T(8,128)(2,1)S(1)}, bf16[2,48,512]{2,1,0:T(8,128)(2,1)S(1)}, u32[]{:S(2)}, u32[]{:S(2)}) %collective-permute-start) | collective-permute-done | bytes 98336 | tf_op jit(solution)/shard_map/ppermute | solution.py:289
  14.9 0.5 %collective-permute-start.8 = (bf16[2,48,512]{2,1,0:T(8,128)(2,1)S(1)}, bf16[2,48,512]{2,1,0:T(8,128)(2,1)S(1)}, u32[]{:S(2)}, u32[]{:S(2)}) collective-permute-start(bf16[2,48,512]{2,1,0:T(8,128)(2,1)S(1)} %collective-permute-done.5.rest_4_), channel_id=1, source_target_pairs={{0,1},{1,0},{2,3},{3,2},{4,5},{5,4},{6,7},{7,6},{8,9},{9,8},{10,11... | collective-permute-start | bytes 294920 | tf_op jit(solution)/shard_map/ppermute | solution.py:298
  15.4 0.8 %collective-permute-done.7.rest_6_ = bf16[2,48,512]{2,1,0:T(8,128)(2,1)S(1)} collective-permute-done((bf16[2,48,512]{2,1,0:T(8,128)(2,1)S(1)}, bf16[2,48,512]{2,1,0:T(8,128)(2,1)S(1)}, u32[]{:S(2)}, u32[]{:S(2)}) %collective-permute-start.7) | collective-permute-done | bytes 98336 | tf_op jit(solution)/shard_map/ppermute | solution.py:298
  16.2 0.2 collective-permute-done.8.rest_9_
  16.3 5.3 %shard_map.120 = (bf16[4096,512]{1,0:T(8,128)(2,1)S(1)}, bf16[128,512]{1,0:T(8,128)(2,1)S(1)}, bf16[128,512]{1,0:T(8,128)(2,1)S(1)}, f32[2,48,512]{2,1,0:T(8,128...) custom-call(f32[128,128]{1,0:T(8,128)S(1)} %get-tuple-element.34.liv, ...), custom_call_target="tpu_custom_call" | custom-call | flops 2684354560 | bytes 5242880 | tf_op jit(solution)/shard_map/pallas_call | solution.py:215
  21.6 0.4 %collective-permute-start.9 = (bf16[2,48,512]{2,1,0:T(8,128)(2,1)S(1)}, bf16[2,48,512]{2,1,0:T(8,128)(2,1)S(1)}, u32[]{:S(2)}, u32[]{:S(2)}) collective-permute-start(bf16[2,48,512]{2,1,0:T(8,128)(2,1)S(1)} %get-tuple-element.47), channel_id=1, source_target_pairs={{0,1},{1,0},{2,3},{3,2},{4,5},{5,4},{6,7},{7,6},{8,9},{9,8},{10,11... | collective-permute-start | bytes 294920 | tf_op jit(solution)/shard_map/ppermute | solution.py:298
  22.0 0.2 collective-permute-start.10
  22.2 0.4 %collective-permute-start.11 = (bf16[2,48,512]{2,1,0:T(8,128)(2,1)S(1)}, bf16[2,48,512]{2,1,0:T(8,128)(2,1)S(1)}, u32[]{:S(2)}, u32[]{:S(2)}) collective-permute-start(bf16[2,48,512]{2,1,0:T(8,128)(2,1)S(1)} %get-tuple-element.51), channel_id=1, source_target_pairs={{0,1},{1,0},{2,3},{3,2},{4,5},{5,4},{6,7},{7,6},{8,9},{9,8},{10,11... | collective-permute-start | bytes 294920 | tf_op jit(solution)/shard_map/ppermute | solution.py:298
  22.6 0.4 %collective-permute-done.9 = bf16[2,48,512]{2,1,0:T(8,128)(2,1)S(1)} collective-permute-done((bf16[2,48,512]{2,1,0:T(8,128)(2,1)S(1)}, bf16[2,48,512]{2,1,0:T(8,128)(2,1)S(1)}, u32[]{:S(2)}, u32[]{:S(2)}) %collective-permute-start.9) | collective-permute-done | bytes 98336 | tf_op jit(solution)/shard_map/ppermute | solution.py:298
  23.0 2.0 %collective-permute-start.12 = (bf16[2,48,512]{2,1,0:T(8,128)(2,1)S(1)}, bf16[2,48,512]{2,1,0:T(8,128)(2,1)S(1)}, u32[]{:S(2)}, u32[]{:S(2)}) collective-permute-start(bf16[2,48,512]{2,1,0:T(8,128)(2,1)S(1)} %add_convert_fusion.3), channel_id=1, source_target_pairs={{0,4},{1,5},{4,0},{5,1},{2,6},{3,7},{6,2},{7,3},{8,12},{9,13},{12,... | collective-permute-start | bytes 294920 | tf_op jit(solution)/shard_map/ppermute | solution.py:289
  25.0 2.0 %collective-permute-start.14 = (bf16[2,48,512]{2,1,0:T(8,128)(2,1)S(1)}, bf16[2,48,512]{2,1,0:T(8,128)(2,1)S(1)}, u32[]{:S(2)}, u32[]{:S(2)}) collective-permute-start(bf16[2,48,512]{2,1,0:T(8,128)(2,1)S(1)} %add_convert_fusion.2), channel_id=1, source_target_pairs={{0,6},{1,7},{6,0},{7,1},{2,4},{3,5},{4,2},{5,3},{8,14},{9,15},{14,... | collective-permute-start | bytes 294920 | tf_op jit(solution)/shard_map/ppermute | solution.py:289
  27.3 2.2 %shard_map.121 = (bf16[128,4096]{1,0:T(8,128)(2,1)}, bf16[128,512]{1,0:T(8,128)(2,1)}, bf16[128,512]{1,0:T(8,128)(2,1)}) custom-call(bf16[4096,512]{1,0:T(8,128)(2,1)S(1)} %get-tuple-element.52.ds_ref, bf16[128,512]{1,0:T(8,128)(2,1)S(1)} %get-tuple-element.39.rk_ref, bf16[128,512]{1,0:T(8,128)(2,1)S(1)} %get-tuple-element.53.drk_in, ...), custom_call_target="tpu_custom_call" | custom-call | flops 1073741824 | bytes 8388608 | tf_op jit(solution)/shard_map/pallas_call | solution.py:270
  29.5 4.3 %collective-permute-done.12 = bf16[2,48,512]{2,1,0:T(8,128)(2,1)S(1)} collective-permute-done((bf16[2,48,512]{2,1,0:T(8,128)(2,1)S(1)}, bf16[2,48,512]{2,1,0:T(8,128)(2,1)S(1)}, u32[]{:S(2)}, u32[]{:S(2)}) %collective-permute-start.12) | collective-permute-done | bytes 98336 | tf_op jit(solution)/shard_map/ppermute | solution.py:289
  33.9 0.9 %collective-permute-done.15 = bf16[2,48,512]{2,1,0:T(8,128)(2,1)S(1)} collective-permute-done((bf16[2,48,512]{2,1,0:T(8,128)(2,1)S(1)}, bf16[2,48,512]{2,1,0:T(8,128)(2,1)S(1)}, u32[]{:S(2)}, u32[]{:S(2)}) %collective-permute-start.15) | collective-permute-done | bytes 98336 | tf_op jit(solution)/shard_map/ppermute | solution.py:289
  34.9 0.6 %slice_bitcast_fusion = (bf16[48,512]{1,0:T(8,128)(2,1)}, bf16[48,512]{1,0:T(8,128)(2,1)}) fusion(bf16[2,48,512]{2,1,0:T(8,128)(2,1)S(1)} %add_convert_fusion), kind=kLoop, calls=%fused_computation.5 | loop fusion | bytes 196608 | tf_op jit(solution)/shard_map/squeeze | solution.py:326
  (18 shorter events, 0.3 us)
Async XLA Ops:
  0.6 12.5 %collective-permute-start.1 = (bf16[48,512]{1,0:T(8,128)(2,1)}, bf16[48,512]{1,0:T(8,128)(2,1)S(1)}, u32[]{:S(2)}, u32[]{:S(2)}) collective-permute-start(bf16[48,512]{1,0:T(8,128)(2,1)} %param.14), channel_id=1, source_target_pairs={{0,4},{1,5},{4,0},{5,1},{2,6},{3,7},{6,2},{7,3},{8,12},{9,13},{12,... | collective-permute-start | bytes 147464 | tf_op jit(solution)/shard_map/ppermute | solution.py:289
  4.7 8.4 %collective-permute-start.3 = (bf16[48,512]{1,0:T(8,128)(2,1)}, bf16[48,512]{1,0:T(8,128)(2,1)S(1)}, u32[]{:S(2)}, u32[]{:S(2)}) collective-permute-start(bf16[48,512]{1,0:T(8,128)(2,1)} %param.15), channel_id=1, source_target_pairs={{0,4},{1,5},{4,0},{5,1},{2,6},{3,7},{6,2},{7,3},{8,12},{9,13},{12,... | collective-permute-start | bytes 147464 | tf_op jit(solution)/shard_map/ppermute | solution.py:289
  5.7 7.9 %collective-permute-start.5 = (bf16[2,48,512]{2,1,0:T(8,128)(2,1)S(1)}, bf16[2,48,512]{2,1,0:T(8,128)(2,1)S(1)}, u32[]{:S(2)}, u32[]{:S(2)}) collective-permute-start(bf16[2,48,512]{2,1,0:T(8,128)(2,1)S(1)} %broadcast_select_fusion.rest_0_), channel_id=1, source_target_pairs={{0,6},{1,7},{6,0},{7,1},{2,4},{3,5},{4,2},{5,3},{8,14},{9,15},{14,... | collective-permute-start | bytes 294920 | tf_op jit(solution)/shard_map/ppermute | solution.py:289
  9.7 5.2 %collective-permute-start = (bf16[2,48,512]{2,1,0:T(8,128)(2,1)S(1)}, bf16[2,48,512]{2,1,0:T(8,128)(2,1)S(1)}, u32[]{:S(2)}, u32[]{:S(2)}) collective-permute-start(bf16[2,48,512]{2,1,0:T(8,128)(2,1)S(1)} %broadcast_select_fusion.rest_0_), channel_id=1, source_target_pairs={{0,2},{1,3},{2,0},{3,1},{4,6},{5,7},{6,4},{7,5},{8,10},{9,11},{10,... | collective-permute-start | bytes 294920 | tf_op jit(solution)/shard_map/ppermute | solution.py:289
  13.1 1.2 %collective-permute-start.2 = (bf16[48,512]{1,0:T(8,128)(2,1)S(1)}, bf16[48,512]{1,0:T(8,128)(2,1)S(1)}, u32[]{:S(2)}, u32[]{:S(2)}) collective-permute-start(bf16[48,512]{1,0:T(8,128)(2,1)S(1)} %collective-permute-done.1.rest_2_), channel_id=1, source_target_pairs={{0,1},{1,0},{2,3},{3,2},{4,5},{5,4},{6,7},{7,6},{8,9},{9,8},{10,11... | collective-permute-start | bytes 147464 | tf_op jit(solution)/shard_map/ppermute | solution.py:298
  13.1 1.4 %collective-permute-start.4 = (bf16[48,512]{1,0:T(8,128)(2,1)S(1)}, bf16[48,512]{1,0:T(8,128)(2,1)S(1)}, u32[]{:S(2)}, u32[]{:S(2)}) collective-permute-start(bf16[48,512]{1,0:T(8,128)(2,1)S(1)} %collective-permute-done.3.rest_3_), channel_id=1, source_target_pairs={{0,1},{1,0},{2,3},{3,2},{4,5},{5,4},{6,7},{7,6},{8,9},{9,8},{10,11... | collective-permute-start | bytes 147464 | tf_op jit(solution)/shard_map/ppermute | solution.py:298
  13.6 1.8 %collective-permute-start.6 = (bf16[2,48,512]{2,1,0:T(8,128)(2,1)S(1)}, bf16[2,48,512]{2,1,0:T(8,128)(2,1)S(1)}, u32[]{:S(2)}, u32[]{:S(2)}) collective-permute-start(bf16[2,48,512]{2,1,0:T(8,128)(2,1)S(1)} %broadcast_select_fusion.rest_0_), channel_id=1, source_target_pairs={{0,1},{1,0},{2,3},{3,2},{4,5},{5,4},{6,7},{7,6},{8,9},{9,8},{10,11... | collective-permute-start | bytes 294920 | tf_op jit(solution)/shard_map/ppermute | solution.py:298
  14.9 1.3 %collective-permute-start.7 = (bf16[2,48,512]{2,1,0:T(8,128)(2,1)S(1)}, bf16[2,48,512]{2,1,0:T(8,128)(2,1)S(1)}, u32[]{:S(2)}, u32[]{:S(2)}) collective-permute-start(bf16[2,48,512]{2,1,0:T(8,128)(2,1)S(1)} %collective-permute-done.rest_1_), channel_id=1, source_target_pairs={{0,1},{1,0},{2,3},{3,2},{4,5},{5,4},{6,7},{7,6},{8,9},{9,8},{10,11... | collective-permute-start | bytes 294920 | tf_op jit(solution)/shard_map/ppermute | solution.py:298
  14.9 1.5 %collective-permute-start.8 = (bf16[2,48,512]{2,1,0:T(8,128)(2,1)S(1)}, bf16[2,48,512]{2,1,0:T(8,128)(2,1)S(1)}, u32[]{:S(2)}, u32[]{:S(2)}) collective-permute-start(bf16[2,48,512]{2,1,0:T(8,128)(2,1)S(1)} %collective-permute-done.5.rest_4_), channel_id=1, source_target_pairs={{0,1},{1,0},{2,3},{3,2},{4,5},{5,4},{6,7},{7,6},{8,9},{9,8},{10,11... | collective-permute-start | bytes 294920 | tf_op jit(solution)/shard_map/ppermute | solution.py:298
  21.6 1.4 %collective-permute-start.9 = (bf16[2,48,512]{2,1,0:T(8,128)(2,1)S(1)}, bf16[2,48,512]{2,1,0:T(8,128)(2,1)S(1)}, u32[]{:S(2)}, u32[]{:S(2)}) collective-permute-start(bf16[2,48,512]{2,1,0:T(8,128)(2,1)S(1)} %get-tuple-element.47), channel_id=1, source_target_pairs={{0,1},{1,0},{2,3},{3,2},{4,5},{5,4},{6,7},{7,6},{8,9},{9,8},{10,11... | collective-permute-start | bytes 294920 | tf_op jit(solution)/shard_map/ppermute | solution.py:298
  22.0 3.0 %collective-permute-start.10 = (bf16[2,48,512]{2,1,0:T(8,128)(2,1)S(1)}, bf16[2,48,512]{2,1,0:T(8,128)(2,1)S(1)}, u32[]{:S(2)}, u32[]{:S(2)}) collective-permute-start(bf16[2,48,512]{2,1,0:T(8,128)(2,1)S(1)} %get-tuple-element.49), channel_id=1, source_target_pairs={{0,1},{1,0},{2,3},{3,2},{4,5},{5,4},{6,7},{7,6},{8,9},{9,8},{10,11... | collective-permute-start | bytes 294920 | tf_op jit(solution)/shard_map/ppermute | solution.py:298
  22.2 4.9 %collective-permute-start.11 = (bf16[2,48,512]{2,1,0:T(8,128)(2,1)S(1)}, bf16[2,48,512]{2,1,0:T(8,128)(2,1)S(1)}, u32[]{:S(2)}, u32[]{:S(2)}) collective-permute-start(bf16[2,48,512]{2,1,0:T(8,128)(2,1)S(1)} %get-tuple-element.51), channel_id=1, source_target_pairs={{0,1},{1,0},{2,3},{3,2},{4,5},{5,4},{6,7},{7,6},{8,9},{9,8},{10,11... | collective-permute-start | bytes 294920 | tf_op jit(solution)/shard_map/ppermute | solution.py:298
  23.0 10.8 %collective-permute-start.12 = (bf16[2,48,512]{2,1,0:T(8,128)(2,1)S(1)}, bf16[2,48,512]{2,1,0:T(8,128)(2,1)S(1)}, u32[]{:S(2)}, u32[]{:S(2)}) collective-permute-start(bf16[2,48,512]{2,1,0:T(8,128)(2,1)S(1)} %add_convert_fusion.3), channel_id=1, source_target_pairs={{0,4},{1,5},{4,0},{5,1},{2,6},{3,7},{6,2},{7,3},{8,12},{9,13},{12,... | collective-permute-start | bytes 294920 | tf_op jit(solution)/shard_map/ppermute | solution.py:289
  25.0 8.8 %collective-permute-start.14 = (bf16[2,48,512]{2,1,0:T(8,128)(2,1)S(1)}, bf16[2,48,512]{2,1,0:T(8,128)(2,1)S(1)}, u32[]{:S(2)}, u32[]{:S(2)}) collective-permute-start(bf16[2,48,512]{2,1,0:T(8,128)(2,1)S(1)} %add_convert_fusion.2), channel_id=1, source_target_pairs={{0,6},{1,7},{6,0},{7,1},{2,4},{3,5},{4,2},{5,3},{8,14},{9,15},{14,... | collective-permute-start | bytes 294920 | tf_op jit(solution)/shard_map/ppermute | solution.py:289
  27.1 7.7 %collective-permute-start.15 = (bf16[2,48,512]{2,1,0:T(8,128)(2,1)S(1)}, bf16[2,48,512]{2,1,0:T(8,128)(2,1)S(1)}, u32[]{:S(2)}, u32[]{:S(2)}) collective-permute-start(bf16[2,48,512]{2,1,0:T(8,128)(2,1)S(1)} %add_convert_fusion.1), channel_id=1, source_target_pairs={{0,2},{1,3},{2,0},{3,1},{4,6},{5,7},{6,4},{7,5},{8,10},{9,11},{10,... | collective-permute-start | bytes 294920 | tf_op jit(solution)/shard_map/ppermute | solution.py:289
  27.2 6.7 %collective-permute-start.13 = (bf16[2,48,512]{2,1,0:T(8,128)(2,1)S(1)}, bf16[2,48,512]{2,1,0:T(8,128)(2,1)S(1)}, u32[]{:S(2)}, u32[]{:S(2)}) collective-permute-start(bf16[2,48,512]{2,1,0:T(8,128)(2,1)S(1)} %get-tuple-element.61), channel_id=1, source_target_pairs={{0,1},{1,0},{2,3},{3,2},{4,5},{5,4},{6,7},{7,6},{8,9},{9,8},{10,11... | collective-permute-start | bytes 294920 | tf_op jit(solution)/shard_map/ppermute | solution.py:298

commit v6 on v5

--- a/solution.py
+++ b/solution.py
@@ -12,7 +12,7 @@
 LOG2E = 1.4426950408889634
 NT = (((1,), (1,)), ((), ()))
 CORES = 2
-CHUNK = 32
+CHUNK = 16
 DELTA_TERMS = 2
 BF16 = jnp.bfloat16
 F32 = jnp.float32
@@ -313,13 +313,13 @@
     other = [first if i == 2 else [swap_core(x, chips) for x in piece] for i, piece in enumerate(own)]
     ds, drk, drv, *grads = attention(prepared, own + other)
     both = [None] * chips
-    for step in steps[1:] + steps[:1]:
+    for step in steps[1:2] + steps[:1] + steps[2:]:
         both[step] = grads[step] + swap_core(grads[chips + step], chips).astype(F32)
     sent = [x.astype(BF16) for x in both[1:]]
-    home = lax.optimization_barrier((grads[chips], sent[0]))[0]
+    home = lax.optimization_barrier((grads[chips], sent[-1]))[0]
     both[0] = grads[0] + swap_core(home, chips).astype(F32)
-    back = [exchange(sent[step - 1], chip_links(chips, step)) for step in steps[1:] + steps[:1]]
-    ds = lax.optimization_barrier((ds, [sent[step - 1] for step in steps[1:] + steps[:1]]))[0]
+    back = [exchange(sent[step - 1], chip_links(chips, step)) for step in steps[1:2] + steps[:1] + steps[2:]]
+    ds = lax.optimization_barrier((ds, [sent[step - 1] for step in steps[1:2] + steps[:1] + steps[2:]]))[0]
     dq, drk, drv = query_grads(ds, prepared[5], drk, drv, own + other)
     dq, back[0] = lax.optimization_barrier((dq, back[0]))
     total = sum([x.astype(F32) for x in back], both[0]).astype(BF16)

time: 35.7 us -> 35.1 us (0.983)
  waiting for transfers between devices: 8.29 us -> 7.3 us
  starting transfers between devices: 14.3 us -> 14.7 us
    ppermute x7, waiting for transfers between devices: 6.04 us -> 5.04 us  [exchange(): return lax.ppermute(x, 'seq', pairs)]
    ppermute x7, starting transfers between devices: 12.2 us -> 12.7 us  [exchange(): return lax.ppermute(x, 'seq', pairs)]
where the time goes in v6:
time: 35.1 us; the launch traced here: 34.9 us
  starting transfers between devices  14.7 us (42%)
  Pallas kernels  10.6 us (30%)
  waiting for transfers between devices  7.3 us (21%)
  other arithmetic  1.04 us (3%)
  between operations  0.69 us (2%)
  local copies, waits for them, and re-layouts  0.64 us (2%)
    ppermute x7, starting transfers between devices, exchange(): return lax.ppermute(x, 'seq', pairs)  12.7 us
    pallas_call x1, Pallas kernels, attention(): pl.pallas_call(functools.partial(attention_kernel, chips, piece_rows, joi...  5.26 us
    ppermute x7, waiting for transfers between devices, exchange(): return lax.ppermute(x, 'seq', pairs)  5.04 us
    pallas_call x1, Pallas kernels, prepare(): pl.pallas_call(functools.partial(prepare_kernel, groups), in_specs=[HBM_S...  3.06 us
    ppermute x9, waiting for transfers between devices, swap_core(): return lax.ppermute(x, 'seq', pairs)  2.26 us
    pallas_call x1, Pallas kernels, query_grads(): pl.pallas_call(functools.partial(query_grad_kernel, joined), in_specs=[VM...  2.24 us
    ppermute x9, starting transfers between devices, swap_core(): return lax.ppermute(x, 'seq', pairs)  1.96 us
    select_n x1, other arithmetic, local(): kv = [jnp.where(kind == 0, prompt_keys[None], prompt_values[None])]  0.91 us
  transfers between devices with their start and end apart: 16, of which 9 were waited for; matrix products, arithmetic and copies ran while one was open for 3% of the time, Pallas kernels for 15%

profile of v6, /device:TPU:0, one launch (start us, length us, event | category | flops | bytes accessed | tf_op | source)
XLA Modules:
  0.0 34.9 jit_solution(13601554418455408666)
XLA Ops:
  0.6 4.1 %collective-permute-start.1 = (bf16[48,512]{1,0:T(8,128)(2,1)}, bf16[48,512]{1,0:T(8,128)(2,1)S(1)}, u32[]{:S(2)}, u32[]{:S(2)}) collective-permute-start(bf16[48,512]{1,0:T(8,128)(2,1)} %param.14), channel_id=1, source_target_pairs={{0,4},{1,5},{4,0},{5,1},{2,6},{3,7},{6,2},{7,3},{8,12},{9,13},{12,... | collective-permute-start | bytes 147464 | tf_op jit(solution)/shard_map/ppermute | solution.py:289
  4.8 0.9 %broadcast_select_fusion.rest_0_ = bf16[2,48,512]{2,1,0:T(8,128)(2,1)S(1)} fusion(pred[2]{0:T(512)(128)(4,1)S(1)} %iota_compare_fusion, bf16[48,512]{1,0:T(8,128)(2,1)} %param.15, bf16[48,512]{1,0:T(8,128)(2,1)} %param.14), kind=kLoop, calls=%fused_computation.4 | loop fusion | flops 49152 | bytes 196610 | tf_op jit(solution)/shard_map/jit(_where)/select_n | solution.py:305
  5.7 3.9 %collective-permute-start.5 = (bf16[2,48,512]{2,1,0:T(8,128)(2,1)S(1)}, bf16[2,48,512]{2,1,0:T(8,128)(2,1)S(1)}, u32[]{:S(2)}, u32[]{:S(2)}) collective-permute-start(bf16[2,48,512]{2,1,0:T(8,128)(2,1)S(1)} %broadcast_select_fusion.rest_0_), channel_id=1, source_target_pairs={{0,6},{1,7},{6,0},{7,1},{2,4},{3,5},{4,2},{5,3},{8,14},{9,15},{14,... | collective-permute-start | bytes 294920 | tf_op jit(solution)/shard_map/ppermute | solution.py:289
  9.7 3.1 %shard_map.119 = (bf16[4096,128]{1,0:T(8,128)(2,1)S(1)}, bf16[4096,256]{1,0:T(8,128)(2,1)S(1)}, bf16[128,4096]{1,0:T(8,128)(2,1)S(1)}, bf16[128,4096]{1,0:T(8,12...) custom-call(s32[8]{0:T(128)} %refs_0_.1, ...), custom_call_target="tpu_custom_call" | custom-call | flops 2097152000 | bytes 8388608 | tf_op jit(solution)/shard_map/pallas_call | solution.py:102
  12.7 0.4 %collective-permute-done.3.rest_3_ = bf16[48,512]{1,0:T(8,128)(2,1)S(1)} collective-permute-done((bf16[48,512]{1,0:T(8,128)(2,1)}, bf16[48,512]{1,0:T(8,128)(2,1)S(1)}, u32[]{:S(2)}, u32[]{:S(2)}) %collective-permute-start.3) | collective-permute-done | bytes 49184 | tf_op jit(solution)/shard_map/ppermute | solution.py:289
  13.1 0.5 %collective-permute-start.4 = (bf16[48,512]{1,0:T(8,128)(2,1)S(1)}, bf16[48,512]{1,0:T(8,128)(2,1)S(1)}, u32[]{:S(2)}, u32[]{:S(2)}) collective-permute-start(bf16[48,512]{1,0:T(8,128)(2,1)S(1)} %collective-permute-done.3.rest_3_), channel_id=1, source_target_pairs={{0,1},{1,0},{2,3},{3,2},{4,5},{5,4},{6,7},{7,6},{8,9},{9,8},{10,11... | collective-permute-start | bytes 147464 | tf_op jit(solution)/shard_map/ppermute | solution.py:298
  13.6 0.7 %collective-permute-done.2.rest_7_ = bf16[48,512]{1,0:T(8,128)(2,1)S(1)} collective-permute-done((bf16[48,512]{1,0:T(8,128)(2,1)S(1)}, bf16[48,512]{1,0:T(8,128)(2,1)S(1)}, u32[]{:S(2)}, u32[]{:S(2)}) %collective-permute-start.2) | collective-permute-done | bytes 49184 | tf_op jit(solution)/shard_map/ppermute | solution.py:298
  14.3 0.2 collective-permute-done.4.rest_8_
  14.5 0.4 %collective-permute-done.rest_1_ = bf16[2,48,512]{2,1,0:T(8,128)(2,1)S(1)} collective-permute-done((bf16[2,48,512]{2,1,0:T(8,128)(2,1)S(1)}, bf16[2,48,512]{2,1,0:T(8,128)(2,1)S(1)}, u32[]{:S(2)}, u32[]{:S(2)}) %collective-permute-start) | collective-permute-done | bytes 98336 | tf_op jit(solution)/shard_map/ppermute | solution.py:289
  14.9 0.5 %collective-permute-start.8 = (bf16[2,48,512]{2,1,0:T(8,128)(2,1)S(1)}, bf16[2,48,512]{2,1,0:T(8,128)(2,1)S(1)}, u32[]{:S(2)}, u32[]{:S(2)}) collective-permute-start(bf16[2,48,512]{2,1,0:T(8,128)(2,1)S(1)} %collective-permute-done.5.rest_4_), channel_id=1, source_target_pairs={{0,1},{1,0},{2,3},{3,2},{4,5},{5,4},{6,7},{7,6},{8,9},{9,8},{10,11... | collective-permute-start | bytes 294920 | tf_op jit(solution)/shard_map/ppermute | solution.py:298
  15.4 0.8 %collective-permute-done.7.rest_6_ = bf16[2,48,512]{2,1,0:T(8,128)(2,1)S(1)} collective-permute-done((bf16[2,48,512]{2,1,0:T(8,128)(2,1)S(1)}, bf16[2,48,512]{2,1,0:T(8,128)(2,1)S(1)}, u32[]{:S(2)}, u32[]{:S(2)}) %collective-permute-start.7) | collective-permute-done | bytes 98336 | tf_op jit(solution)/shard_map/ppermute | solution.py:298
  16.2 0.2 collective-permute-done.8.rest_9_
  16.3 5.3 %shard_map.120 = (bf16[4096,512]{1,0:T(8,128)(2,1)S(1)}, bf16[128,512]{1,0:T(8,128)(2,1)S(1)}, bf16[128,512]{1,0:T(8,128)(2,1)S(1)}, f32[2,48,512]{2,1,0:T(8,128...) custom-call(f32[128,128]{1,0:T(8,128)S(1)} %get-tuple-element.34.liv, ...), custom_call_target="tpu_custom_call" | custom-call | flops 2684354560 | bytes 5242880 | tf_op jit(solution)/shard_map/pallas_call | solution.py:215
  21.6 0.4 %collective-permute-start.9 = (bf16[2,48,512]{2,1,0:T(8,128)(2,1)S(1)}, bf16[2,48,512]{2,1,0:T(8,128)(2,1)S(1)}, u32[]{:S(2)}, u32[]{:S(2)}) collective-permute-start(bf16[2,48,512]{2,1,0:T(8,128)(2,1)S(1)} %get-tuple-element.47), channel_id=1, source_target_pairs={{0,1},{1,0},{2,3},{3,2},{4,5},{5,4},{6,7},{7,6},{8,9},{9,8},{10,11... | collective-permute-start | bytes 294920 | tf_op jit(solution)/shard_map/ppermute | solution.py:298
  22.0 0.2 collective-permute-start.10
  22.2 0.4 %collective-permute-start.11 = (bf16[2,48,512]{2,1,0:T(8,128)(2,1)S(1)}, bf16[2,48,512]{2,1,0:T(8,128)(2,1)S(1)}, u32[]{:S(2)}, u32[]{:S(2)}) collective-permute-start(bf16[2,48,512]{2,1,0:T(8,128)(2,1)S(1)} %get-tuple-element.51), channel_id=1, source_target_pairs={{0,1},{1,0},{2,3},{3,2},{4,5},{5,4},{6,7},{7,6},{8,9},{9,8},{10,11... | collective-permute-start | bytes 294920 | tf_op jit(solution)/shard_map/ppermute | solution.py:298
  22.5 0.4 %collective-permute-done.9 = bf16[2,48,512]{2,1,0:T(8,128)(2,1)S(1)} collective-permute-done((bf16[2,48,512]{2,1,0:T(8,128)(2,1)S(1)}, bf16[2,48,512]{2,1,0:T(8,128)(2,1)S(1)}, u32[]{:S(2)}, u32[]{:S(2)}) %collective-permute-start.9) | collective-permute-done | bytes 98336 | tf_op jit(solution)/shard_map/ppermute | solution.py:298
  23.0 2.0 %collective-permute-start.12 = (bf16[2,48,512]{2,1,0:T(8,128)(2,1)S(1)}, bf16[2,48,512]{2,1,0:T(8,128)(2,1)S(1)}, u32[]{:S(2)}, u32[]{:S(2)}) collective-permute-start(bf16[2,48,512]{2,1,0:T(8,128)(2,1)S(1)} %add_convert_fusion.3), channel_id=1, source_target_pairs={{0,4},{1,5},{4,0},{5,1},{2,6},{3,7},{6,2},{7,3},{8,12},{9,13},{12,... | collective-permute-start | bytes 294920 | tf_op jit(solution)/shard_map/ppermute | solution.py:289
  25.0 1.4 %collective-permute-start.14 = (bf16[2,48,512]{2,1,0:T(8,128)(2,1)S(1)}, bf16[2,48,512]{2,1,0:T(8,128)(2,1)S(1)}, u32[]{:S(2)}, u32[]{:S(2)}) collective-permute-start(bf16[2,48,512]{2,1,0:T(8,128)(2,1)S(1)} %add_convert_fusion.2), channel_id=1, source_target_pairs={{0,2},{1,3},{2,0},{3,1},{4,6},{5,7},{6,4},{7,5},{8,10},{9,11},{10,... | collective-permute-start | bytes 294920 | tf_op jit(solution)/shard_map/ppermute | solution.py:289
  26.5 1.2 %collective-permute-start.15 = (bf16[2,48,512]{2,1,0:T(8,128)(2,1)S(1)}, bf16[2,48,512]{2,1,0:T(8,128)(2,1)S(1)}, u32[]{:S(2)}, u32[]{:S(2)}) collective-permute-start(bf16[2,48,512]{2,1,0:T(8,128)(2,1)S(1)} %add_convert_fusion.1), channel_id=1, source_target_pairs={{0,6},{1,7},{6,0},{7,1},{2,4},{3,5},{4,2},{5,3},{8,14},{9,15},{14,... | collective-permute-start | bytes 294920 | tf_op jit(solution)/shard_map/ppermute | solution.py:289
  27.7 2.2 %shard_map.121 = (bf16[128,4096]{1,0:T(8,128)(2,1)}, bf16[128,512]{1,0:T(8,128)(2,1)}, bf16[128,512]{1,0:T(8,128)(2,1)}) custom-call(bf16[4096,512]{1,0:T(8,128)(2,1)S(1)} %get-tuple-element.52.ds_ref, bf16[128,512]{1,0:T(8,128)(2,1)S(1)} %get-tuple-element.39.rk_ref, bf16[128,512]{1,0:T(8,128)(2,1)S(1)} %get-tuple-element.53.drk_in, ...), custom_call_target="tpu_custom_call" | custom-call | flops 1073741824 | bytes 8388608 | tf_op jit(solution)/shard_map/pallas_call | solution.py:270
  29.9 2.3 %collective-permute-done.12 = bf16[2,48,512]{2,1,0:T(8,128)(2,1)S(1)} collective-permute-done((bf16[2,48,512]{2,1,0:T(8,128)(2,1)S(1)}, bf16[2,48,512]{2,1,0:T(8,128)(2,1)S(1)}, u32[]{:S(2)}, u32[]{:S(2)}) %collective-permute-start.12) | collective-permute-done | bytes 98336 | tf_op jit(solution)/shard_map/ppermute | solution.py:289
  32.2 2.0 %collective-permute-done.15 = bf16[2,48,512]{2,1,0:T(8,128)(2,1)S(1)} collective-permute-done((bf16[2,48,512]{2,1,0:T(8,128)(2,1)S(1)}, bf16[2,48,512]{2,1,0:T(8,128)(2,1)S(1)}, u32[]{:S(2)}, u32[]{:S(2)}) %collective-permute-start.15) | collective-permute-done | bytes 98336 | tf_op jit(solution)/shard_map/ppermute | solution.py:289
  34.2 0.6 %slice_bitcast_fusion = (bf16[48,512]{1,0:T(8,128)(2,1)}, bf16[48,512]{1,0:T(8,128)(2,1)}) fusion(bf16[2,48,512]{2,1,0:T(8,128)(2,1)S(1)} %add_convert_fusion), kind=kLoop, calls=%fused_computation.5 | loop fusion | bytes 196608 | tf_op jit(solution)/shard_map/squeeze | solution.py:326
  (18 shorter events, 0.2 us)
Async XLA Ops:
  0.6 12.5 %collective-permute-start.1 = (bf16[48,512]{1,0:T(8,128)(2,1)}, bf16[48,512]{1,0:T(8,128)(2,1)S(1)}, u32[]{:S(2)}, u32[]{:S(2)}) collective-permute-start(bf16[48,512]{1,0:T(8,128)(2,1)} %param.14), channel_id=1, source_target_pairs={{0,4},{1,5},{4,0},{5,1},{2,6},{3,7},{6,2},{7,3},{8,12},{9,13},{12,... | collective-permute-start | bytes 147464 | tf_op jit(solution)/shard_map/ppermute | solution.py:289
  4.7 8.4 %collective-permute-start.3 = (bf16[48,512]{1,0:T(8,128)(2,1)}, bf16[48,512]{1,0:T(8,128)(2,1)S(1)}, u32[]{:S(2)}, u32[]{:S(2)}) collective-permute-start(bf16[48,512]{1,0:T(8,128)(2,1)} %param.15), channel_id=1, source_target_pairs={{0,4},{1,5},{4,0},{5,1},{2,6},{3,7},{6,2},{7,3},{8,12},{9,13},{12,... | collective-permute-start | bytes 147464 | tf_op jit(solution)/shard_map/ppermute | solution.py:289
  5.7 7.9 %collective-permute-start.5 = (bf16[2,48,512]{2,1,0:T(8,128)(2,1)S(1)}, bf16[2,48,512]{2,1,0:T(8,128)(2,1)S(1)}, u32[]{:S(2)}, u32[]{:S(2)}) collective-permute-start(bf16[2,48,512]{2,1,0:T(8,128)(2,1)S(1)} %broadcast_select_fusion.rest_0_), channel_id=1, source_target_pairs={{0,6},{1,7},{6,0},{7,1},{2,4},{3,5},{4,2},{5,3},{8,14},{9,15},{14,... | collective-permute-start | bytes 294920 | tf_op jit(solution)/shard_map/ppermute | solution.py:289
  9.7 5.2 %collective-permute-start = (bf16[2,48,512]{2,1,0:T(8,128)(2,1)S(1)}, bf16[2,48,512]{2,1,0:T(8,128)(2,1)S(1)}, u32[]{:S(2)}, u32[]{:S(2)}) collective-permute-start(bf16[2,48,512]{2,1,0:T(8,128)(2,1)S(1)} %broadcast_select_fusion.rest_0_), channel_id=1, source_target_pairs={{0,2},{1,3},{2,0},{3,1},{4,6},{5,7},{6,4},{7,5},{8,10},{9,11},{10,... | collective-permute-start | bytes 294920 | tf_op jit(solution)/shard_map/ppermute | solution.py:289
  13.1 1.2 %collective-permute-start.2 = (bf16[48,512]{1,0:T(8,128)(2,1)S(1)}, bf16[48,512]{1,0:T(8,128)(2,1)S(1)}, u32[]{:S(2)}, u32[]{:S(2)}) collective-permute-start(bf16[48,512]{1,0:T(8,128)(2,1)S(1)} %collective-permute-done.1.rest_2_), channel_id=1, source_target_pairs={{0,1},{1,0},{2,3},{3,2},{4,5},{5,4},{6,7},{7,6},{8,9},{9,8},{10,11... | collective-permute-start | bytes 147464 | tf_op jit(solution)/shard_map/ppermute | solution.py:298
  13.1 1.4 %collective-permute-start.4 = (bf16[48,512]{1,0:T(8,128)(2,1)S(1)}, bf16[48,512]{1,0:T(8,128)(2,1)S(1)}, u32[]{:S(2)}, u32[]{:S(2)}) collective-permute-start(bf16[48,512]{1,0:T(8,128)(2,1)S(1)} %collective-permute-done.3.rest_3_), channel_id=1, source_target_pairs={{0,1},{1,0},{2,3},{3,2},{4,5},{5,4},{6,7},{7,6},{8,9},{9,8},{10,11... | collective-permute-start | bytes 147464 | tf_op jit(solution)/shard_map/ppermute | solution.py:298
  13.6 1.8 %collective-permute-start.6 = (bf16[2,48,512]{2,1,0:T(8,128)(2,1)S(1)}, bf16[2,48,512]{2,1,0:T(8,128)(2,1)S(1)}, u32[]{:S(2)}, u32[]{:S(2)}) collective-permute-start(bf16[2,48,512]{2,1,0:T(8,128)(2,1)S(1)} %broadcast_select_fusion.rest_0_), channel_id=1, source_target_pairs={{0,1},{1,0},{2,3},{3,2},{4,5},{5,4},{6,7},{7,6},{8,9},{9,8},{10,11... | collective-permute-start | bytes 294920 | tf_op jit(solution)/shard_map/ppermute | solution.py:298
  14.9 1.3 %collective-permute-start.7 = (bf16[2,48,512]{2,1,0:T(8,128)(2,1)S(1)}, bf16[2,48,512]{2,1,0:T(8,128)(2,1)S(1)}, u32[]{:S(2)}, u32[]{:S(2)}) collective-permute-start(bf16[2,48,512]{2,1,0:T(8,128)(2,1)S(1)} %collective-permute-done.rest_1_), channel_id=1, source_target_pairs={{0,1},{1,0},{2,3},{3,2},{4,5},{5,4},{6,7},{7,6},{8,9},{9,8},{10,11... | collective-permute-start | bytes 294920 | tf_op jit(solution)/shard_map/ppermute | solution.py:298
  14.9 1.5 %collective-permute-start.8 = (bf16[2,48,512]{2,1,0:T(8,128)(2,1)S(1)}, bf16[2,48,512]{2,1,0:T(8,128)(2,1)S(1)}, u32[]{:S(2)}, u32[]{:S(2)}) collective-permute-start(bf16[2,48,512]{2,1,0:T(8,128)(2,1)S(1)} %collective-permute-done.5.rest_4_), channel_id=1, source_target_pairs={{0,1},{1,0},{2,3},{3,2},{4,5},{5,4},{6,7},{7,6},{8,9},{9,8},{10,11... | collective-permute-start | bytes 294920 | tf_op jit(solution)/shard_map/ppermute | solution.py:298
  21.6 1.4 %collective-permute-start.9 = (bf16[2,48,512]{2,1,0:T(8,128)(2,1)S(1)}, bf16[2,48,512]{2,1,0:T(8,128)(2,1)S(1)}, u32[]{:S(2)}, u32[]{:S(2)}) collective-permute-start(bf16[2,48,512]{2,1,0:T(8,128)(2,1)S(1)} %get-tuple-element.47), channel_id=1, source_target_pairs={{0,1},{1,0},{2,3},{3,2},{4,5},{5,4},{6,7},{7,6},{8,9},{9,8},{10,11... | collective-permute-start | bytes 294920 | tf_op jit(solution)/shard_map/ppermute | solution.py:298
  22.0 3.0 %collective-permute-start.10 = (bf16[2,48,512]{2,1,0:T(8,128)(2,1)S(1)}, bf16[2,48,512]{2,1,0:T(8,128)(2,1)S(1)}, u32[]{:S(2)}, u32[]{:S(2)}) collective-permute-start(bf16[2,48,512]{2,1,0:T(8,128)(2,1)S(1)} %get-tuple-element.49), channel_id=1, source_target_pairs={{0,1},{1,0},{2,3},{3,2},{4,5},{5,4},{6,7},{7,6},{8,9},{9,8},{10,11... | collective-permute-start | bytes 294920 | tf_op jit(solution)/shard_map/ppermute | solution.py:298
  22.2 4.3 %collective-permute-start.11 = (bf16[2,48,512]{2,1,0:T(8,128)(2,1)S(1)}, bf16[2,48,512]{2,1,0:T(8,128)(2,1)S(1)}, u32[]{:S(2)}, u32[]{:S(2)}) collective-permute-start(bf16[2,48,512]{2,1,0:T(8,128)(2,1)S(1)} %get-tuple-element.51), channel_id=1, source_target_pairs={{0,1},{1,0},{2,3},{3,2},{4,5},{5,4},{6,7},{7,6},{8,9},{9,8},{10,11... | collective-permute-start | bytes 294920 | tf_op jit(solution)/shard_map/ppermute | solution.py:298
  23.0 9.2 %collective-permute-start.12 = (bf16[2,48,512]{2,1,0:T(8,128)(2,1)S(1)}, bf16[2,48,512]{2,1,0:T(8,128)(2,1)S(1)}, u32[]{:S(2)}, u32[]{:S(2)}) collective-permute-start(bf16[2,48,512]{2,1,0:T(8,128)(2,1)S(1)} %add_convert_fusion.3), channel_id=1, source_target_pairs={{0,4},{1,5},{4,0},{5,1},{2,6},{3,7},{6,2},{7,3},{8,12},{9,13},{12,... | collective-permute-start | bytes 294920 | tf_op jit(solution)/shard_map/ppermute | solution.py:289
  25.0 7.2 %collective-permute-start.14 = (bf16[2,48,512]{2,1,0:T(8,128)(2,1)S(1)}, bf16[2,48,512]{2,1,0:T(8,128)(2,1)S(1)}, u32[]{:S(2)}, u32[]{:S(2)}) collective-permute-start(bf16[2,48,512]{2,1,0:T(8,128)(2,1)S(1)} %add_convert_fusion.2), channel_id=1, source_target_pairs={{0,2},{1,3},{2,0},{3,1},{4,6},{5,7},{6,4},{7,5},{8,10},{9,11},{10,... | collective-permute-start | bytes 294920 | tf_op jit(solution)/shard_map/ppermute | solution.py:289
  26.5 7.7 %collective-permute-start.15 = (bf16[2,48,512]{2,1,0:T(8,128)(2,1)S(1)}, bf16[2,48,512]{2,1,0:T(8,128)(2,1)S(1)}, u32[]{:S(2)}, u32[]{:S(2)}) collective-permute-start(bf16[2,48,512]{2,1,0:T(8,128)(2,1)S(1)} %add_convert_fusion.1), channel_id=1, source_target_pairs={{0,6},{1,7},{6,0},{7,1},{2,4},{3,5},{4,2},{5,3},{8,14},{9,15},{14,... | collective-permute-start | bytes 294920 | tf_op jit(solution)/shard_map/ppermute | solution.py:289
  27.7 4.6 %collective-permute-start.13 = (bf16[2,48,512]{2,1,0:T(8,128)(2,1)S(1)}, bf16[2,48,512]{2,1,0:T(8,128)(2,1)S(1)}, u32[]{:S(2)}, u32[]{:S(2)}) collective-permute-start(bf16[2,48,512]{2,1,0:T(8,128)(2,1)S(1)} %get-tuple-element.61), channel_id=1, source_target_pairs={{0,1},{1,0},{2,3},{3,2},{4,5},{5,4},{6,7},{7,6},{8,9},{9,8},{10,11... | collective-permute-start | bytes 294920 | tf_op jit(solution)/shard_map/ppermute | solution.py:298
